TPU v7x, 128 devices: a whole 4x4x4 slice. The times are simulated.
128 devices in a mesh: pert: 4 (over x), band: 8 (over y_hi, z), slab: 4 (over y_lo, core).
Axes of the slice: x: 4, y: 4 (y_hi: 2, y_lo: 2; y = y_hi * 2 + y_lo), z: 4, core: 2. Of those that a mesh axis runs over, the one named last changes fastest.
Arguments:
- wave_coeffs: bfloat16 [64, 55296], P('band', 'slab'), may hold values from -0.02734375 to 0.02734375
- band_energies: float32 [64], P('band'), may hold values from -2 to -0.5
- trial_potentials: float32 [4, 96, 9216], P('pert', 'slab'), may hold values from -1 to 1
- wave_map: int32 [55296], P('slab'), may hold values from 0 to 221183, as said below
Outputs:
- residual_field: float32 [4, 96, 9216], P('pert', 'slab', 'band')
- projected: float32 [4, 4], P(None, 'pert')
Inputs may be any that keep to these rules, and one draw needn't show every extreme that they name: `wave_map`: within each of the 4 blocks of 13824 entries the positions are distinct and increasing, and every block holds 0 and the block's largest position.
All inputs are finite; a program needn't handle non-finite values.
Results may differ from a plain program's by a relative error of at most 0.025.
Values may be sent and summed in bfloat16 or wider, within the bound.
A program may use at most 192 MiB of HBM per device.

v0:
```python
import jax
import jax.numpy as jnp
from jax import lax
from jax.sharding import PartitionSpec as P

N1 = 96
N2 = 96
N3 = 96


def cosines(n):
    rows = jnp.arange(n, dtype=jnp.int32).astype(jnp.float32)[:, None]
    cols = jnp.arange(n, dtype=jnp.int32).astype(jnp.float32)[None, :]
    table = jnp.sqrt(2.0 / n) * jnp.cos(jnp.pi * rows * (cols + 0.5) / n)
    table = table * jnp.where(rows == 0, jnp.sqrt(0.5), 1.0)
    return table.astype(jnp.bfloat16)


def per_device(wave_coeffs, band_energies, trial_potentials, wave_map):
    slab_count = lax.axis_size("slab")
    slab_index = lax.axis_index("slab")
    bands, npw_dev = wave_coeffs.shape
    pert_dev, planes, cross = trial_potentials.shape
    stick = N2 * N3 // slab_count
    tab_x, tab_y, tab_z = (cosines(N1), cosines(N2), cosines(N3))
    xpos = wave_map // stick
    jpos = slab_index * stick + wave_map % stick
    ypos = jpos // N3
    zpos = jpos % N3
    kin = 2.0 * (
        xpos.astype(jnp.float32) ** 2 / (N1 * N1)
        + ypos.astype(jnp.float32) ** 2 / (N2 * N2)
        + zpos.astype(jnp.float32) ** 2 / (N3 * N3)
    )

    def sticks_of(values):
        count = values.shape[0]
        return (
            jnp.zeros((count, N1 * stick), jnp.bfloat16)
            .at[:, wave_map]
            .set(values)
            .reshape(count, N1, stick)
        )

    def first_inverse(sticks):
        return jnp.einsum("ki,bks->bis", tab_x, sticks, preferred_element_type=jnp.float32).astype(
            jnp.bfloat16
        )

    def planes_inverse(items):
        count = items.shape[0]
        cube = items.reshape(count, items.shape[1], N2, N3)
        cube = jnp.einsum("ki,bxkz->bxiz", tab_y, cube, preferred_element_type=jnp.float32).astype(
            jnp.bfloat16
        )
        cube = jnp.einsum("ki,bxyk->bxyi", tab_z, cube, preferred_element_type=jnp.float32).astype(
            jnp.bfloat16
        )
        return cube.reshape(count, items.shape[1], N2 * N3)

    psi_real = planes_inverse(
        lax.all_to_all(
            first_inverse(sticks_of(wave_coeffs)), "slab", split_axis=1, concat_axis=2, tiled=True
        )
    )
    pairs = pert_dev * bands
    product = (trial_potentials[:, None] * psi_real[None].astype(jnp.float32)).astype(jnp.bfloat16)
    cube = product.reshape(pairs, planes, N2, N3)
    cube = jnp.einsum("ik,bxyk->bxyi", tab_z, cube, preferred_element_type=jnp.float32).astype(
        jnp.bfloat16
    )
    cube = jnp.einsum("ik,bxkz->bxiz", tab_y, cube, preferred_element_type=jnp.float32).astype(
        jnp.bfloat16
    )
    items = lax.all_to_all(
        cube.reshape(pairs, planes, cross), "slab", split_axis=2, concat_axis=1, tiled=True
    )
    count = items.shape[0]
    full = jnp.einsum("ik,bks->bis", tab_x, items, preferred_element_type=jnp.float32).reshape(
        count, N1 * stick
    )
    waves = jnp.take(full, wave_map, axis=1).astype(jnp.bfloat16)
    all_bands = lax.all_gather(wave_coeffs, "band", axis=0, tiled=True)
    correlation = lax.dot_general(
        all_bands, waves, (((1,), (1,)), ((), ())), preferred_element_type=jnp.float32
    )
    correlation = lax.psum(correlation, "slab").astype(jnp.bfloat16)
    removed = lax.dot_general(
        correlation, all_bands, (((0,), (0,)), ((), ())), preferred_element_type=jnp.float32
    )
    rhs = (waves.astype(jnp.float32) - removed).astype(jnp.bfloat16)
    squares = rhs.astype(jnp.float32) ** 2
    energies = jnp.tile(band_energies, pert_dev)
    numer = jnp.sum(squares, axis=1)
    denom = jnp.sum((kin[None, :] - energies[:, None]) * squares, axis=1)
    numer, denom = lax.psum((numer, denom), "slab")
    step = -numer / denom
    field = planes_inverse(
        lax.all_to_all(
            first_inverse(sticks_of(rhs)), "slab", split_axis=1, concat_axis=2, tiled=True
        )
    )
    scale = 4.0 * N1 * N2 * N3 / all_bands.shape[0]
    weighted = (step[:, None, None] * field.astype(jnp.float32)).reshape(
        pert_dev, bands, planes, cross
    )
    partial_density = scale * jnp.sum(weighted * psi_real.astype(jnp.float32)[None], axis=1)
    potentials = lax.all_gather(
        trial_potentials.astype(jnp.bfloat16), "pert", axis=0, tiled=True
    ).astype(trial_potentials.dtype)
    npert = potentials.shape[0]
    cells = N1 * N2 * N3
    width = cross // lax.axis_size("band")
    offset = lax.axis_index("band") * width
    pot_share = lax.dynamic_slice_in_dim(potentials, offset, width, 2)
    density = lax.psum(partial_density.astype(jnp.bfloat16), "band").astype(jnp.float32)
    flat_pot = potentials.reshape(npert, -1)
    flat_den = density.reshape(pert_dev, -1)
    gram = jnp.dot(flat_pot, flat_pot.T, precision=lax.Precision.HIGHEST)
    projected = jnp.dot(flat_pot, flat_den.T, precision=lax.Precision.HIGHEST)
    gram, projected = lax.psum((gram, projected), "slab")
    density_share = lax.dynamic_slice_in_dim(density, offset, width, 2)
    gram = gram / cells
    projected = projected / cells
    factor = jnp.linalg.cholesky(gram)
    coeffs = jax.scipy.linalg.cho_solve((factor, True), projected)
    residual_field = density_share - jnp.einsum(
        "pq,pxc->qxc", coeffs, pot_share, precision=lax.Precision.HIGHEST
    )
    return (residual_field, projected)


def solution(mesh):
    return jax.shard_map(
        per_device,
        mesh=mesh,
        in_specs=(P("band", "slab"), P("band"), P("pert", "slab", None), P("slab")),
        out_specs=(P("pert", "slab", "band"), P(None, "pert")),
        check_vma=False,
    )
```

profile of v0, /device:TPU:1, one launch (start us, length us, event | category | flops | bytes accessed | tf_op | source)
XLA Modules:
  0.0 906.2 jit_solution(6312756050887446919)
XLA Ops:
  8.9 9.1 %sort = (s32[13824]{0:T(1024)}, s32[13824]{0:T(1024)S(1)}) sort(s32[13824]{0:T(1024)S(1)} %compare_select_fusion, s32[13824]{0:T(1024)S(1)} %iota.64), dimensions={0}, to_apply=%compare | sort | flops 193536 | bytes 221184 | tf_op jit(solution)/shard_map/scatter | solution.py:41
  18.7 2.8 copy.34
  21.5 111.0 %scatter_custom_fusion = bf16[8,221184]{0,1:T(8,128)(2,1)} fusion(s32[13824]{0:T(1024)} %get-tuple-element.2, bf16[]{:T(256)} %constant.118.clone.1, bf16[13824,8]{1,0:T(8,128)(2,1)S(1)} %copy.34, s32[14336]{0:T(1024)} %pad_clamp_fusion.1), kind=kCustom, calls=%fused_computation.7 | custom fusion | bytes 3539456 | tf_op jit(solution)/shard_map/scatter | solution.py:41
  132.5 43.1 %copy.35 = bf16[8,96,2304]{2,1,0:T(8,128)(2,1)S(1)} copy(bf16[8,96,2304]{0,2,1:T(8,128)(2,1)} %bitcast.104) | data formatting | bytes 7077888 | tf_op jit(solution)/shard_map/reshape | solution.py:42
  177.0 3.7 copy.37
  180.7 5.1 all-to-all-start
  189.4 40.2 %all-to-all-done = bf16[8,96,2304]{2,0,1:T(8,128)(2,1)S(1)} async-done(((bf16[8,96,2304]{2,0,1:T(8,128)(2,1)}), bf16[8,96,2304]{2,0,1:T(8,128)(2,1)S(1)}, u32[]{:S(2)}, u32[]{:S(2)}) %all-to-all-start) | async-done | bytes 3538976 | tf_op jit(solution)/shard_map/all_to_all | solution.py:62
  229.6 4.5 copy.90
  234.1 10.5 %reshape.118 = bf16[8,24,96,96]{3,2,1,0:T(8,128)(2,1)} reshape(bf16[8,24,4,2304]{3,2,1,0:T(4,128)(2,1)} %bitcast.110) | data formatting | bytes 7077888 | tf_op jit(solution)/shard_map/reshape | solution.py:52
  244.5 6.9 fusion.40
  251.5 6.9 convert_bitcast_fusion
  258.3 32.5 %copy.72 = bf16[8,24,96,96]{1,0,3,2:T(8,128)(2,1)} copy(bf16[8,24,96,96]{2,3,1,0:T(8,128)(2,1)} %convert_bitcast_fusion) | data formatting | bytes 7077888 | tf_op jit(solution)/shard_map/reshape | solution.py:76
  290.8 37.9 %reshape.171 = bf16[4,2,221184]{2,1,0:T(2,128)(2,1)} reshape(bf16[9216,8,24]{2,1,0:T(8,128)(2,1)} %bitcast.105) | data formatting | bytes 7077888
  328.7 5.7 all-to-all-start.1
  338.3 36.4 %all-to-all-done.1 = bf16[4,2,221184]{2,1,0:T(2,128)(2,1)S(1)} async-done(((bf16[4,2,221184]{2,1,0:T(2,128)(2,1)}), bf16[4,2,221184]{2,1,0:T(2,128)(2,1)S(1)}, u32[]{:S(2)}, u32[]{:S(2)}) %all-to-all-start.1) | async-done | bytes 3538976 | tf_op jit(solution)/shard_map/all_to_all | solution.py:75
  374.7 35.4 %reshape.172 = bf16[9216,8,24]{2,1,0:T(8,128)(2,1)} reshape(bf16[4,2,221184]{2,1,0:T(2,128)(2,1)S(1)} %all-to-all-done.1) | data formatting | bytes 7077888
  410.1 19.5 %copy.73 = bf16[8,24,4,2304]{3,2,1,0:T(4,128)(2,1)S(1)} copy(bf16[8,24,4,2304]{1,0,3,2:T(8,128)(2,1)} %bitcast.106) | data formatting | bytes 7077888 | tf_op jit(solution)/shard_map/all_to_all | solution.py:75
  431.6 36.8 %copy.74 = bf16[8,96,2304]{0,2,1:T(8,128)(2,1)} copy(bf16[8,96,2304]{2,1,0:T(8,128)(2,1)S(1)} %convolution_bitcast_fusion) | data formatting | bytes 7077888 | tf_op jit(solution)/shard_map/reshape | solution.py:79
  468.4 67.3 %gather_fusion = bf16[13824,8]{1,0:T(8,128)(2,1)S(1)} fusion(bf16[8,221184]{0,1:T(8,128)(2,1)} %bitcast.107, s32[14336]{0:T(1024)} %pad_clamp_fusion), kind=kCustom, calls=%fused_computation | custom fusion | bytes 497664 | tf_op jit(solution)/shard_map/jit(_take)/gather | solution.py:82
  540.0 17.0 %psum.42 = bf16[64,8]{0,1:T(8,128)(2,1)S(1)} all-reduce(f32[64,8]{0,1:T(8,128)S(1)} %convolution_bitcast_fusion.1), channel_id=1, replica_groups=mesh['pert'=4,'band'=8,'slab'=4] {'slab'}, use_global_device_ids=true, to_apply=%region_1.2 | all-reduce | flops 512 | bytes 3072 | tf_op jit(solution)/shard_map/psum | solution.py:87
  556.9 3.2 fusion.50
  563.0 111.1 %scatter_custom_fusion.1 = bf16[8,221184]{0,1:T(8,128)(2,1)} fusion(s32[13824]{0:T(1024)} %get-tuple-element.2, bf16[]{:T(256)} %constant.118.clone.1, bf16[13824,8]{1,0:T(8,128)(2,1)S(1)} %copy.48, s32[14336]{0:T(1024)} %pad_clamp_fusion.1), kind=kCustom, calls=%fused_computation.5 | custom fusion | bytes 3539456 | tf_op jit(solution)/shard_map/scatter | solution.py:41
  674.0 42.9 %copy.49 = bf16[8,96,2304]{2,1,0:T(8,128)(2,1)S(1)} copy(bf16[8,96,2304]{0,2,1:T(8,128)(2,1)} %bitcast.103) | data formatting | bytes 7077888 | tf_op jit(solution)/shard_map/reshape | solution.py:42
  718.3 3.7 copy.51
  722.0 4.8 all-to-all-start.2
  728.9 40.0 %all-reduce.1 = (f32[8]{0:T(128)}, f32[8]{0:T(128)}) all-reduce(f32[8]{0:T(128)} %get-tuple-element.7, f32[8]{0:T(128)S(1)} %copy-done.12), channel_id=1, replica_groups=mesh['pert'=4,'band'=8,'slab'=4] {'slab'}, use_global_device_ids=true, to_apply=%region_5.6 | all-reduce | flops 16 | bytes 128 | tf_op jit(solution)/shard_map/psum | solution.py:96
  769.6 4.5 copy.89
  774.1 10.3 %reshape.122 = bf16[8,24,96,96]{3,2,1,0:T(8,128)(2,1)} reshape(bf16[8,24,4,2304]{3,2,1,0:T(4,128)(2,1)} %bitcast.112) | data formatting | bytes 7077888 | tf_op jit(solution)/shard_map/reshape | solution.py:52
  784.4 7.8 fusion.8
  794.0 3.0 copy.79
  799.6 79.6 %all-reduce.4.cloned.1.call-done = bf16[1,24,9216]{2,1,0:T(8,128)(2,1)} async-done(((bf16[1,24,9216]{2,1,0:T(8,128)(2,1)}), bf16[1,24,9216]{2,1,0:T(8,128)(2,1)}) %all-reduce.4.cloned.1.call-update) | async-done | bytes 442384 | tf_op jit(solution)/shard_map/psum | solution.py:116
  883.4 10.7 %all-reduce = (f32[4,1]{0,1:T(1,128)S(1)}, f32[4,4]{0,1:T(4,128)S(1)}) all-reduce(f32[4,1]{0,1:T(1,128)S(1)} %convolution_bitcast_fusion.4, f32[4,4]{0,1:T(4,128)S(1)} %fusion.47), channel_id=1, replica_groups=mesh['pert'=4,'band'=8,'slab'=4] {'slab'}, use_global_device_ids=true, to_apply=%region_12.13 | all-reduce | flops 20 | bytes 160 | tf_op jit(solution)/shard_map/psum | solution.py:121
  (74 shorter events, 36.2 us)
Async XLA Ops:
  8.0 243.4 %copy-start.3 = (f32[96]{0:T(128)}, f32[96]{0:T(128)S(1)}, u32[]{:S(2)}) copy-start(f32[96]{0:T(128)S(1)} %get-tuple-element.13) | copy-start | bytes 1156
  8.0 243.4 %copy-start.6 = (f32[96]{0:T(128)}, f32[96]{0:T(128)S(1)}, u32[]{:S(2)}) copy-start(f32[96]{0:T(128)S(1)} %get-tuple-element.14) | copy-start | bytes 1156
  8.0 243.4 %copy-start.9 = (f32[96]{0:T(128)}, f32[96]{0:T(128)S(1)}, u32[]{:S(2)}) copy-start(f32[96]{0:T(128)S(1)} %convert_multiply_fusion.3) | copy-start | bytes 1156
  8.9 9.8 %copy-start.2 = (s32[13824]{0:T(1024)}, s32[13824]{0:T(1024)S(1)}, u32[]{:S(2)}) copy-start(s32[13824]{0:T(1024)S(1)} %compare_select_fusion) | copy-start | bytes 165892
  180.7 48.8 %all-to-all-start = ((bf16[8,96,2304]{2,0,1:T(8,128)(2,1)}), bf16[8,96,2304]{2,0,1:T(8,128)(2,1)S(1)}, u32[]{:S(2)}, u32[]{:S(2)}) async-start(bf16[8,96,2304]{2,0,1:T(8,128)(2,1)} %copy.37), calls=%async_computation | async-start | bytes 7077888 | tf_op jit(solution)/shard_map/all_to_all | solution.py:62
  185.9 351.9 %all-gather.3.cloned.1.call-start = ((), (), s32[]{:S(2)}) async-start(), calls=%async_computation.3 | async-start | bytes 1990656 | tf_op jit(solution)/shard_map/all_gather | solution.py:83
  244.5 6.9 copy-start
  328.7 46.0 %all-to-all-start.1 = ((bf16[4,2,221184]{2,1,0:T(2,128)(2,1)}), bf16[4,2,221184]{2,1,0:T(2,128)(2,1)S(1)}, u32[]{:S(2)}, u32[]{:S(2)}) async-start(bf16[4,2,221184]{2,1,0:T(2,128)(2,1)} %reshape.171), calls=%async_computation.1 | async-start | bytes 7077888 | tf_op jit(solution)/shard_map/all_to_all | solution.py:75
  429.6 0.7 copy-start.4
  429.6 0.6 copy-start.7
  429.6 0.7 copy-start.10
  674.0 42.9 %copy-start.5 = (f32[96]{0:T(128)S(1)}, f32[96]{0:T(128)}, u32[]{:S(2)}) copy-start(f32[96]{0:T(128)} %copy-done.3) | copy-start | bytes 1156
  674.0 42.9 %copy-start.8 = (f32[96]{0:T(128)S(1)}, f32[96]{0:T(128)}, u32[]{:S(2)}) copy-start(f32[96]{0:T(128)} %copy-done.6) | copy-start | bytes 1156
  674.0 42.9 %copy-start.11 = (f32[96]{0:T(128)S(1)}, f32[96]{0:T(128)}, u32[]{:S(2)}) copy-start(f32[96]{0:T(128)} %copy-done.9) | copy-start | bytes 1156
  722.0 6.8 copy-start.12
  722.0 47.5 %all-to-all-start.2 = ((bf16[8,96,2304]{2,0,1:T(8,128)(2,1)}), bf16[8,96,2304]{2,0,1:T(8,128)(2,1)S(1)}, u32[]{:S(2)}, u32[]{:S(2)}) async-start(bf16[8,96,2304]{2,0,1:T(8,128)(2,1)} %copy.51), calls=%async_computation.2 | async-start | bytes 7077888 | tf_op jit(solution)/shard_map/all_to_all | solution.py:99
  726.8 67.2 %all-gather.5.cloned.1.call-start = ((), (), s32[]{:S(2)}) async-start(), calls=%async_computation.5 | async-start | bytes 2211840 | tf_op jit(solution)/shard_map/all_gather | solution.py:108
  728.8 150.4 %all-reduce.4.cloned.1.call-start = ((), (), s32[]{:S(2)}) async-start(), calls=%async_computation.4 | async-start | bytes 884736 | tf_op jit(solution)/shard_map/psum | solution.py:116
  794.0 3.0 copy-start.1
  896.2 2.3 copy-start.13
Sparse Core Ops, SparseCore 0:
  189.0 58.9 all-gather.2
  794.1 85.1 all-reduce.3
Sparse Core Ops, SparseCore 1:
  729.0 31.9 all-gather.4
where the time goes:
time: 917 us; the launch traced here: 906 us
  local copies, waits for them, and re-layouts  592 us (65%)
  waiting for transfers between devices  157 us (17%)
  blocking collectives  67.7 us (7%)
  matrix products  36.7 us (4%)
  other arithmetic  20.7 us (2%)
  between operations  16 us (2%)
  starting transfers between devices  15.7 us (2%)
    scatter x3, local copies, waits for them, and re-layouts, sticks_of(): return jnp.zeros((count, N1 * stick), jnp.bfloat16).at[:, wave_map].set(v...  222 us
    reshape x2, local copies, waits for them, and re-layouts, sticks_of(): return jnp.zeros((count, N1 * stick), jnp.bfloat16).at[:, wave_map].set(v...  86 us
    unnamed x33, local copies, waits for them, and re-layouts  81 us
    psum x1, waiting for transfers between devices, per_device(): lax.psum(partial_density.astype(jnp.bfloat16), 'band').astype(jnp.float32)  79.6 us
    gather x2, local copies, waits for them, and re-layouts, per_device(): waves = jnp.take(full, wave_map, axis=1).astype(jnp.bfloat16)  69.4 us
    all_to_all x1, waiting for transfers between devices, per_device(): lax.all_to_all(first_inverse(sticks_of(wave_coeffs)), 'slab', split_axis=...  40.2 us
    psum x1, blocking collectives, per_device(): numer, denom = lax.psum((numer, denom), 'slab')  40 us
    reshape x1, local copies, waits for them, and re-layouts, per_device(): jnp.einsum('ik,bks->bis', tab_x, items, preferred_element_type=jnp.float32)  36.8 us
  transfers between devices with their start and end apart: 6, of which 3 were waited for; matrix products, arithmetic and copies ran while one was open for 33% of the time, Pallas kernels for 0%

commit v1 on v0

v1 whole, which is shorter than its diff:
```python
import jax
import jax.numpy as jnp
from jax import lax
from jax.experimental import pallas as pl
from jax.experimental.pallas import tpu as pltpu
from jax.sharding import PartitionSpec as P

N1 = 96
N2 = 96
N3 = 96
LANES = 128
WIN = 384
F32 = jnp.float32
BF16 = jnp.bfloat16


def cosines(n):
    rows = jnp.arange(n, dtype=jnp.int32).astype(jnp.float32)[:, None]
    cols = jnp.arange(n, dtype=jnp.int32).astype(jnp.float32)[None, :]
    table = jnp.sqrt(2.0 / n) * jnp.cos(jnp.pi * rows * (cols + 0.5) / n)
    table = table * jnp.where(rows == 0, jnp.sqrt(0.5), 1.0)
    return table.astype(jnp.bfloat16)


def dot(a, b):
    return jnp.dot(a, b, preferred_element_type=F32)


def row_range(starts_ref, s, kx):
    first = starts_ref[s, kx]
    end = starts_ref[s, kx + 1]
    base = pl.multiple_of((first // LANES) * LANES, LANES)
    return first, end, base


def scatter_window(data_ref, s, base, first, end, ny):
    rows = data_ref[s, :, pl.ds(base, WIN)]
    place = base + lax.broadcasted_iota(jnp.int32, (1, WIN), 1)
    inside = (place >= first) & (place < end)
    ypos = jnp.where(inside, rows[2:3], -1.0)
    hot_y = (lax.broadcasted_iota(jnp.int32, (ny, WIN), 0).astype(F32) == ypos).astype(F32)
    hot_z = lax.broadcasted_iota(jnp.int32, (N3, WIN), 0).astype(F32) == rows[3:4]
    spread = jnp.concatenate(
        [jnp.where(hot_z, rows[0:1], 0.0), jnp.where(hot_z, rows[1:2], 0.0)], axis=0
    )
    return lax.dot_general(
        hot_y.astype(BF16),
        spread.astype(BF16),
        (((1,), (1,)), ((), ())),
        preferred_element_type=F32,
    )


def scatter_planes(starts_ref, data_ref, plane_ref):
    slabs = data_ref.shape[0]
    ny = N2 // slabs

    @pl.loop(0, N1)
    def _(kx):
        parts = []
        for s in range(slabs):
            first, end, base = row_range(starts_ref, s, kx)
            parts.append(scatter_window(data_ref, s, base, first, end, ny))
        plane_ref[kx] = jnp.concatenate(parts, axis=0).astype(BF16)

    @pl.when(starts_ref[0, N1 + 1] > 0)
    def _():
        @pl.loop(0, N1)
        def _(kx):
            parts = []
            for s in range(slabs):
                first, end, base = row_range(starts_ref, s, kx)

                def more(i, acc):
                    at = pl.multiple_of(base + i * WIN, LANES)
                    return acc + scatter_window(data_ref, s, at, first, end, ny)

                windows = (end - base + WIN - 1) // WIN
                parts.append(lax.fori_loop(1, windows, more, jnp.zeros((ny, 2 * N3), F32)))
            total = plane_ref[kx].astype(F32) + jnp.concatenate(parts, axis=0)
            plane_ref[kx] = total.astype(BF16)


def inverse_zy(plane_ref, turned_ref, inv_y, inv_z):
    @pl.loop(0, N1)
    def _(kx):
        z_done = dot(plane_ref[kx], inv_z).astype(BF16)
        done = dot(inv_y, z_done)
        turned_ref[0, pl.ds(kx, N2, stride=N1), :] = done[:, :LANES]
        turned_ref[1, pl.ds(kx, N2, stride=N1), :] = done[:, LANES:]


def turned_rows(turned_ref, i):
    at = pl.ds(pl.multiple_of(i * N1, 8), N1)
    return jnp.concatenate([turned_ref[0, at, :], turned_ref[1, at, :]], axis=1).astype(BF16)


def psi_kernel(starts_ref, data_ref, inv_x_ref, inv_y_ref, inv_z_ref, psi_ref, plane_ref, turned_ref):
    scatter_planes(starts_ref, data_ref, plane_ref)
    inverse_zy(plane_ref, turned_ref, inv_y_ref[...], inv_z_ref[...])

    @pl.loop(0, N2)
    def _(y):
        psi_ref[y] = dot(inv_x_ref[...], turned_rows(turned_ref, y)).astype(BF16)


def field_kernel(
    starts_ref, step_ref, data_ref, psi_ref, inv_x_ref, inv_y_ref, inv_z_ref, out_ref, plane_ref, turned_ref
):
    scatter_planes(starts_ref, data_ref, plane_ref)
    inverse_zy(plane_ref, turned_ref, inv_y_ref[...], inv_z_ref[...])

    @pl.loop(0, N2)
    def _(y):
        field = dot(inv_x_ref[...], turned_rows(turned_ref, y)).astype(BF16).astype(F32)
        terms = psi_ref[y].astype(F32) * field
        density = step_ref[0] * terms[:, :LANES] + step_ref[1] * terms[:, LANES:]
        out_ref[y] = density.astype(out_ref.dtype)


def gather_window(data_ref, wave_ref, out_ref, s, kx, base, first, end, ny):
    at = pl.ds(base, WIN)
    rows = data_ref[s, :, at]
    place = base + lax.broadcasted_iota(jnp.int32, (1, WIN), 1)
    inside = (place >= first) & (place < end)
    hot_z = (lax.broadcasted_iota(jnp.int32, (LANES, WIN), 0).astype(F32) == rows[3:4]).astype(F32)
    hot_y = lax.broadcasted_iota(jnp.int32, (ny, WIN), 0).astype(F32) == rows[2:3]
    mine = wave_ref[kx, s * ny : (s + 1) * ny, :]
    both = jnp.concatenate([mine[:, :LANES], mine[:, LANES:]], axis=0).astype(BF16)
    picked = dot(both, hot_z.astype(BF16))
    one = jnp.sum(jnp.where(hot_y, picked[:ny], 0.0), axis=0, keepdims=True)
    two = jnp.sum(jnp.where(hot_y, picked[ny:], 0.0), axis=0, keepdims=True)
    found = jnp.concatenate([one, two], axis=0)
    out_ref[s, 0:2, at] = jnp.where(inside, found, out_ref[s, 0:2, at])


def waves_kernel(
    starts_ref, data_ref, psi_ref, pot_ref, fwd_x_ref, fwd_y_ref, fwd_z_ref, out_ref, turned_ref, wave_ref
):
    slabs = data_ref.shape[0]
    ny = N2 // slabs
    out_ref[...] = jnp.zeros_like(out_ref)

    @pl.loop(0, N2)
    def _(y):
        pot = jnp.concatenate([pot_ref[s, y].astype(F32) for s in range(slabs)], axis=0)
        pot = jnp.concatenate([pot, pot], axis=1)
        product = (pot * psi_ref[y].astype(F32)).astype(BF16)
        done = dot(fwd_x_ref[...], product)
        turned_ref[0, pl.ds(y, N1, stride=N2), :] = done[:, :LANES]
        turned_ref[1, pl.ds(y, N1, stride=N2), :] = done[:, LANES:]

    @pl.loop(0, N1)
    def _(kx):
        y_done = dot(fwd_y_ref[...], turned_rows(turned_ref, kx)).astype(BF16)
        wave_ref[kx] = dot(y_done, fwd_z_ref[...])

    @pl.loop(0, N1)
    def _(kx):
        for s in range(slabs):
            first, end, base = row_range(starts_ref, s, kx)
            gather_window(data_ref, wave_ref, out_ref, s, kx, base, first, end, ny)

    @pl.when(starts_ref[0, N1 + 1] > 0)
    def _():
        @pl.loop(0, N1)
        def _(kx):
            for s in range(slabs):
                first, end, base = row_range(starts_ref, s, kx)

                @pl.loop(1, (end - base + WIN - 1) // WIN)
                def _(i):
                    at = pl.multiple_of(base + i * WIN, LANES)
                    gather_window(data_ref, wave_ref, out_ref, s, kx, at, first, end, ny)


SMEM = pl.BlockSpec(memory_space=pltpu.SMEM)
VMEM = pl.BlockSpec(memory_space=pltpu.VMEM)
PARAMS = dict(vmem_limit_bytes=56 * 1024 * 1024)


def cost(flops, moved):
    return pl.CostEstimate(flops=int(flops), bytes_accessed=int(moved), transcendentals=0)


def plane_scratch():
    return [pltpu.VMEM((N1, N2, 2 * N3), BF16), pltpu.VMEM((2, N1 * N2, LANES), F32)]


def psi_of(starts, data, inv_x, inv_y, inv_z):
    return pl.pallas_call(
        psi_kernel,
        out_shape=jax.ShapeDtypeStruct((N2, N1, 2 * LANES), BF16),
        in_specs=[SMEM] + [VMEM] * 4,
        out_specs=VMEM,
        scratch_shapes=plane_scratch(),
        compiler_params=pltpu.CompilerParams(**PARAMS),
        cost_estimate=cost(2e10, 8e6),
        name="psi",
    )(starts, data, inv_x, inv_y, inv_z)


def waves_of(starts, data, psi, pot, fwd_x, fwd_y, fwd_z):
    return pl.pallas_call(
        waves_kernel,
        out_shape=jax.ShapeDtypeStruct(data.shape[:1] + (2,) + data.shape[2:], F32),
        in_specs=[SMEM] + [VMEM] * 6,
        out_specs=VMEM,
        scratch_shapes=[pltpu.VMEM((2, N1 * N2, LANES), F32), pltpu.VMEM((N1, N2, 2 * LANES), F32)],
        compiler_params=pltpu.CompilerParams(**PARAMS),
        cost_estimate=cost(2e10, 8e6),
        name="waves",
    )(starts, data, psi, pot, fwd_x, fwd_y, fwd_z)


def density_of(starts, step, data, psi, inv_x, inv_y, inv_z):
    return pl.pallas_call(
        field_kernel,
        out_shape=jax.ShapeDtypeStruct((N2, N1, LANES), BF16),
        in_specs=[SMEM, SMEM] + [VMEM] * 5,
        out_specs=VMEM,
        scratch_shapes=plane_scratch(),
        compiler_params=pltpu.CompilerParams(**PARAMS),
        cost_estimate=cost(2e10, 8e6),
        name="field",
    )(starts, step, data, psi, inv_x, inv_y, inv_z)


def tables():
    tab_x, tab_y, tab_z = (cosines(N1), cosines(N2), cosines(N3))
    pad = LANES - N3
    wide = jnp.pad(tab_z, ((0, 0), (0, pad)))
    none = jnp.zeros_like(wide)
    inv_z = jnp.block([[wide, none], [none, wide]])
    square = jnp.pad(tab_z.T, ((0, pad), (0, pad)))
    empty = jnp.zeros_like(square)
    fwd_z = jnp.block([[square, empty], [empty, square]])
    return tab_x, tab_y, inv_z, fwd_z


def row_starts(wave_map, stick):
    edges = jnp.arange(N1 + 1, dtype=jnp.int32) * stick
    return jnp.sum((wave_map[None, :] < edges[:, None]).astype(jnp.int32), axis=1)


def with_flag(starts):
    base = starts[:, :-1] // LANES * LANES
    over = jnp.any(starts[:, 1:] > base + WIN).astype(jnp.int32)
    return jnp.concatenate([starts, jnp.full((starts.shape[0], 1), over)], axis=1)


def packed(two, ypos, zpos):
    count = two.shape[2]
    rows = jnp.concatenate(
        [two.astype(F32), ypos[:, None].astype(F32), zpos[:, None].astype(F32)], axis=1
    )
    return jnp.pad(rows, ((0, 0), (0, 4), (0, WIN)))


def per_device(wave_coeffs, band_energies, trial_potentials, wave_map):
    slabs = lax.axis_size("slab")
    me = lax.axis_index("slab")
    bands, npw = wave_coeffs.shape
    planes, cross = trial_potentials.shape[1:]
    stick = N2 * N3 // slabs
    ny = N2 // slabs
    tab_x, tab_y, inv_z, fwd_z = tables()

    starts = row_starts(wave_map, stick)
    both = lax.all_gather(jnp.concatenate([wave_map, starts]), "slab", axis=0)
    maps = both[:, :npw]
    starts = with_flag(both[:, npw:])
    xpos = maps // stick
    ypos = maps % stick // N3
    zpos = maps % N3
    mine = lax.all_to_all(
        wave_coeffs.reshape(slabs, bands // slabs, npw), "slab", split_axis=0, concat_axis=0
    )
    all_bands = lax.all_gather(wave_coeffs, "band", axis=0, tiled=True)
    local_pot = trial_potentials.reshape(planes, N2, N3)
    pot = jnp.pad(local_pot.astype(BF16).swapaxes(0, 1), ((0, 0), (0, 0), (0, LANES - N3)))
    pot = lax.all_gather(pot, "slab", axis=0)

    psi = psi_of(starts, packed(mine, ypos, zpos), tab_x.T, tab_y.T, inv_z)
    waves = waves_of(starts, packed(mine, ypos, zpos), psi, pot, tab_x, tab_y, fwd_z)
    waves = waves[:, :, :npw].astype(BF16)
    waves = lax.all_to_all(waves, "slab", split_axis=0, concat_axis=0).reshape(bands, npw)
    correlation = lax.dot_general(
        all_bands, waves, (((1,), (1,)), ((), ())), preferred_element_type=F32
    )
    correlation = lax.psum(correlation, "slab").astype(BF16)
    removed = lax.dot_general(
        correlation, all_bands, (((0,), (0,)), ((), ())), preferred_element_type=F32
    )
    rhs = (waves.astype(F32) - removed).astype(BF16)
    rhs = lax.all_to_all(
        rhs.reshape(slabs, bands // slabs, npw), "slab", split_axis=0, concat_axis=0
    )
    yall = ypos + ny * jnp.arange(slabs, dtype=jnp.int32)[:, None]
    kin = 2.0 * (
        xpos.astype(F32) ** 2 / (N1 * N1)
        + yall.astype(F32) ** 2 / (N2 * N2)
        + zpos.astype(F32) ** 2 / (N3 * N3)
    )
    energies = lax.dynamic_slice_in_dim(band_energies, me * (bands // slabs), bands // slabs, 0)
    squares = rhs.astype(F32) ** 2
    numer = jnp.sum(squares, axis=(0, 2))
    denom = jnp.sum((kin[:, None, :] - energies[None, :, None]) * squares, axis=(0, 2))
    step = -numer / denom
    scale = 4.0 * N1 * N2 * N3 / all_bands.shape[0]
    density = density_of(
        starts, scale * step, packed(rhs, ypos, zpos), psi, tab_x.T, tab_y.T, inv_z
    )
    width = cross // lax.axis_size("band")
    density = density[:, :, :N3]
    density = lax.psum_scatter(density, "band", scatter_dimension=0, tiled=True)
    density = lax.psum_scatter(density, "slab", scatter_dimension=1, tiled=True)
    density = density.astype(F32).swapaxes(0, 1).reshape(1, planes, width)
    offset = lax.axis_index("band") * width
    share = lax.dynamic_slice_in_dim(trial_potentials, offset, width, 2)
    potentials = lax.all_gather(share, "pert", axis=0, tiled=True)
    cells = N1 * N2 * N3
    flat_pot = potentials.reshape(potentials.shape[0], -1)
    flat_den = density.reshape(density.shape[0], -1)
    gram = jnp.dot(flat_pot, flat_pot.T, precision=lax.Precision.HIGHEST)
    projected = jnp.dot(flat_pot, flat_den.T, precision=lax.Precision.HIGHEST)
    gram, projected = lax.psum((gram, projected), ("band", "slab"))
    gram = gram / cells
    projected = projected / cells
    factor = jnp.linalg.cholesky(gram)
    coeffs = jax.scipy.linalg.cho_solve((factor, True), projected)
    residual_field = density - jnp.einsum(
        "pq,pxc->qxc", coeffs, potentials, precision=lax.Precision.HIGHEST
    )
    return (residual_field, projected)


def solution(mesh):
    return jax.shard_map(
        per_device,
        mesh=mesh,
        in_specs=(P("band", "slab"), P("band"), P("pert", "slab", None), P("slab")),
        out_specs=(P("pert", "slab", "band"), P(None, "pert")),
        check_vma=False,
    )
```

time: 917 us -> 538 us (0.59)
  local copies, waits for them, and re-layouts: 592 us -> 14.7 us
  Pallas kernels: 0 us -> 252 us
  matrix products: 36.7 us -> 6.64 us
  waiting for transfers between devices: 157 us -> 140 us
  blocking collectives: 67.7 us -> 78.3 us
    pallas_call x0 -> x3, Pallas kernels: none -> 252 us  [the longest x1 88.9 us: density_of(): pl.pallas_call(field_kernel, out_shape=jax.ShapeDtypeStruct((N2, N1, LANE...]
    scatter x3 -> x0, local copies, waits for them, and re-layouts: 222 us -> none  [sticks_of(): return jnp.zeros((count, N1 * stick), jnp.bfloat16).at[:, wave_map].set(v...]
    reshape x6 -> x5, local copies, waits for them, and re-layouts: 176 us -> 1.77 us  [the longest x1 0.78 us: per_device(): rhs.reshape(slabs, bands // slabs, npw)]
    psum x1 -> x0, waiting for transfers between devices: 79.6 us -> none  [per_device(): lax.psum(partial_density.astype(jnp.bfloat16), 'band').astype(jnp.float32)]
    unnamed x33 -> x18, local copies, waits for them, and re-layouts: 81 us -> 2.39 us
    reduce_scatter x0 -> x1, waiting for transfers between devices: none -> 75.9 us  [per_device(): density = lax.psum_scatter(density, 'band', scatter_dimension=0, tiled=True)]
    gather x2 -> x0, local copies, waits for them, and re-layouts: 69.4 us -> none  [per_device(): waves = jnp.take(full, wave_map, axis=1).astype(jnp.bfloat16)]
    all_to_all x3, waiting for transfers between devices: 76.6 us -> 10.6 us  [the longest x1 4.65 us: per_device(): lax.all_to_all(waves, 'slab', split_axis=0, concat_axis=0)]
  transfers between devices with their start and end apart: 6 -> 8, of which waited for: 3 -> 6; matrix products, arithmetic and copies ran while one was open for 33% -> 3% of each run, Pallas kernels for 0% -> 31%
where the time goes in v1:
time: 538 us; the launch traced here: 534 us
  Pallas kernels  252 us (47%)
  waiting for transfers between devices  140 us (26%)
  blocking collectives  78.3 us (15%)
  between operations  15.9 us (3%)
  local copies, waits for them, and re-layouts  14.7 us (3%)
  other arithmetic  13.6 us (3%)
  starting transfers between devices  12.5 us (2%)
  matrix products  6.64 us (1%)
    pallas_call x1, Pallas kernels, density_of(): pl.pallas_call(field_kernel, out_shape=jax.ShapeDtypeStruct((N2, N1, LANE...  88.9 us
    pallas_call x1, Pallas kernels, psi_of(): pl.pallas_call(psi_kernel, out_shape=jax.ShapeDtypeStruct((N2, N1, 2 * LA...  87.4 us
    reduce_scatter x1, waiting for transfers between devices, per_device(): density = lax.psum_scatter(density, 'band', scatter_dimension=0, tiled=True)  75.9 us
    pallas_call x1, Pallas kernels, waves_of(): pl.pallas_call(waves_kernel, out_shape=jax.ShapeDtypeStruct(data.shape[:1...  75.8 us
    psum x1, blocking collectives, per_device(): gram, projected = lax.psum((gram, projected), ('band', 'slab'))  62.2 us
    unnamed x7, waiting for transfers between devices  53.8 us
  transfers between devices with their start and end apart: 8, of which 6 were waited for; matrix products, arithmetic and copies ran while one was open for 3% of the time, Pallas kernels for 31%

profile of v1, /device:TPU:1, one launch (start us, length us, event | category | flops | bytes accessed | tf_op | source)
XLA Modules:
  0.0 534.0 jit_solution(7252944770141343665)
XLA Ops:
  7.2 1.3 fusion.27
  9.2 1.6 convert_reduce_fusion
  10.8 1.1 add_dynamic-update-slice_fusion
  12.7 1.2 convert_element_type.126
  14.8 0.9 pad.27.clone
  16.5 4.8 all-to-all-start
  23.8 2.2 all-to-all-done
  26.2 26.6 %all-reduce.16.cloned.1.call-done = s32[55684]{0:T(1024)} async-done(((s32[55684]{0:T(1024)}), s32[55684]{0:T(1024)}) %all-reduce.16.cloned.1.call-update) | async-done | bytes 222752
  52.7 1.1 reshape.96
  56.9 1.4 pad.25.data_ref
  58.9 87.4 %psi.1.psi_ref = bf16[96,96,256]{2,1,0:T(8,128)(2,1)} custom-call(s32[4,98]{1,0:T(4,128)} %concatenate.38.starts_ref, f32[4,8,14208]{2,1,0:T(8,128)} %pad.25.data_ref, bf16[96,96]{1,0:T(8,128)(2,1)} %copy-done.3, bf16[96,96]{1,0:T(8,128)(2,1)} %copy-done.3, bf16[192,256]{1,0:T(8,128)(2,1)} %fusion.13.inv_z_ref), custom_call_target="tpu_custom_call" | custom-call | flops 20000000000 | bytes 8000000 | tf_op jit(solution)/shard_map/psi/pallas_call | solution.py:191
  146.3 75.8 %waves.1 = f32[4,2,14208]{2,1,0:T(2,128)} custom-call(s32[4,98]{1,0:T(4,128)} %concatenate.38.starts_ref, f32[4,8,14208]{2,1,0:T(8,128)} %pad.25.data_ref, bf16[96,96,256]{2,1,0:T(8,128)(2,1)} %psi.1.psi_ref, bf16[4,96,24,128]{3,2,1,0:T(8,128)(2,1)} %bitcast.60, bf16[96,96]{1,0:T(8,128)(2,1)} %copy-done.4, bf16[96,96]{1,0:T(8,128)(2,1)} %copy-done.4, ...), custom_call_target="tpu_custom_call" | custom-call | flops 20000000000 | bytes 8000000 | tf_op jit(solution)/shard_map/waves/pallas_call | solution.py:204
  222.1 1.9 slice.67
  223.9 3.5 all-to-all-start.1
  227.5 4.7 all-to-all-done.1
  232.3 2.2 convolution_bitcast_fusion
  234.5 5.9 %psum.21 = bf16[64,8]{0,1:T(8,128)(2,1)S(1)} all-reduce(f32[64,8]{0,1:T(8,128)S(1)} %convolution_bitcast_fusion), channel_id=1, replica_groups=mesh['pert'=4,'band'=8,'slab'=4] {'slab'}, use_global_device_ids=true, to_apply=%region_2.3 | all-reduce | flops 512 | bytes 3072 | tf_op jit(solution)/shard_map/psum | solution.py:291
  241.5 4.1 all-to-all-start.2
  245.6 1.0 add_multiply_fusion
  246.6 3.7 all-to-all-done.2
  251.0 1.4 pad.29.data_ref
  252.5 0.8 multiply_reduce_fusion.1
  253.8 88.9 %field.1 = bf16[96,96,128]{2,1,0:T(8,128)(2,1)} custom-call(s32[4,98]{1,0:T(4,128)} %concatenate.38.starts_ref, f32[2]{0:T(128)} %fusion.26.step_ref, f32[4,8,14208]{2,1,0:T(8,128)} %pad.29.data_ref, bf16[96,96,256]{2,1,0:T(8,128)(2,1)} %psi.1.psi_ref, bf16[96,96]{1,0:T(8,128)(2,1)} %copy-done.3, bf16[96,96]{1,0:T(8,128)(2,1)} %copy-done.3, ...), custom_call_target="tpu_custom_call" | custom-call | flops 20000000000 | bytes 8000000 | tf_op jit(solution)/shard_map/field/pallas_call | solution.py:217
  342.8 0.9 constant_dynamic-slice_fusion
  343.8 75.9 %reduce-scatter.3.cloned.1.call-done = bf16[12,96,96]{2,1,0:T(8,128)(2,1)} async-done(((bf16[96,96,96]{2,1,0:T(8,128)(2,1)}), bf16[12,96,96]{2,1,0:T(8,128)(2,1)}) %reduce-scatter.3.cloned.1.call-update) | async-done | bytes 221200 | tf_op jit(solution)/shard_map/reduce_scatter | solution.py:316
  419.7 10.2 %all_gather.23 = f32[4,24,1152]{2,1,0:T(8,128)S(1)} all-gather(f32[1,24,1152]{2,1,0:T(8,128)S(1)} %constant_dynamic-slice_fusion), channel_id=1, replica_groups=mesh['pert'=4,'band'=8,'slab'=4] {'pert'}, dimensions={0}, use_global_device_ids=true | all-gather | bytes 552960 | tf_op jit(solution)/shard_map/all_gather | solution.py:321
  430.7 2.0 convolution_bitcast_fusion.1
  432.7 26.4 %all-reduce.18.cloned.1.call-done = bf16[12,96,96]{2,1,0:T(8,128)(2,1)} async-done(((bf16[12,96,96]{2,1,0:T(8,128)(2,1)}), bf16[12,96,96]{2,1,0:T(8,128)(2,1)}) %all-reduce.18.cloned.1.call-update) | async-done | bytes 221200
  459.1 0.9 dynamic-slice_bitcast_fusion
  460.2 1.0 convolution_bitcast_fusion.4
  461.2 62.2 %all-reduce.12 = (f32[4,1]{0,1:T(1,128)S(1)}, f32[4,4]{0,1:T(4,128)S(1)}) all-reduce(f32[4,1]{0,1:T(1,128)S(1)} %convolution_bitcast_fusion.4, f32[4,4]{0,1:T(4,128)S(1)} %convolution_bitcast_fusion.1), channel_id=1, replica_groups=mesh['pert'=4,'band'=8,'slab'=4] {'band','slab'}, use_global_device_ids=true, to_apply=%region_10.11 | all-reduce | flops 20 | bytes 160 | tf_op jit(solution)/shard_map/psum | solution.py:327
  525.9 0.9 fusion.1
  (71 shorter events, 14.2 us)
Async XLA Ops:
  7.2 45.6 %all-reduce.16.cloned.1.call-start = ((), (), s32[]{:S(2)}) async-start(), calls=%async_computation.7 | async-start | bytes 450560
  11.9 0.7 copy-start.1
  12.6 133.7 %all-gather.7.cloned.1.call-start = ((), (), s32[]{:S(2)}) async-start(), calls=%async_computation.6 | async-start | bytes 2949120 | tf_op jit(solution)/shard_map/all_gather | solution.py:282
  13.9 1.8 copy-start.2
  16.5 9.5 %all-to-all-start = ((bf16[4,2,13824]{2,1,0:T(2,128)(2,1)}), bf16[4,2,13824]{2,1,0:T(2,128)(2,1)S(1)}, u32[]{:S(2)}, u32[]{:S(2)}) async-start(bf16[4,2,13824]{2,1,0:T(2,128)(2,1)} %reshape.86), calls=%async_computation | async-start | bytes 442368 | tf_op jit(solution)/shard_map/all_to_all | solution.py:276
  21.3 211.0 %all-gather.5.cloned.1.call-start = ((), (), s32[]{:S(2)}) async-start(), calls=%async_computation.4 | async-start | bytes 1990656 | tf_op jit(solution)/shard_map/all_gather | solution.py:279
  22.4 34.4 %copy-start.3 = (bf16[96,96]{1,0:T(8,128)(2,1)}, bf16[96,96]{1,0:T(8,128)(2,1)S(1)}, u32[]{:S(2)}) copy-start(bf16[96,96]{1,0:T(8,128)(2,1)S(1)} %get-tuple-element.9.inv_x_ref.inv_y_ref) | copy-start | bytes 55300
  22.4 34.4 %copy-start.4 = (bf16[96,96]{1,0:T(8,128)(2,1)}, bf16[96,96]{1,0:T(8,128)(2,1)S(1)}, u32[]{:S(2)}) copy-start(bf16[96,96]{1,0:T(8,128)(2,1)S(1)} %get-tuple-element.8.fwd_x_ref.fwd_y_ref) | copy-start | bytes 55300
  146.3 81.1 %copy-start.5 = (f32[8]{0:T(128)S(1)}, f32[8]{0:T(128)}, u32[]{:S(2)}) copy-start(f32[8]{0:T(128)} %param.5) | copy-start | bytes 100
  223.9 8.3 %all-to-all-start.1 = ((bf16[4,2,13824]{2,1,0:T(2,128)(2,1)}), bf16[4,2,13824]{2,1,0:T(2,128)(2,1)S(1)}, u32[]{:S(2)}, u32[]{:S(2)}) async-start(bf16[4,2,13824]{2,1,0:T(2,128)(2,1)} %slice.67), calls=%async_computation.1 | async-start | bytes 442368 | tf_op jit(solution)/shard_map/all_to_all | solution.py:287
  232.3 8.1 %copy-start = (bf16[64,13824]{1,0:T(8,128)(2,1)S(1)}, bf16[64,13824]{1,0:T(8,128)(2,1)}, u32[]{:S(2)}) copy-start(bf16[64,13824]{1,0:T(8,128)(2,1)} %all-gather.5.cloned.1.call-done) | copy-start | bytes 5308420
  241.5 8.8 %all-to-all-start.2 = ((bf16[4,2,13824]{2,1,0:T(2,128)(2,1)}), bf16[4,2,13824]{2,1,0:T(2,128)(2,1)S(1)}, u32[]{:S(2)}, u32[]{:S(2)}) async-start(bf16[4,2,13824]{2,1,0:T(2,128)(2,1)} %reshape.88), calls=%async_computation.2 | async-start | bytes 442368 | tf_op jit(solution)/shard_map/all_to_all | solution.py:296
  245.6 174.1 %reduce-scatter.3.cloned.1.call-start = ((), (), s32[]{:S(2)}) async-start(), calls=%async_computation.5 | async-start | bytes 2654208 | tf_op jit(solution)/shard_map/reduce_scatter | solution.py:316
  342.8 116.3 %all-reduce.18.cloned.1.call-start = ((), (), s32[]{:S(2)}) async-start(), calls=%async_computation.8 | async-start | bytes 589824
  525.6 1.9 copy-start.6
Sparse Core Ops, SparseCore 0:
  12.8 39.9 all-reduce.15
  54.5 32.2 all-gather.6
  89.3 52.4 all-gather.4
  342.9 76.7 reduce-scatter.2
  422.2 36.8 all-reduce.17

commit v2 on v0

v2 whole, which is shorter than its diff:
```python
import jax
import jax.numpy as jnp
from jax import lax
from jax.experimental import pallas as pl
from jax.experimental.pallas import tpu as pltpu
from jax.sharding import PartitionSpec as P

N1 = 96
N2 = 96
N3 = 96
LANES = 128
WIN = 512
TILE = 2
F32 = jnp.float32
BF16 = jnp.bfloat16
NT = (((1,), (1,)), ((), ()))
MESH = pl.DeviceIdType.MESH


def cosines(n):
    rows = jnp.arange(n, dtype=jnp.int32).astype(jnp.float32)[:, None]
    cols = jnp.arange(n, dtype=jnp.int32).astype(jnp.float32)[None, :]
    table = jnp.sqrt(2.0 / n) * jnp.cos(jnp.pi * rows * (cols + 0.5) / n)
    table = table * jnp.where(rows == 0, jnp.sqrt(0.5), 1.0)
    return table.astype(jnp.bfloat16)


def dot(a, b):
    return jnp.dot(a, b, preferred_element_type=F32)


def window_base(starts_ref, s, tile):
    return pl.multiple_of((starts_ref[s, tile] // LANES) * LANES, LANES)


def hot_rows(rows, tile, cells):
    at = rows[2:3] - (tile * cells).astype(F32)
    return lax.broadcasted_iota(jnp.int32, (cells, WIN), 0).astype(F32) == at


def hot_z(rows):
    here = lax.broadcasted_iota(jnp.int32, (N3, WIN), 0).astype(F32) == rows[3:4]
    return here.astype(F32).astype(BF16)


def scatter_window(data_ref, s, base, tile, cells):
    rows = data_ref[s, :, pl.ds(base, WIN)]
    hot = hot_rows(rows, tile, cells)
    both = [jnp.where(hot, rows[0:1], 0.0), jnp.where(hot, rows[1:2], 0.0)]
    left = jnp.concatenate(both, axis=0).astype(BF16)
    return lax.dot_general(left, hot_z(rows), NT, preferred_element_type=F32)


def plane_of(parts, t, ny):
    cells = TILE * ny
    rows = [p[b * cells + t * ny : b * cells + (t + 1) * ny] for b in range(2) for p in parts]
    return jnp.concatenate(rows, axis=0)


def scatter_planes(starts_ref, data_ref, plane_ref):
    slabs = data_ref.shape[0]
    ny = N2 // slabs
    cells = TILE * ny
    tiles = N1 // TILE
    unroll = 4

    @pl.loop(0, tiles // unroll)
    def _(group):
        for u in range(unroll):
            tile = group * unroll + u
            parts = [
                scatter_window(data_ref, s, window_base(starts_ref, s, tile), tile, cells)
                for s in range(slabs)
            ]
            for t in range(TILE):
                plane_ref[tile * TILE + t] = plane_of(parts, t, ny).astype(BF16)

    @pl.when(starts_ref[0, tiles + 1] > 0)
    def _():
        @pl.loop(0, tiles)
        def _(tile):
            parts = []
            for s in range(slabs):
                base = window_base(starts_ref, s, tile)

                def more(i, acc):
                    at = pl.multiple_of(base + i * WIN, LANES)
                    return acc + scatter_window(data_ref, s, at, tile, cells)

                windows = (starts_ref[s, tile + 1] - base + WIN - 1) // WIN
                zero = jnp.zeros((2 * cells, N3), F32)
                parts.append(lax.fori_loop(1, windows, more, zero))
            for t in range(TILE):
                old = plane_ref[tile * TILE + t].astype(F32)
                plane_ref[tile * TILE + t] = (old + plane_of(parts, t, ny)).astype(BF16)


def inverse_zy(plane_ref, turned_ref, inv_y, inv_z):
    width = 16

    @pl.loop(0, N1 // width)
    def _(group):
        first = pl.multiple_of(group * width, width)
        flat = plane_ref[pl.ds(first, width)].reshape(width * 2 * N2, N3)
        z_done = dot(flat, inv_z).astype(BF16)
        done = []
        for u in range(width):
            one = z_done[2 * N2 * u : 2 * N2 * u + N2]
            two = z_done[2 * N2 * u + N2 : 2 * N2 * (u + 1)]
            done.append(dot(inv_y, jnp.concatenate([one, two], axis=1)).astype(BF16))
        turned_ref[:, pl.ds(first, width), :] = jnp.swapaxes(jnp.stack(done, axis=0), 0, 1)


def psi_kernel(starts_ref, data_ref, inv_x_ref, inv_y_ref, inv_z_ref, psi_ref, plane_ref, turned_ref):
    scatter_planes(starts_ref, data_ref, plane_ref)
    inverse_zy(plane_ref, turned_ref, inv_y_ref[...], inv_z_ref[...])
    unroll = 8

    @pl.loop(0, N2 // unroll)
    def _(group):
        for u in range(unroll):
            y = group * unroll + u
            psi_ref[y] = dot(inv_x_ref[...], turned_ref[y]).astype(BF16)


def field_kernel(
    starts_ref, data_ref, step_ref, psi_ref, inv_x_ref, inv_y_ref, inv_z_ref, out_ref, plane_ref, turned_ref
):
    scatter_planes(starts_ref, data_ref, plane_ref)
    inverse_zy(plane_ref, turned_ref, inv_y_ref[...], inv_z_ref[...])
    slabs, _, planes, _ = out_ref.shape
    unroll = 8

    @pl.loop(0, N2 // unroll)
    def _(group):
        for u in range(unroll):
            y = group * unroll + u
            field = dot(inv_x_ref[...], turned_ref[y]).astype(BF16).astype(F32)
            terms = psi_ref[y].astype(F32) * field
            density = step_ref[0:1] * terms[:, :LANES] + step_ref[1:2] * terms[:, LANES:]
            for s in range(slabs):
                out_ref[s, y] = density[s * planes : (s + 1) * planes].astype(out_ref.dtype)


def gather_window(data_ref, wave_ref, sum_ref, s, base, tile, ny):
    cells = TILE * ny
    at = pl.ds(base, WIN)
    rows = data_ref[s, :, at]
    hot = hot_rows(rows, tile, cells)
    both = [
        wave_ref[tile * TILE + t, b * N2 + s * ny : b * N2 + (s + 1) * ny, :]
        for b in range(2)
        for t in range(TILE)
    ]
    picked = dot(jnp.concatenate(both, axis=0).astype(BF16), hot_z(rows))
    one = jnp.sum(jnp.where(hot, picked[:cells], 0.0), axis=0, keepdims=True)
    two = jnp.sum(jnp.where(hot, picked[cells:], 0.0), axis=0, keepdims=True)
    sum_ref[s, 0:2, at] += jnp.concatenate([one, two], axis=0)


def waves_kernel(
    starts_ref, data_ref, psi_ref, pot_ref, fwd_x_ref, fwd_y_ref, fwd_z_ref, out_ref, turned_ref, wave_ref, sum_ref
):
    slabs = data_ref.shape[0]
    ny = N2 // slabs
    tiles = N1 // TILE
    sum_ref[...] = jnp.zeros_like(sum_ref)
    width = 16

    @pl.loop(0, N2 // width)
    def _(group):
        first = pl.multiple_of(group * width, width)
        done = []
        for u in range(width):
            y = first + u
            pot = jnp.concatenate([pot_ref[s, y].astype(F32) for s in range(slabs)], axis=0)
            pot = jnp.concatenate([pot, pot], axis=1)
            product = (pot * psi_ref[y].astype(F32)).astype(BF16)
            done.append(dot(fwd_x_ref[...], product).astype(BF16))
        turned_ref[:, pl.ds(first, width), :] = jnp.swapaxes(jnp.stack(done, axis=0), 0, 1)

    unroll = 8

    @pl.loop(0, N1 // unroll)
    def _(group):
        done = []
        for u in range(unroll):
            y_done = dot(fwd_y_ref[...], turned_ref[group * unroll + u]).astype(BF16)
            done += [y_done[:, :LANES], y_done[:, LANES:]]
        waves = dot(jnp.concatenate(done, axis=0), fwd_z_ref[...])
        for u in range(unroll):
            wave_ref[group * unroll + u] = waves[u * 2 * N2 : (u + 1) * 2 * N2]

    several = 4

    @pl.loop(0, tiles // several)
    def _(group):
        for u in range(several):
            tile = group * several + u
            for s in range(slabs):
                base = window_base(starts_ref, s, tile)
                gather_window(data_ref, wave_ref, sum_ref, s, base, tile, ny)

    @pl.when(starts_ref[0, tiles + 1] > 0)
    def _():
        @pl.loop(0, tiles)
        def _(tile):
            for s in range(slabs):
                base = window_base(starts_ref, s, tile)

                @pl.loop(1, (starts_ref[s, tile + 1] - base + WIN - 1) // WIN)
                def _(i):
                    at = pl.multiple_of(base + i * WIN, LANES)
                    gather_window(data_ref, wave_ref, sum_ref, s, at, tile, ny)

    out_ref[...] = sum_ref[:, :, : out_ref.shape[2]].astype(out_ref.dtype)


SMEM = pl.BlockSpec(memory_space=pltpu.SMEM)
VMEM = pl.BlockSpec(memory_space=pltpu.VMEM)
LIMIT = 56 * 1024 * 1024


def greet(peers):
    barrier = pltpu.get_barrier_semaphore()
    for peer in peers:
        pl.semaphore_signal(barrier, inc=1, device_id=peer, device_id_type=MESH)
    pl.semaphore_wait(barrier, len(peers))


def send(src, dst, send_sem, recv_sem, peer):
    copy = pltpu.make_async_remote_copy(
        src_ref=src, dst_ref=dst, send_sem=send_sem, recv_sem=recv_sem, device_id=peer, device_id_type=MESH
    )
    copy.start()
    return copy


def slab_peers(slabs):
    me = lax.axis_index("slab")
    return [lax.rem(me + d, slabs) for d in range(1, slabs)]


def start_kernel(coef_ref, map_ref, coefs_ref, maps_ref, send_sem, recv_sem):
    slabs = coef_ref.shape[0]
    me = lax.axis_index("slab")
    peers = slab_peers(slabs)
    greet([{"slab": peer} for peer in peers])
    copies = []
    for i, peer in enumerate(peers):
        to = {"slab": peer}
        copies.append(send(coef_ref.at[peer], coefs_ref.at[me], send_sem.at[0, i], recv_sem.at[0, i], to))
        copies.append(send(map_ref, maps_ref.at[me], send_sem.at[1, i], recv_sem.at[1, i], to))
    coefs_ref[me] = coef_ref[me]
    maps_ref[me] = map_ref[...]
    for copy in copies:
        copy.wait()


def middle_kernel(
    waves_ref, bands_ref, index_ref, energy_ref, data_ref, step_ref,
    got_ref, corr_ref, rhs_ref, back_ref, total_ref, send_sem, recv_sem,
):
    slabs, two, npw = waves_ref.shape
    chunk = 1536
    me = lax.axis_index("slab")
    peers = slab_peers(slabs)
    greet([{"slab": peer} for peer in peers])
    copies = []
    for i, peer in enumerate(peers):
        to = {"slab": peer}
        copies.append(send(waves_ref.at[peer], got_ref.at[me], send_sem.at[0, i], recv_sem.at[0, i], to))
    got_ref[me] = waves_ref[me]
    for copy in copies:
        copy.wait()

    def waves_at(at):
        return jnp.concatenate([got_ref[t, :, at].astype(F32) for t in range(slabs)], axis=0)

    total_ref[...] = jnp.zeros_like(total_ref)

    @pl.loop(0, npw // chunk)
    def _(i):
        at = pl.ds(pl.multiple_of(i * chunk, chunk), chunk)
        total_ref[...] += lax.dot_general(
            waves_at(at).astype(BF16), bands_ref[:, at], NT, preferred_element_type=F32
        )

    copies = []
    for i, peer in enumerate(peers):
        to = {"slab": peer}
        copies.append(send(total_ref, corr_ref.at[i], send_sem.at[1, i], recv_sem.at[1, i], to))
    for copy in copies:
        copy.wait()
    correlation = total_ref[...]
    for i in range(slabs - 1):
        correlation = correlation + corr_ref[i]
    correlation = correlation.astype(BF16)

    @pl.loop(0, npw // chunk)
    def _(i):
        at = pl.ds(pl.multiple_of(i * chunk, chunk), chunk)
        rhs = (waves_at(at) - dot(correlation, bands_ref[:, at])).astype(BF16)
        for t in range(slabs):
            rhs_ref[t, :, at] = rhs[two * t : two * (t + 1)]

    copies = []
    for i, peer in enumerate(peers):
        to = {"slab": peer}
        copies.append(send(rhs_ref.at[peer], back_ref.at[me], send_sem.at[2, i], recv_sem.at[2, i], to))
    back_ref[me] = rhs_ref[me]
    for copy in copies:
        copy.wait()

    data_ref[...] = index_ref[...]
    numer = jnp.zeros((two, chunk), F32)
    denom = jnp.zeros((two, chunk), F32)
    energy = jnp.concatenate([jnp.full((1, chunk), energy_ref[b], F32) for b in range(two)], axis=0)
    for s in range(slabs):
        for i in range(npw // chunk):
            at = pl.ds(i * chunk, chunk)
            mine = back_ref[s, :, at].astype(F32)
            data_ref[s, 0:2, at] = mine
            squares = mine * mine
            numer = numer + squares
            denom = denom + (index_ref[s, 4:5, at] - energy) * squares
    step = -jnp.sum(numer, axis=1, keepdims=True) / jnp.sum(denom, axis=1, keepdims=True)
    step_ref[...] = jnp.broadcast_to(step, step_ref.shape)


def reduce_kernel(
    density_ref, share_ref, out_ref, projected_ref,
    from_core, half_ref, from_y, quarter_ref, from_z, pots_ref, sums_ref, from_sums, send_sem, recv_sem,
):
    slabs, _, planes, lanes = density_ref.shape
    perts, rows = pots_ref.shape[:2]
    pert, band, slab = (lax.axis_index(name) for name in ("pert", "band", "slab"))
    y_lo, core = slab // 2, lax.rem(slab, 2)
    y_hi, z = band // 4, lax.rem(band, 4)

    def id_of(y_hi, y_lo, z):
        return {"band": y_hi * 4 + z, "slab": y_lo * 2 + core}

    sibling = {"slab": y_lo * 2 + 1 - core}
    y_steps = [(0, 1), (1, 0), (1, 1)]
    y_coords = [(lax.rem(y_hi + a, 2), lax.rem(y_lo + b, 2)) for a, b in y_steps]
    y_peers = [id_of(a, b, z) for a, b in y_coords]
    z_coords = [lax.rem(z + d, 4) for d in range(1, 4)]
    z_peers = [id_of(y_hi, y_lo, c) for c in z_coords]
    p_coords = [lax.rem(pert + d, perts) for d in range(1, perts)]
    p_peers = [{"pert": c} for c in p_coords]
    greet([sibling] + y_peers + z_peers + p_peers)

    copies = []
    for a in range(2):
        src = density_ref.at[a * 2 + 1 - core]
        copies.append(send(src, from_core.at[a], send_sem.at[0, a], recv_sem.at[0, a], sibling))
    pot_copies = []
    for i, peer in enumerate(p_peers):
        pot_copies.append(send(share_ref, pots_ref.at[pert], send_sem.at[1, i], recv_sem.at[1, i], peer))
    pots_ref[pert] = share_ref[...]
    for copy in copies:
        copy.wait()
    for a in range(2):
        @pl.loop(0, N2 // 8)
        def _(i):
            at = pl.ds(pl.multiple_of(i * 8, 8), 8)
            total = density_ref[a * 2 + core, at].astype(F32) + from_core[a, at].astype(F32)
            half_ref[a, at] = total.astype(BF16)

    quarter = N2 // 2
    copies = []
    for i, (a, b) in enumerate(y_coords):
        src = half_ref.at[b, pl.ds(a * quarter, quarter)]
        copies.append(send(src, from_y.at[i], send_sem.at[2, i], recv_sem.at[2, i], y_peers[i]))
    for copy in copies:
        copy.wait()
    mine = y_hi * quarter

    @pl.loop(0, 4)
    def _(i):
        total = half_ref[y_lo, pl.ds(mine + i * rows, rows)].astype(F32)
        for j in range(3):
            total = total + from_y[j, pl.ds(i * rows, rows)].astype(F32)
        quarter_ref[i] = total.astype(BF16)

    copies = []
    for i, c in enumerate(z_coords):
        copies.append(send(quarter_ref.at[c], from_z.at[i], send_sem.at[3, i], recv_sem.at[3, i], z_peers[i]))
    for copy in pot_copies:
        copy.wait()

    def total_of(a):
        a = jnp.sum(a, axis=0)
        a = a[0:8] + a[8:16] + a[16:24]
        return jnp.sum(a, axis=0, keepdims=True)

    pots = [pots_ref[p] for p in range(perts)]
    pairs = [(p, q) for p in range(perts) for q in range(p + 1)]
    sums = [total_of(pots[p] * pots[q]) for p, q in pairs]
    for copy in copies:
        copy.wait()
    density = quarter_ref[z].astype(F32)
    for j in range(3):
        density = density + from_z[j].astype(F32)
    sums += [total_of(pots[p] * density) for p in range(perts)]
    used = len(sums)
    sums += [jnp.zeros((1, lanes), F32)] * (16 - used)
    sums_ref[0] = jnp.concatenate(sums, axis=0)

    at = 0
    for level, group in enumerate([[sibling], y_peers, z_peers]):
        copies = []
        for i, peer in enumerate(group):
            copies.append(
                send(sums_ref.at[level], from_sums.at[at + i], send_sem.at[4 + level, i], recv_sem.at[4 + level, i], peer)
            )
        for copy in copies:
            copy.wait()
        total = sums_ref[level]
        for i in range(len(group)):
            total = total + from_sums[at + i]
        sums_ref[level + 1] = total
        at += len(group)

    cells = 1.0 / (N1 * N2 * N3)
    totals = jnp.broadcast_to(jnp.sum(sums_ref[3], axis=1, keepdims=True) * cells, (16, lanes))
    gram = {pair: totals[k : k + 1] for k, pair in enumerate(pairs)}
    rhs = [totals[len(pairs) + p : len(pairs) + p + 1] for p in range(perts)]
    factor = {}
    for p in range(perts):
        for q in range(p + 1):
            value = gram[p, q]
            for k in range(q):
                value = value - factor[p, k] * factor[q, k]
            factor[p, q] = jnp.sqrt(value) if p == q else value / factor[q, q]
    coeffs = []
    for p in range(perts):
        value = rhs[p]
        for k in range(p):
            value = value - factor[p, k] * coeffs[k]
        coeffs.append(value / factor[p, p])
    for p in reversed(range(perts)):
        value = coeffs[p]
        for k in range(p + 1, perts):
            value = value - factor[k, p] * coeffs[k]
        coeffs[p] = value / factor[p, p]
    for p in range(perts):
        density = density - coeffs[p][None] * pots[p]
    out_ref[...] = density
    projected_ref[...] = jnp.concatenate(rhs + rhs, axis=0)


def cost(flops, moved):
    return pl.CostEstimate(flops=int(flops), bytes_accessed=int(moved), transcendentals=0)


def params(remote=None):
    if remote is None:
        return pltpu.CompilerParams(vmem_limit_bytes=LIMIT)
    return pltpu.CompilerParams(vmem_limit_bytes=LIMIT, collective_id=remote, has_side_effects=True)


def shape(dims, kind):
    return jax.ShapeDtypeStruct(dims, kind)


def plane_scratch():
    return [pltpu.VMEM((N1, 2 * N2, N3), BF16), pltpu.VMEM((N2, N1, 2 * LANES), BF16)]


def start_of(coefs, wave_map):
    slabs, _, npw = coefs.shape
    return pl.pallas_call(
        start_kernel,
        out_shape=(shape(coefs.shape, BF16), shape((slabs, 1, npw), jnp.int32)),
        in_specs=[VMEM] * 2,
        out_specs=(VMEM, VMEM),
        scratch_shapes=[pltpu.SemaphoreType.DMA((2, slabs - 1))] * 2,
        compiler_params=params(1),
        name="start",
    )(coefs, wave_map.reshape(1, npw))


def psi_of(starts, data, inv_x, inv_y, inv_z):
    return pl.pallas_call(
        psi_kernel,
        out_shape=shape((N2, N1, 2 * LANES), BF16),
        in_specs=[SMEM] + [VMEM] * 4,
        out_specs=VMEM,
        scratch_shapes=plane_scratch(),
        compiler_params=params(),
        cost_estimate=cost(2e10, 8e6),
        name="psi",
    )(starts, data, inv_x, inv_y, inv_z)


def waves_of(starts, data, psi, pot, fwd_x, fwd_y, fwd_z, npw):
    slabs = data.shape[0]
    return pl.pallas_call(
        waves_kernel,
        out_shape=shape((slabs, 2, npw), BF16),
        in_specs=[SMEM] + [VMEM] * 6,
        out_specs=VMEM,
        scratch_shapes=[
            pltpu.VMEM((N1, N2, 2 * LANES), BF16),
            pltpu.VMEM((N1, 2 * N2, N3), F32),
            pltpu.VMEM((slabs, 2, data.shape[2]), F32),
        ],
        compiler_params=params(),
        cost_estimate=cost(2e10, 8e6),
        name="waves",
    )(starts, data, psi, pot, fwd_x, fwd_y, fwd_z)


def middle_of(waves, bands, index, energies):
    slabs, two, npw = waves.shape
    block = pltpu.VMEM(waves.shape, BF16)
    small = (slabs * two, bands.shape[0])
    return pl.pallas_call(
        middle_kernel,
        out_shape=(shape(index.shape, F32), shape((two, LANES), F32)),
        in_specs=[VMEM] * 3 + [SMEM],
        out_specs=(VMEM, VMEM),
        scratch_shapes=[
            block,
            pltpu.VMEM((slabs - 1,) + small, F32),
            block,
            block,
            pltpu.VMEM(small, F32),
            pltpu.SemaphoreType.DMA((3, slabs - 1)),
            pltpu.SemaphoreType.DMA((3, slabs - 1)),
        ],
        compiler_params=params(2),
        name="middle",
    )(waves, bands, index, energies)


def density_of(starts, data, step, psi, inv_x, inv_y, inv_z, slabs):
    return pl.pallas_call(
        field_kernel,
        out_shape=shape((slabs, N2, N1 // slabs, LANES), BF16),
        in_specs=[SMEM] + [VMEM] * 6,
        out_specs=VMEM,
        scratch_shapes=plane_scratch(),
        compiler_params=params(),
        cost_estimate=cost(2e10, 8e6),
        name="field",
    )(starts, data, step, psi, inv_x, inv_y, inv_z)


def reduced(density, share, perts):
    slabs, _, planes, lanes = density.shape
    rows = share.shape[0]
    block = (rows, planes, lanes)
    return pl.pallas_call(
        reduce_kernel,
        out_shape=(shape(block, F32), shape((8, lanes), F32)),
        in_specs=[VMEM] * 2,
        out_specs=(VMEM, VMEM),
        scratch_shapes=[
            pltpu.VMEM((2, N2, planes, lanes), BF16),
            pltpu.VMEM((2, N2, planes, lanes), BF16),
            pltpu.VMEM((3, N2 // 2, planes, lanes), BF16),
            pltpu.VMEM((4,) + block, BF16),
            pltpu.VMEM((3,) + block, BF16),
            pltpu.VMEM((perts,) + block, F32),
            pltpu.VMEM((4, 16, lanes), F32),
            pltpu.VMEM((7, 16, lanes), F32),
            pltpu.SemaphoreType.DMA((7, 3)),
            pltpu.SemaphoreType.DMA((7, 3)),
        ],
        compiler_params=params(3),
        name="reduce",
    )(density, share)


def tables():
    tab_x, tab_y, tab_z = (cosines(N1), cosines(N2), cosines(N3))
    inv_z = jnp.pad(tab_z, ((0, 0), (0, LANES - N3)))
    return tab_x, tab_y, inv_z


def tile_starts(maps, stick):
    edges = jnp.arange(N1 // TILE + 1, dtype=jnp.int32) * (TILE * stick)
    starts = jnp.sum((maps[:, None, :] < edges[None, :, None]).astype(jnp.int32), axis=2)
    over = jnp.any(starts[:, 1:] > starts[:, :-1] // LANES * LANES + WIN).astype(jnp.int32)
    return jnp.concatenate([starts, jnp.full((starts.shape[0], 1), over)], axis=1)


def index_rows(maps, ny):
    slabs, npw = maps.shape
    xpos = maps // (ny * N3)
    ypos = maps // N3 % ny + ny * jnp.arange(slabs, dtype=jnp.int32)[:, None]
    zpos = maps % N3
    kin = 2.0 * (
        xpos.astype(F32) ** 2 / (N1 * N1)
        + ypos.astype(F32) ** 2 / (N2 * N2)
        + zpos.astype(F32) ** 2 / (N3 * N3)
    )
    rows = jnp.stack([(maps // N3).astype(F32), zpos.astype(F32), kin], axis=1)
    return jnp.pad(rows, ((0, 0), (2, 3), (0, 2 * WIN)), constant_values=-1.0)


def per_device(wave_coeffs, band_energies, trial_potentials, wave_map):
    slabs = lax.axis_size("slab")
    me = lax.axis_index("slab")
    bands, npw = wave_coeffs.shape
    planes, cross = trial_potentials.shape[1:]
    ny = N2 // slabs
    tab_x, tab_y, inv_z = tables()

    coefs, maps = start_of(wave_coeffs.reshape(slabs, bands // slabs, npw), wave_map)
    maps = maps.reshape(slabs, npw)
    all_bands = lax.all_gather(wave_coeffs, "band", axis=0, tiled=True)
    turned = trial_potentials.reshape(planes, N2, N3).swapaxes(0, 1)
    turned = jnp.pad(turned, ((0, 0), (0, 0), (0, LANES - N3)))
    pot = lax.all_gather(turned.astype(BF16), "slab", axis=0)
    rows = N2 // lax.axis_size("band")
    share = lax.dynamic_slice_in_dim(turned, lax.axis_index("band") * rows, rows, 0)

    starts = tile_starts(maps, ny * N3)
    index = index_rows(maps, ny)
    data = lax.dynamic_update_slice(index, coefs.astype(F32), (0, 0, 0))
    psi = psi_of(starts, data, tab_x.T, tab_y.T, inv_z)
    waves = waves_of(starts, data, psi, pot, tab_x, tab_y, inv_z.T, npw)
    energies = lax.dynamic_slice_in_dim(band_energies, me * (bands // slabs), bands // slabs, 0)
    data, step = middle_of(waves, all_bands, index, energies)
    step = step * (4.0 * N1 * N2 * N3 / all_bands.shape[0])
    density = density_of(starts, data, step, psi, tab_x.T, tab_y.T, inv_z, slabs)
    residual, projected = reduced(density, share, lax.axis_size("pert"))
    residual = residual[:, :, :N3].swapaxes(0, 1).reshape(1, planes, rows * N3)
    return (residual, projected[: lax.axis_size("pert"), :1])


def solution(mesh):
    return jax.shard_map(
        per_device,
        mesh=mesh,
        in_specs=(P("band", "slab"), P("band"), P("pert", "slab", None), P("slab")),
        out_specs=(P("pert", "slab", "band"), P(None, "pert")),
        check_vma=False,
    )
```

time: 917 us -> 186 us (0.20); the launches traced: 906 us -> 185 us
  local copies, waits for them, and re-layouts: 592 us -> 14 us
  waiting for transfers between devices: 157 us -> 17.6 us
  Pallas kernels: 0 us -> 125 us
  blocking collectives: 67.7 us -> 0 us
  matrix products: 36.7 us -> 0 us
  starting transfers between devices: 15.7 us -> 0.08 us
    scatter x3 -> x0, local copies, waits for them, and re-layouts: 222 us -> none  [sticks_of(): return jnp.zeros((count, N1 * stick), jnp.bfloat16).at[:, wave_map].set(v...]
    reshape x6 -> x5, local copies, waits for them, and re-layouts: 176 us -> 4.5 us  [the longest x2 2.32 us: per_device(): turned = trial_potentials.reshape(planes, N2, N3).swapaxes(0, 1)]
    pallas_call x0 -> x6, Pallas kernels: none -> 125 us  [the longest x1 36.2 us: reduced(): pl.pallas_call(reduce_kernel, out_shape=(shape(block, F32), shape((8, lan...]
    psum x1 -> x0, waiting for transfers between devices: 79.6 us -> none  [per_device(): lax.psum(partial_density.astype(jnp.bfloat16), 'band').astype(jnp.float32)]
    unnamed x33 -> x17, local copies, waits for them, and re-layouts: 81 us -> 3.5 us
    all_to_all x3 -> x0, waiting for transfers between devices: 76.6 us -> none  [the longest x1 40.2 us: per_device(): lax.all_to_all(first_inverse(sticks_of(wave_coeffs)), 'slab', split_axis=...]
    gather x2 -> x0, local copies, waits for them, and re-layouts: 69.4 us -> none  [per_device(): waves = jnp.take(full, wave_map, axis=1).astype(jnp.bfloat16)]
    psum x3 -> x0, blocking collectives: 67.7 us -> none  [the longest x1 40 us: per_device(): numer, denom = lax.psum((numer, denom), 'slab')]
  transfers between devices with their start and end apart: 6 -> 2, of which waited for: 3 -> 1; matrix products, arithmetic and copies ran while one was open for 33% -> 10% of each run, Pallas kernels for 0% -> 27%
where the time goes in v2:
time: 186 us; the launch traced here: 185 us
  Pallas kernels  125 us (67%)
  waiting for transfers between devices  17.6 us (9%)
  between operations  14.9 us (8%)
  local copies, waits for them, and re-layouts  14 us (8%)
  other arithmetic  13.5 us (7%)
    pallas_call x1, Pallas kernels, reduced(): pl.pallas_call(reduce_kernel, out_shape=(shape(block, F32), shape((8, lan...  36.2 us
    pallas_call x1, Pallas kernels, waves_of(): pl.pallas_call(waves_kernel, out_shape=shape((slabs, 2, npw), BF16), in_s...  21.2 us
    pallas_call x1, Pallas kernels, density_of(): pl.pallas_call(field_kernel, out_shape=shape((slabs, N2, N1 // slabs, LAN...  19.8 us
    pallas_call x1, Pallas kernels, middle_of(): pl.pallas_call(middle_kernel, out_shape=(shape(index.shape, F32), shape((...  19.1 us
    pallas_call x1, Pallas kernels, psi_of(): pl.pallas_call(psi_kernel, out_shape=shape((N2, N1, 2 * LANES), BF16), in...  18.9 us
    all_gather x1, waiting for transfers between devices, per_device(): all_bands = lax.all_gather(wave_coeffs, 'band', axis=0, tiled=True)  16.9 us
    pallas_call x1, Pallas kernels, start_of(): pl.pallas_call(start_kernel, out_shape=(shape(coefs.shape, BF16), shape((...  10.3 us
    mul x1, other arithmetic, index_rows(): 2.0 * (xpos.astype(F32) ** 2 / (N1 * N1) + ypos.astype(F32) ** 2 / (N2 *...  4.16 us
  transfers between devices with their start and end apart: 2, of which 1 were waited for; matrix products, arithmetic and copies ran while one was open for 10% of the time, Pallas kernels for 27%

profile of v2, /device:TPU:1, one launch (start us, length us, event | category | flops | bytes accessed | tf_op | source)
XLA Modules:
  0.0 185.4 jit_solution(18301863747785216528)
XLA Ops:
  7.2 1.6 reshape.52
  8.9 0.7 copy.29
  9.6 1.0 pad_convert_fusion
  10.6 0.7 all-gather.4.cloned.1.call-update
  11.3 0.8 reshape.50.coef_ref
  12.1 0.7 reshape.51.map_ref
  12.8 10.3 %start.1 = (bf16[4,2,13824]{2,1,0:T(2,128)(2,1)}, s32[4,1,13824]{2,1,0:T(1,128)}) custom-call(bf16[4,2,13824]{2,1,0:T(2,128)(2,1)} %reshape.50.coef_ref, s32[1,13824]{1,0:T(1,128)} %reshape.51.map_ref), custom_call_target="tpu_custom_call" | custom-call | tf_op jit(solution)/shard_map/start/pallas_call | solution.py:474
  23.1 1.0 copy.30
  24.1 3.1 %convert_reduce_fusion = s32[4,49]{0,1:T(8,128)S(1)} fusion(s32[4,13824]{1,0:T(4,128)S(1)} %bitcast.13, s32[49]{0:T(128)S(1)} %iota_multiply_fusion.1), kind=kLoop, calls=%fused_computation | loop fusion | flops 8128316 | bytes 222164 | tf_op jit(solution)/shard_map/reduce_sum | solution.py:586
  27.3 0.7 fusion.13
  28.0 2.1 %fusion.15 = (f32[4,1,13824]{2,1,0:T(1,128)S(1)}, s32[4,1,13824]{2,1,0:T(1,128)S(1)}) fusion(s32[4,1,13824]{2,1,0:T(1,128)} %get-tuple-element.8), kind=kLoop, calls=%fused_computation.45 | loop fusion | flops 497664 | bytes 663552 | tf_op jit(solution)/shard_map/convert_element_type | solution.py:601
  30.8 4.2 %fusion.7 = (f32[4,1,13824]{2,1,0:T(1,128)S(1)}, f32[4,1,13824]{2,1,0:T(1,128)S(1)}) fusion(s32[4,1,13824]{2,1,0:T(1,128)S(1)} %get-tuple-element.25, s32[4,1,13824]{2,1,0:T(1,128)} %get-tuple-element.8, s32[4]{0:T(128)S(1)} %iota_multiply_fusion), kind=kLoop, calls=%fused_computation.22 | loop fusion | flops 1658880 | bytes 884752 | tf_op jit(solution)/shard_map/mul | solution.py:596
  35.0 1.0 select_maximum_fusion.index_ref
  36.1 1.2 copy-done
  37.3 0.8 multiply_convert_fusion
  38.2 0.6 pad_bitcast_fusion
  38.8 0.7 copy.23.fwd_z_ref
  39.5 0.7 pad_dynamic-slice_fusion.share_ref
  40.2 0.6 concatenate.3.starts_ref
  41.1 0.7 dynamic_slice.6.energy_ref
  41.8 0.6 copy-done.1
  42.3 18.9 %psi.1.psi_ref = bf16[96,96,256]{2,1,0:T(8,128)(2,1)} custom-call(s32[4,50]{1,0:T(4,128)} %concatenate.3.starts_ref, f32[4,8,14848]{2,1,0:T(8,128)} %copy-done.1, bf16[96,96]{1,0:T(8,128)(2,1)} %get-tuple-element.31.inv_x_ref.inv_y_ref, bf16[96,96]{1,0:T(8,128)(2,1)} %get-tuple-element.31.inv_x_ref.inv_y_ref, bf16[96,128]{1,0:T(8,128)(2,1)} %get-tuple-element.29.inv_z_ref), custom_call_target="tpu_custom_call" | custom-call | flops 20000000000 | bytes 8000000 | tf_op jit(solution)/shard_map/psi/pallas_call | solution.py:486
  61.2 21.2 %waves.1.waves_ref = bf16[4,2,13824]{2,1,0:T(2,128)(2,1)} custom-call(s32[4,50]{1,0:T(4,128)} %concatenate.3.starts_ref, f32[4,8,14848]{2,1,0:T(8,128)} %copy-done.1, bf16[96,96,256]{2,1,0:T(8,128)(2,1)} %psi.1.psi_ref, bf16[4,96,24,128]{3,2,1,0:T(8,128)(2,1)} %bitcast.14, bf16[96,96]{1,0:T(8,128)(2,1)} %copy-done.4, bf16[96,96]{1,0:T(8,128)(2,1)} %copy-done.4, ...), custom_call_target="tpu_custom_call" | custom-call | flops 20000000000 | bytes 8000000 | tf_op jit(solution)/shard_map/waves/pallas_call | solution.py:500
  82.4 16.9 %all-gather.4.cloned.1.call-done.bands_ref = bf16[64,13824]{1,0:T(8,128)(2,1)} async-done(((bf16[8,13824]{1,0:T(8,128)(2,1)}), bf16[64,13824]{1,0:T(8,128)(2,1)}) %all-gather.4.cloned.1.call-update) | async-done | bytes 1769488 | tf_op jit(solution)/shard_map/all_gather | solution.py:615
  99.3 19.1 %middle.1 = (f32[4,8,14848]{2,1,0:T(8,128)}, f32[2,128]{1,0:T(2,128)}) custom-call(bf16[4,2,13824]{2,1,0:T(2,128)(2,1)} %waves.1.waves_ref, bf16[64,13824]{1,0:T(8,128)(2,1)} %all-gather.4.cloned.1.call-done.bands_ref, f32[4,8,14848]{2,1,0:T(8,128)} %copy-done, f32[2]{0:T(128)} %dynamic_slice.6.energy_ref), custom_call_target="tpu_custom_call" | custom-call | tf_op jit(solution)/shard_map/middle/pallas_call | solution.py:520
  118.4 1.2 broadcast_multiply_fusion.step_ref
  119.6 19.8 %field.1.density_ref = bf16[4,96,24,128]{3,2,1,0:T(8,128)(2,1)} custom-call(s32[4,50]{1,0:T(4,128)} %concatenate.3.starts_ref, f32[4,8,14848]{2,1,0:T(8,128)} %get-tuple-element.10.data_ref, f32[2,128]{1,0:T(2,128)} %broadcast_multiply_fusion.step_ref, bf16[96,96,256]{2,1,0:T(8,128)(2,1)} %psi.1.psi_ref, ...), custom_call_target="tpu_custom_call" | custom-call | flops 20000000000 | bytes 8000000 | tf_op jit(solution)/shard_map/field/pallas_call | solution.py:540
  139.4 36.2 %reduce.1 = (f32[12,24,128]{2,1,0:T(8,128)}, f32[8,128]{1,0:T(8,128)}) custom-call(bf16[4,96,24,128]{3,2,1,0:T(8,128)(2,1)} %field.1.density_ref, f32[12,24,128]{2,1,0:T(8,128)} %pad_dynamic-slice_fusion.share_ref), custom_call_target="tpu_custom_call" | custom-call | tf_op jit(solution)/shard_map/reduce/pallas_call | solution.py:556
  175.6 0.9 slice_bitcast_fusion
  176.6 0.8 reshape.53
  177.3 0.7 slice.15
  178.0 0.6 copy.25
  (24 shorter events, 0.7 us)
Async XLA Ops:
  7.2 54.0 %all-gather.6.cloned.1.call-start = ((), (), s32[]{:S(2)}) async-start(), calls=%async_computation.1 | async-start | bytes 2949120 | tf_op jit(solution)/shard_map/all_gather | solution.py:618
  8.8 2.5 %copy-start.2 = (bf16[8,13824]{1,0:T(8,128)(2,1)S(1)}, bf16[8,13824]{1,0:T(8,128)(2,1)}, u32[]{:S(2)}) copy-start(bf16[8,13824]{1,0:T(8,128)(2,1)} %param.4) | copy-start | bytes 663556
  9.6 2.6 %copy-start.5 = (s32[13824]{0:T(1024)S(1)}, s32[13824]{0:T(1024)}, u32[]{:S(2)}) copy-start(s32[13824]{0:T(1024)} %param.7) | copy-start | bytes 165892
  10.6 88.7 %all-gather.4.cloned.1.call-start = ((), (), s32[]{:S(2)}) async-start(), calls=%async_computation | async-start | bytes 1990656 | tf_op jit(solution)/shard_map/all_gather | solution.py:615
  36.0 1.3 copy-start
  36.0 4.8 %copy-start.3 = (bf16[4,2,13824]{2,1,0:T(2,128)(2,1)S(1)}, bf16[4,2,13824]{2,1,0:T(2,128)(2,1)}, u32[]{:S(2)}) copy-start(bf16[4,2,13824]{2,1,0:T(2,128)(2,1)} %get-tuple-element.9) | copy-start | bytes 663556
  36.1 4.9 %copy-start.6 = (f32[8]{0:T(128)S(1)}, f32[8]{0:T(128)}, u32[]{:S(2)}) copy-start(f32[8]{0:T(128)} %param.5) | copy-start | bytes 100
  38.2 23.1 %copy-start.4 = (bf16[96,96]{1,0:T(8,128)(2,1)}, bf16[96,96]{1,0:T(8,128)(2,1)S(1)}, u32[]{:S(2)}) copy-start(bf16[96,96]{1,0:T(8,128)(2,1)S(1)} %get-tuple-element.30.fwd_x_ref.fwd_y_ref) | copy-start | bytes 55300
  41.0 1.3 copy-start.1
Sparse Core Ops, SparseCore 0:
  10.7 34.9 all-gather.5
  47.9 51.3 all-gather.3

commit v3 on v2

v3 whole, which is shorter than its diff:
```python
import jax
import jax.numpy as jnp
from jax import lax
from jax.experimental import pallas as pl
from jax.experimental.pallas import tpu as pltpu
from jax.sharding import PartitionSpec as P

N1 = 96
N2 = 96
N3 = 96
LANES = 128
WIN = 512
TILE = 2
TILES = N1 // TILE
F32 = jnp.float32
BF16 = jnp.bfloat16
NT = (((1,), (1,)), ((), ()))
MESH = pl.DeviceIdType.MESH


def cosines(n):
    rows = jnp.arange(n, dtype=jnp.int32).astype(jnp.float32)[:, None]
    cols = jnp.arange(n, dtype=jnp.int32).astype(jnp.float32)[None, :]
    table = jnp.sqrt(2.0 / n) * jnp.cos(jnp.pi * rows * (cols + 0.5) / n)
    table = table * jnp.where(rows == 0, jnp.sqrt(0.5), 1.0)
    return table.astype(jnp.bfloat16)


def dot(a, b):
    return jnp.dot(a, b, preferred_element_type=F32)


def dot_nt(a, b):
    return lax.dot_general(a, b, NT, preferred_element_type=F32)


def iota(dims, axis):
    return lax.broadcasted_iota(jnp.int32, dims, axis)


def ones_at(rows, cols):
    return (iota((rows, cols), 0) == iota((rows, cols), 1)).astype(F32).astype(BF16)


def transposed(table):
    return dot_nt(ones_at(table.shape[1], table.shape[1]), table).astype(BF16)


def window_base(starts_ref, s, tile):
    return pl.multiple_of((starts_ref[s, 0, tile] // LANES) * LANES, LANES)


def overflow(starts_ref, slabs):
    total = starts_ref[0, 0, TILES + 1]
    for s in range(1, slabs):
        total = total + starts_ref[s, 0, TILES + 1]
    return total > 0


def hot_rows(rows, tile, cells):
    at = rows[2:3] - (tile * cells).astype(F32)
    return iota((cells, WIN), 0).astype(F32) == at


def hot_z(rows):
    here = iota((N3, WIN), 0).astype(F32) == rows[3:4]
    return here.astype(F32).astype(BF16)


def scatter_window(data_ref, s, base, tile, cells):
    rows = data_ref[s, :, pl.ds(base, WIN)]
    hot = hot_rows(rows, tile, cells)
    both = [jnp.where(hot, rows[0:1], 0.0), jnp.where(hot, rows[1:2], 0.0)]
    return dot_nt(jnp.concatenate(both, axis=0).astype(BF16), hot_z(rows))


def plane_of(parts, t, ny):
    cells = TILE * ny
    rows = [p[b * cells + t * ny : b * cells + (t + 1) * ny] for b in range(2) for p in parts]
    return jnp.concatenate(rows, axis=0)


def scatter_planes(starts_ref, data_ref, plane_ref):
    slabs = data_ref.shape[0]
    ny = N2 // slabs
    cells = TILE * ny
    unroll = 4

    @pl.loop(0, TILES // unroll)
    def _(group):
        for u in range(unroll):
            tile = group * unroll + u
            parts = [
                scatter_window(data_ref, s, window_base(starts_ref, s, tile), tile, cells)
                for s in range(slabs)
            ]
            for t in range(TILE):
                plane_ref[tile * TILE + t] = plane_of(parts, t, ny).astype(BF16)

    @pl.when(overflow(starts_ref, slabs))
    def _():
        @pl.loop(0, TILES)
        def _(tile):
            parts = []
            for s in range(slabs):
                base = window_base(starts_ref, s, tile)

                def more(i, acc):
                    at = pl.multiple_of(base + i * WIN, LANES)
                    return acc + scatter_window(data_ref, s, at, tile, cells)

                windows = (starts_ref[s, 0, tile + 1] - base + WIN - 1) // WIN
                zero = jnp.zeros((2 * cells, N3), F32)
                parts.append(lax.fori_loop(1, windows, more, zero))
            for t in range(TILE):
                old = plane_ref[tile * TILE + t].astype(F32)
                plane_ref[tile * TILE + t] = (old + plane_of(parts, t, ny)).astype(BF16)


def zy_kernel(starts_ref, data_ref, tab_ref, turned_ref, plane_ref):
    scatter_planes(starts_ref, data_ref, plane_ref)
    inv_y = transposed(tab_ref[...])
    inv_z = dot(tab_ref[...], ones_at(N3, LANES)).astype(BF16)
    width = 16

    @pl.loop(0, N1 // width)
    def _(group):
        first = pl.multiple_of(group * width, width)
        flat = plane_ref[pl.ds(first, width)].reshape(width * 2 * N2, N3)
        z_done = dot(flat, inv_z).astype(BF16)
        done = []
        for u in range(width):
            one = z_done[2 * N2 * u : 2 * N2 * u + N2]
            two = z_done[2 * N2 * u + N2 : 2 * N2 * (u + 1)]
            done.append(dot(inv_y, jnp.concatenate([one, two], axis=1)).astype(BF16))
        turned_ref[:, pl.ds(first, width), :] = jnp.swapaxes(jnp.stack(done, axis=0), 0, 1)


def gather_window(data_ref, wave_ref, sum_ref, s, base, tile, ny):
    cells = TILE * ny
    at = pl.ds(base, WIN)
    rows = data_ref[s, :, at]
    hot = hot_rows(rows, tile, cells)
    mine = wave_ref[s, pl.ds(tile * TILE, TILE)].reshape(TILE * 2 * ny, N3)
    picked = dot(mine, hot_z(rows))
    found = []
    for b in range(2):
        part = jnp.concatenate(
            [picked[(2 * t + b) * ny : (2 * t + b + 1) * ny] for t in range(TILE)], axis=0
        )
        found.append(jnp.sum(jnp.where(hot, part, 0.0), axis=0, keepdims=True))
    sum_ref[s, :, at] += jnp.concatenate(found, axis=0)


def gather_kernel(starts_ref, data_ref, wave_ref, out_ref, sum_ref):
    slabs = data_ref.shape[0]
    ny = N2 // slabs
    sum_ref[...] = jnp.zeros_like(sum_ref)
    several = 4

    @pl.loop(0, TILES // several)
    def _(group):
        for u in range(several):
            tile = group * several + u
            for s in range(slabs):
                gather_window(data_ref, wave_ref, sum_ref, s, window_base(starts_ref, s, tile), tile, ny)

    @pl.when(overflow(starts_ref, slabs))
    def _():
        @pl.loop(0, TILES)
        def _(tile):
            for s in range(slabs):
                base = window_base(starts_ref, s, tile)

                @pl.loop(1, (starts_ref[s, 0, tile + 1] - base + WIN - 1) // WIN)
                def _(i):
                    at = pl.multiple_of(base + i * WIN, LANES)
                    gather_window(data_ref, wave_ref, sum_ref, s, at, tile, ny)

    out_ref[...] = sum_ref[:, :, : out_ref.shape[2]].astype(out_ref.dtype)


SMEM = pl.BlockSpec(memory_space=pltpu.SMEM)
VMEM = pl.BlockSpec(memory_space=pltpu.VMEM)
LIMIT = 32 * 1024 * 1024


def greet(peers):
    barrier = pltpu.get_barrier_semaphore()
    for peer in peers:
        pl.semaphore_signal(barrier, inc=1, device_id=peer, device_id_type=MESH)
    pl.semaphore_wait(barrier, len(peers))


def remote(src, dst, send_sem, recv_sem, peer):
    return pltpu.make_async_remote_copy(
        src_ref=src, dst_ref=dst, send_sem=send_sem, recv_sem=recv_sem, device_id=peer, device_id_type=MESH
    )


def send(src, dst, send_sem, recv_sem, peer):
    copy = remote(src, dst, send_sem, recv_sem, peer)
    copy.start()
    return copy


def wait_all(copies):
    for copy in copies:
        copy.wait()


def slab_peers(slabs):
    me = lax.axis_index("slab")
    return [lax.rem(me + d, slabs) for d in range(1, slabs)]


def place():
    band, slab = lax.axis_index("band"), lax.axis_index("slab")
    return band // 4, slab // 2, lax.rem(band, 4), lax.rem(slab, 2)


def device(y_hi, y_lo, z, core):
    return {"band": y_hi * 4 + z, "slab": y_lo * 2 + core}


def start_kernel(
    coef_ref, map_ref, data_ref, starts_ref, own_coef, own_map, coefs_ref, maps_ref, send_sem, recv_sem
):
    slabs, two, npw = coefs_ref.shape
    ny = N2 // slabs
    me = lax.axis_index("slab")
    peers = slab_peers(slabs)
    chunk = 1536
    for r in range(npw // LANES):
        own_map[0:1, r * LANES : (r + 1) * LANES] = map_ref[r : r + 1, :]
    for i in range(npw // chunk):
        at = pl.ds(i * chunk, chunk)
        block = coef_ref[:, at].astype(F32)
        for t in range(slabs):
            own_coef[t, :, at] = block[two * t : two * (t + 1)].astype(BF16)
    greet([{"slab": peer} for peer in peers])
    coef_copies = []
    for i, peer in enumerate(peers):
        to = {"slab": peer}
        coef_copies.append(send(own_coef.at[peer], coefs_ref.at[me], send_sem.at[0, i], recv_sem.at[0, i], to))
    coefs_ref[me] = own_coef[me]
    edges = iota((56, LANES), 0) * (TILE * ny * N3)
    below = jnp.zeros((56, LANES), jnp.int32)
    for r in range(npw // LANES):
        below = below + (own_map[0:1, r * LANES : (r + 1) * LANES] < edges).astype(jnp.int32)
    count = jnp.sum(below.astype(F32), axis=1, keepdims=True)
    spread = jnp.where(iota((56, LANES), 0) == iota((56, LANES), 1), count, 0.0)
    starts = jnp.sum(spread, axis=0, keepdims=True).astype(jnp.int32)
    after = pltpu.roll(starts, LANES - 1, 1)
    lane = iota((1, LANES), 1)
    over = (after > jnp.bitwise_and(starts, -LANES) + WIN) & (lane < TILES)
    flag = jnp.max(over.astype(F32), axis=1, keepdims=True).astype(jnp.int32)
    own_map[0:1, npw : npw + LANES] = jnp.where(lane == TILES + 1, flag, starts)
    copies = []
    for i, peer in enumerate(peers):
        to = {"slab": peer}
        copies.append(send(own_map, maps_ref.at[me], send_sem.at[1, i], recv_sem.at[1, i], to))
    maps_ref[me] = own_map[...]
    data_ref[...] = jnp.full(data_ref.shape, -1.0, F32)
    wait_all(copies)
    for s in range(slabs):
        starts_ref[s] = maps_ref[s, :, npw : npw + LANES]
    y_first = (iota((slabs, 1), 0) * ny).astype(F32)
    for i in range(npw // chunk):
        at = pl.ds(i * chunk, chunk)
        cell = jnp.concatenate([maps_ref[s, :, at] for s in range(slabs)], axis=0).astype(F32)
        row = jnp.floor((cell + 0.5) * (1.0 / N3))
        zpos = cell - row * N3
        xpos = jnp.floor((row + 0.5) * (1.0 / ny))
        ypos = row - xpos * ny + y_first
        kin = 2.0 * (xpos * xpos / (N1 * N1) + ypos * ypos / (N2 * N2) + zpos * zpos / (N3 * N3))
        for s in range(slabs):
            lines = [part[s : s + 1] for part in (row, zpos, kin)]
            data_ref[s, 2:5, at] = jnp.concatenate(lines, axis=0)
    wait_all(coef_copies)
    for s in range(slabs):
        for i in range(npw // chunk):
            at = pl.ds(i * chunk, chunk)
            data_ref[s, 0:2, at] = coefs_ref[s, :, at].astype(F32)


def dense_kernel(
    turned_ref, pot_ref, tab_ref, psi_ref, wave_ref, pots_ref, back_ref, send_sem, recv_sem
):
    slabs = wave_ref.shape[0]
    ny = N2 // slabs
    y_hi, y_lo, z, core = place()
    me = lax.axis_index("slab")
    y = y_hi * 2 + y_lo
    sibling = device(y_hi, y_lo, z, 1 - core)

    def around(step, other):
        to = lax.rem(y + step + 4, 4)
        return device(to // 2, lax.rem(to, 2), z, other)

    for i in range(3):
        at = pl.ds(i * 3072, 3072)
        pots_ref[me, :, at] = pot_ref[:, at].astype(BF16)
    greet([sibling] + [around(step, other) for step in (-1, 1) for other in (0, 1)])
    mine = pots_ref.at[me]
    copies = [send(mine, mine, send_sem.at[2], recv_sem.at[2], sibling)]
    for other in (0, 1):
        to = around(2 * core - 1, other)
        copies.append(send(mine, mine, send_sem.at[other], recv_sem.at[core], to))

    inv_x = transposed(tab_ref[...])
    unroll = 8

    @pl.loop(0, N2 // unroll)
    def _(group):
        for u in range(unroll):
            row = group * unroll + u
            psi_ref[row] = dot(inv_x, turned_ref[row]).astype(BF16)

    copies[0].wait()
    for copy in copies[1:]:
        copy.wait_send()
    for other in (0, 1):
        slot = pots_ref.at[(1 - y_lo) * 2 + other]
        remote(slot, slot, send_sem.at[other], recv_sem.at[other], sibling).wait_recv()

    width = 16
    lane = iota((N1 // slabs, LANES), 1)

    @pl.loop(0, N2 // width)
    def _(group):
        first = pl.multiple_of(group * width, width)
        done = []
        for v in range(width // 4):
            quads = [[], [], [], []]
            for s in range(slabs):
                parts = []
                for j in range(3):
                    off = pl.multiple_of(group * (width * N3) + (3 * v + j) * LANES, LANES)
                    parts.append(pots_ref[s, :, pl.ds(off, LANES)].astype(F32))
                a, b, c = parts
                quads[0].append(a)
                quads[1].append(jnp.where(lane < 32, pltpu.roll(a, 32, 1), pltpu.roll(b, 32, 1)))
                quads[2].append(jnp.where(lane < 64, pltpu.roll(b, 64, 1), pltpu.roll(c, 64, 1)))
                quads[3].append(pltpu.roll(c, 96, 1))
            for u in range(4):
                pot = jnp.concatenate(quads[u], axis=0)
                psi = psi_ref[first + 4 * v + u].astype(F32)
                product = jnp.concatenate([pot * psi[:, :LANES], pot * psi[:, LANES:]], axis=1)
                done.append(dot(tab_ref[...], product.astype(BF16)).astype(BF16))
        back_ref[:, pl.ds(first, width), :] = jnp.swapaxes(jnp.stack(done, axis=0), 0, 1)

    fwd_z = dot_nt(ones_at(LANES, N3), tab_ref[...]).astype(BF16)

    @pl.loop(0, N1 // unroll)
    def _(group):
        done = []
        for u in range(unroll):
            y_done = dot(tab_ref[...], back_ref[group * unroll + u]).astype(BF16)
            done += [y_done[:, :LANES], y_done[:, LANES:]]
        waves = dot(jnp.concatenate(done, axis=0), fwd_z)
        for u in range(unroll):
            for s in range(slabs):
                one = waves[2 * u * N2 + s * ny : 2 * u * N2 + (s + 1) * ny]
                two = waves[(2 * u + 1) * N2 + s * ny : (2 * u + 1) * N2 + (s + 1) * ny]
                wave_ref[s, group * unroll + u] = jnp.concatenate([one, two], axis=0).astype(BF16)


def middle_kernel(
    waves_ref, bands_ref, index_ref, energy_ref, data_ref, step_ref,
    got_ref, corr_ref, rhs_ref, back_ref, total_ref, send_sem, recv_sem,
):
    slabs, two, npw = waves_ref.shape
    chunk = 1536
    me = lax.axis_index("slab")
    peers = slab_peers(slabs)
    greet([{"slab": peer} for peer in peers])
    copies = []
    for i, peer in enumerate(peers):
        to = {"slab": peer}
        copies.append(send(waves_ref.at[peer], got_ref.at[me], send_sem.at[0, i], recv_sem.at[0, i], to))
    got_ref[me] = waves_ref[me]
    data_ref[...] = index_ref[...]
    wait_all(copies)

    def waves_at(at):
        return jnp.concatenate([got_ref[t, :, at].astype(F32) for t in range(slabs)], axis=0)

    total = jnp.zeros(total_ref.shape, F32)
    for i in range(npw // chunk):
        at = pl.ds(i * chunk, chunk)
        total = total + dot_nt(waves_at(at).astype(BF16), bands_ref[:, at])
    total_ref[...] = total

    copies = []
    for i, peer in enumerate(peers):
        to = {"slab": peer}
        copies.append(send(total_ref, corr_ref.at[i], send_sem.at[1, i], recv_sem.at[1, i], to))
    wait_all(copies)
    correlation = total_ref[...]
    for i in range(slabs - 1):
        correlation = correlation + corr_ref[i]
    correlation = correlation.astype(BF16)

    for i in range(npw // chunk):
        at = pl.ds(i * chunk, chunk)
        rhs = (waves_at(at) - dot(correlation, bands_ref[:, at])).astype(BF16)
        for t in range(slabs):
            rhs_ref[t, :, at] = rhs[two * t : two * (t + 1)]

    copies = []
    for i, peer in enumerate(peers):
        to = {"slab": peer}
        copies.append(send(rhs_ref.at[peer], back_ref.at[me], send_sem.at[2, i], recv_sem.at[2, i], to))
    back_ref[me] = rhs_ref[me]
    wait_all(copies)

    numer = jnp.zeros((two, chunk), F32)
    denom = jnp.zeros((two, chunk), F32)
    energy = jnp.concatenate([jnp.full((1, chunk), energy_ref[b], F32) for b in range(two)], axis=0)
    for s in range(slabs):
        for i in range(npw // chunk):
            at = pl.ds(i * chunk, chunk)
            mine = back_ref[s, :, at].astype(F32)
            data_ref[s, 0:2, at] = mine
            squares = mine * mine
            numer = numer + squares
            denom = denom + (index_ref[s, 4:5, at] - energy) * squares
    step = -jnp.sum(numer, axis=1, keepdims=True) / jnp.sum(denom, axis=1, keepdims=True)
    scale = 4.0 * N1 * N2 * N3 / bands_ref.shape[0]
    step_ref[...] = jnp.broadcast_to(scale * step, step_ref.shape)


PART_A = 5
PART_B = 4
PARTS = PART_A + PART_B


def end_kernel(
    turned_ref, psi_ref, step_ref, pot_ref, tab_ref, out_ref, projected_ref,
    dens_ref, from_core, a_ref, b_ref, a_from_y, b_from_z, a_sum, b_sum, a_from_z, b_from_y,
    pots_ref, sums_ref, from_sums, core_send, core_recv, pot_send, pot_recv, a_send, a_recv, b_send, b_recv,
    a2_send, a2_recv, b2_send, b2_recv, sum_send, sum_recv,
):
    perts, planes, width = pots_ref.shape
    slabs = dens_ref.shape[0]
    y_hi, y_lo, z, core = place()
    pert, band = lax.axis_index("pert"), lax.axis_index("band")
    sibling = device(y_hi, y_lo, z, 1 - core)
    y_coords = [(1 - y_hi, y_lo), (1 - y_hi, 1 - y_lo), (y_hi, 1 - y_lo)]
    y_peers = [device(a, b, z, core) for a, b in y_coords]
    y_others = [device(a, b, z, 1 - core) for a, b in y_coords]
    z_coords = [lax.rem(z + d, 4) for d in range(1, 4)]
    z_peers = [device(y_hi, y_lo, c, core) for c in z_coords]
    p_peers = [{"pert": lax.rem(pert + d, perts)} for d in range(1, perts)]
    greet([sibling] + y_peers + y_others + z_peers + p_peers)

    pots_ref[pert] = pot_ref[:, pl.ds(pl.multiple_of(band * width, LANES), width)]
    pot_copies = []
    for i, peer in enumerate(p_peers):
        mine = pots_ref.at[pert]
        pot_copies.append(send(mine, mine, pot_send.at[i], pot_recv.at[i], peer))

    inv_x = transposed(tab_ref[...])
    lane = iota((N1, LANES), 1)
    half = 4 * PARTS

    def density_half(h):
        @pl.loop(0, 6)
        def _(group):
            for v in range(2):
                quad = h * 12 + group * 2 + v
                parts = []
                for u in range(4):
                    row = quad * 4 + u
                    field = dot(inv_x, turned_ref[row]).astype(BF16).astype(F32)
                    terms = psi_ref[row].astype(F32) * field
                    parts.append(step_ref[0:1] * terms[:, :LANES] + step_ref[1:2] * terms[:, LANES:])
                one, two, three = [pltpu.roll(parts[u], LANES - 32 * u, 1) for u in (1, 2, 3)]
                tiles = [
                    jnp.where(lane < 96, parts[0], one),
                    jnp.where(lane < 64, one, two),
                    jnp.where(lane < 32, two, three),
                ]
                for j, tile in enumerate(tiles):
                    for s in range(slabs):
                        dens_ref[s, quad * 3 + j] = tile[s * planes : (s + 1) * planes].astype(BF16)

    halves = [1 - y_hi, y_hi]
    core_copies = []
    for k, h in enumerate(halves):
        density_half(h)
        for l in range(2):
            src = dens_ref.at[l * 2 + 1 - core, pl.ds(h * half, half)]
            core_copies.append(
                send(src, from_core.at[k, l], core_send.at[k, l], core_recv.at[k, l], sibling)
            )

    a_copies, b_copies = [], []
    for k, h in enumerate(halves):
        wait_all(core_copies[2 * k : 2 * k + 2])
        for l in range(2):
            @pl.loop(0, 4)
            def _(c):
                for j in range(PARTS):
                    at = c * PARTS + j
                    total = dens_ref[l * 2 + core, h * half + at].astype(F32) + from_core[k, l, at].astype(F32)
                    if j < PART_A:
                        a_ref[k, l, c, j] = total.astype(BF16)
                    else:
                        b_ref[k, c, l, j - PART_A] = total.astype(BF16)
        targets = [(0, y_lo), (1, 1 - y_lo)] if k == 0 else [(2, 1 - y_lo)]
        for i, l in targets:
            a_copies.append(send(a_ref.at[k, l], a_from_y.at[i], a_send.at[i], a_recv.at[i], y_peers[i]))
        for i, c in enumerate(z_coords):
            b_copies.append(
                send(b_ref.at[k, c], b_from_z.at[k, i], b_send.at[k, i], b_recv.at[k, i], z_peers[i])
            )

    def total_of(pair):
        total = sum(pair(j) for j in range(PARTS))
        total = total[0:8] + total[8:16] + total[16:24]
        return jnp.sum(total, axis=0, keepdims=True)

    wait_all(pot_copies)

    def pot(p, j):
        return pots_ref[p, :, j * LANES : (j + 1) * LANES]

    pairs = [(p, q) for p in range(perts) for q in range(p + 1)]
    sums = [total_of(lambda j: pot(p, j) * pot(q, j)) for p, q in pairs]

    wait_all(a_copies)

    @pl.loop(0, 4)
    def _(c):
        for j in range(PART_A):
            total = a_ref[1, y_lo, c, j].astype(F32)
            for i in range(3):
                total = total + a_from_y[i, c, j].astype(F32)
            a_sum[c, j] = total.astype(BF16)

    copies = []
    for i, c in enumerate(z_coords):
        copies.append(send(a_sum.at[c], a_from_z.at[i], a2_send.at[i], a2_recv.at[i], z_peers[i]))
    wait_all(b_copies)
    for k in range(2):
        for l in range(2):
            for j in range(PART_B):
                total = b_ref[k, z, l, j].astype(F32)
                for i in range(3):
                    total = total + b_from_z[k, i, l, j].astype(F32)
                b_sum[k, l, j] = total.astype(BF16)
    for i, (k, l) in enumerate([(0, y_lo), (0, 1 - y_lo), (1, 1 - y_lo)]):
        copies.append(send(b_sum.at[k, l], b_from_y.at[i], b2_send.at[i], b2_recv.at[i], y_peers[i]))
    wait_all(copies)
    density = []
    for j in range(PARTS):
        if j < PART_A:
            total = a_sum[z, j].astype(F32)
            for i in range(3):
                total = total + a_from_z[i, j].astype(F32)
        else:
            total = b_sum[1, y_lo, j - PART_A].astype(F32)
            for i in range(3):
                total = total + b_from_y[i, j - PART_A].astype(F32)
        density.append(total)
    sums += [total_of(lambda j: pot(p, j) * density[j]) for p in range(perts)]
    sums += [jnp.zeros((1, LANES), F32)] * (16 - len(sums))
    sums_ref[0] = jnp.concatenate(sums, axis=0)

    at = 0
    for level, group in enumerate([[sibling] + y_peers + y_others, z_peers]):
        copies = []
        for i, peer in enumerate(group):
            k = at + i
            copies.append(send(sums_ref.at[level], from_sums.at[k], sum_send.at[k], sum_recv.at[k], peer))
        wait_all(copies)
        total = sums_ref[level]
        for i in range(len(group)):
            total = total + from_sums[at + i]
        sums_ref[level + 1] = total
        at += len(group)

    cells = 1.0 / (N1 * N2 * N3)
    totals = jnp.broadcast_to(jnp.sum(sums_ref[2], axis=1, keepdims=True) * cells, (16, LANES))
    gram = {pair: totals[k : k + 1] for k, pair in enumerate(pairs)}
    rhs = [totals[len(pairs) + p : len(pairs) + p + 1] for p in range(perts)]
    factor = {}
    for p in range(perts):
        for q in range(p + 1):
            value = gram[p, q]
            for k in range(q):
                value = value - factor[p, k] * factor[q, k]
            factor[p, q] = jnp.sqrt(value) if p == q else value / factor[q, q]
    coeffs = []
    for p in range(perts):
        value = rhs[p]
        for k in range(p):
            value = value - factor[p, k] * coeffs[k]
        coeffs.append(value / factor[p, p])
    for p in reversed(range(perts)):
        value = coeffs[p]
        for k in range(p + 1, perts):
            value = value - factor[k, p] * coeffs[k]
        coeffs[p] = value / factor[p, p]
    for j in range(PARTS):
        value = density[j]
        for p in range(perts):
            value = value - coeffs[p] * pot(p, j)
        out_ref[:, j * LANES : (j + 1) * LANES] = value
    projected_ref[...] = jnp.concatenate(rhs + rhs, axis=0)


def cost(flops, moved):
    return pl.CostEstimate(flops=int(flops), bytes_accessed=int(moved), transcendentals=0)


def params(collective=None):
    if collective is None:
        return pltpu.CompilerParams(vmem_limit_bytes=LIMIT)
    return pltpu.CompilerParams(vmem_limit_bytes=LIMIT, collective_id=collective, has_side_effects=True)


def shape(dims, kind):
    return jax.ShapeDtypeStruct(dims, kind)


def sems(*dims):
    return [pltpu.SemaphoreType.DMA(dims)] * 2


def start_of(coefs, wave_map, slabs):
    bands, npw = coefs.shape
    block = (slabs, bands // slabs, npw)
    return pl.pallas_call(
        start_kernel,
        out_shape=(shape((slabs, 8, npw + 2 * WIN), F32), shape((slabs, 1, LANES), jnp.int32)),
        in_specs=[VMEM] * 2,
        out_specs=(VMEM, VMEM),
        scratch_shapes=[
            pltpu.VMEM(block, BF16),
            pltpu.VMEM((1, npw + LANES), jnp.int32),
            pltpu.VMEM(block, BF16),
            pltpu.VMEM((slabs, 1, npw + LANES), jnp.int32),
        ]
        + sems(2, slabs - 1),
        compiler_params=params(1),
        name="start",
    )(coefs, wave_map.reshape(npw // LANES, LANES))


def zy_of(starts, data, tab):
    return pl.pallas_call(
        zy_kernel,
        out_shape=shape((N2, N1, 2 * LANES), BF16),
        in_specs=[SMEM] + [VMEM] * 2,
        out_specs=VMEM,
        scratch_shapes=[pltpu.VMEM((N1, 2 * N2, N3), BF16)],
        compiler_params=params(),
        cost_estimate=cost(2e10, 8e6),
        name="scatter_zy",
    )(starts, data, tab)


def dense_of(turned, pot, tab, slabs):
    return pl.pallas_call(
        dense_kernel,
        out_shape=(shape((N2, N1, 2 * LANES), BF16), shape((slabs, N1, 2 * N2 // slabs, N3), BF16)),
        in_specs=[VMEM] * 3,
        out_specs=(VMEM, VMEM),
        scratch_shapes=[
            pltpu.VMEM((slabs,) + pot.shape, BF16),
            pltpu.VMEM((N1, N2, 2 * LANES), BF16),
        ]
        + sems(3),
        compiler_params=params(4),
        cost_estimate=cost(2e10, 8e6),
        name="dense",
    )(turned, pot, tab)


def gather_of(starts, data, wave, npw):
    slabs = data.shape[0]
    return pl.pallas_call(
        gather_kernel,
        out_shape=shape((slabs, 2, npw), BF16),
        in_specs=[SMEM] + [VMEM] * 2,
        out_specs=VMEM,
        scratch_shapes=[pltpu.VMEM((slabs, 2, data.shape[2]), F32)],
        compiler_params=params(),
        cost_estimate=cost(2e10, 8e6),
        name="gather",
    )(starts, data, wave)


def middle_of(waves, bands, index, energies):
    slabs, two, npw = waves.shape
    block = pltpu.VMEM(waves.shape, BF16)
    small = (slabs * two, bands.shape[0])
    return pl.pallas_call(
        middle_kernel,
        out_shape=(shape(index.shape, F32), shape((two, LANES), F32)),
        in_specs=[VMEM] * 3 + [SMEM],
        out_specs=(VMEM, VMEM),
        scratch_shapes=[
            block,
            pltpu.VMEM((slabs - 1,) + small, F32),
            block,
            block,
            pltpu.VMEM(small, F32),
        ]
        + sems(3, slabs - 1),
        compiler_params=params(2),
        name="middle",
    )(waves, bands, index, energies)


def end_of(turned, psi, step, pot, tab, slabs, perts):
    planes, cross = pot.shape
    width = cross // 8
    tile = (planes, LANES)
    return pl.pallas_call(
        end_kernel,
        out_shape=(shape((planes, width), F32), shape((8, LANES), F32)),
        in_specs=[VMEM] * 5,
        out_specs=(VMEM, VMEM),
        scratch_shapes=[
            pltpu.VMEM((slabs, 8 * PARTS) + tile, BF16),
            pltpu.VMEM((2, 2, 4 * PARTS) + tile, BF16),
            pltpu.VMEM((2, 2, 4, PART_A) + tile, BF16),
            pltpu.VMEM((2, 4, 2, PART_B) + tile, BF16),
            pltpu.VMEM((3, 4, PART_A) + tile, BF16),
            pltpu.VMEM((2, 3, 2, PART_B) + tile, BF16),
            pltpu.VMEM((4, PART_A) + tile, BF16),
            pltpu.VMEM((2, 2, PART_B) + tile, BF16),
            pltpu.VMEM((3, PART_A) + tile, BF16),
            pltpu.VMEM((3, PART_B) + tile, BF16),
            pltpu.VMEM((perts, planes, width), F32),
            pltpu.VMEM((3, 16, LANES), F32),
            pltpu.VMEM((10, 16, LANES), F32),
        ]
        + sems(2, 2)
        + sems(3)
        + sems(3)
        + sems(2, 3)
        + sems(3)
        + sems(3)
        + sems(10),
        compiler_params=params(3),
        name="density",
    )(turned, psi, step, pot, tab)


def per_device(wave_coeffs, band_energies, trial_potentials, wave_map):
    slabs = lax.axis_size("slab")
    me = lax.axis_index("slab")
    bands, npw = wave_coeffs.shape
    planes, cross = trial_potentials.shape[1:]
    all_bands = lax.all_gather(wave_coeffs, "band", axis=0, tiled=True)
    tab = cosines(N1)
    pot = trial_potentials.reshape(planes, cross)
    energies = lax.dynamic_slice_in_dim(band_energies, me * (bands // slabs), bands // slabs, 0)
    data, starts = start_of(wave_coeffs, wave_map, slabs)
    turned = zy_of(starts, data, tab)
    psi, wave = dense_of(turned, pot, tab, slabs)
    waves = gather_of(starts, data, wave, npw)
    data, step = middle_of(waves, all_bands, data, energies)
    turned = zy_of(starts, data, tab)
    residual, projected = end_of(turned, psi, step, pot, tab, slabs, lax.axis_size("pert"))
    return (residual.reshape(1, planes, -1), projected[: lax.axis_size("pert"), :1])


def solution(mesh):
    return jax.shard_map(
        per_device,
        mesh=mesh,
        in_specs=(P("band", "slab"), P("band"), P("pert", "slab", None), P("slab")),
        out_specs=(P("pert", "slab", "band"), P(None, "pert")),
        check_vma=False,
    )
```

time: 186 us -> 142 us (0.76)
  waiting for transfers between devices: 17.6 us -> 0.7 us
  other arithmetic: 13.5 us -> 0.26 us
  local copies, waits for them, and re-layouts: 14 us -> 7.33 us
  Pallas kernels: 125 us -> 119 us
    all_gather x1, waiting for transfers between devices: 16.9 us -> 0.02 us  [per_device(): all_bands = lax.all_gather(wave_coeffs, 'band', axis=0, tiled=True)]
    pallas_call x5 -> x6, Pallas kernels: 106 us -> 97.1 us  [the longest x1 29.6 us: end_of(): pl.pallas_call(end_kernel, out_shape=(shape((planes, width), F32), shape(...]
    mul x4 -> x0, other arithmetic: 5.39 us -> none  [the longest x1 4.16 us: index_rows(): 2.0 * (xpos.astype(F32) ** 2 / (N1 * N1) + ypos.astype(F32) ** 2 / (N2 *...]
    reshape x5 -> x0, local copies, waits for them, and re-layouts: 4.5 us -> none  [the longest x2 2.32 us: per_device(): turned = trial_potentials.reshape(planes, N2, N3).swapaxes(0, 1)]
    pallas_call x1, Pallas kernels: 19.1 us -> 22.3 us  [middle_of(): pl.pallas_call(middle_kernel, out_shape=(shape(index.shape, F32), shape((...]
    reduce_sum x1 -> x0, other arithmetic: 3.13 us -> none  [tile_starts(): jnp.sum((maps[:, None, :] < edges[None, :, None]).astype(jnp.int32), axis=2)]
    unnamed x17 -> x16, local copies, waits for them, and re-layouts: 3.5 us -> 6.6 us
    transpose x4 -> x0, local copies, waits for them, and re-layouts: 2.29 us -> none  [the longest x2 1.33 us: per_device(): waves = waves_of(starts, data, psi, pot, tab_x, tab_y, inv_z.T, npw)]
  transfers between devices with their start and end apart: 2 -> 1, of which waited for: 1 -> 0; matrix products, arithmetic and copies ran while one was open for 10% -> 1% of each run, Pallas kernels for 27% -> 39%
where the time goes in v3:
time: 142 us
  Pallas kernels  119 us (84%)
  between operations  14.2 us (10%)
  local copies, waits for them, and re-layouts  7.33 us (5%)
    pallas_call x1, Pallas kernels, end_of(): pl.pallas_call(end_kernel, out_shape=(shape((planes, width), F32), shape(...  29.6 us
    pallas_call x2, Pallas kernels, zy_of(): pl.pallas_call(zy_kernel, out_shape=shape((N2, N1, 2 * LANES), BF16), in_...  25.3 us
    pallas_call x1, Pallas kernels, dense_of(): pl.pallas_call(dense_kernel, out_shape=(shape((N2, N1, 2 * LANES), BF16),...  23.7 us
    pallas_call x1, Pallas kernels, middle_of(): pl.pallas_call(middle_kernel, out_shape=(shape(index.shape, F32), shape((...  22.3 us
    pallas_call x1, Pallas kernels, start_of(): pl.pallas_call(start_kernel, out_shape=(shape((slabs, 8, npw + 2 * WIN),...  9.54 us
    pallas_call x1, Pallas kernels, gather_of(): pl.pallas_call(gather_kernel, out_shape=shape((slabs, 2, npw), BF16), in_...  8.96 us
    unnamed x16, local copies, waits for them, and re-layouts  6.6 us
  transfers between devices with their start and end apart: 1, of which 0 were waited for; matrix products, arithmetic and copies ran while one was open for 1% of the time, Pallas kernels for 39%

profile of v3, /device:TPU:1, one launch (start us, length us, event | category | flops | bytes accessed | tf_op | source)
XLA Modules:
  0.0 142.0 jit_solution(6986872828125691117)
XLA Ops:
  7.2 0.0 all-gather.2.cloned.1.call-start
  7.2 0.7 all-gather.2.cloned.1.call-update
  7.9 0.0 copy-start.3
  7.9 0.9 copy-done.3
  8.9 0.0 copy-start.4
  8.9 0.8 copy-done.4
  9.7 9.5 %start.1 = (f32[4,8,14848]{2,1,0:T(8,128)S(1)}, s32[4,1,128]{2,1,0:T(1,128)S(1)}) custom-call(bf16[8,13824]{1,0:T(8,128)(2,1)S(1)} %copy-done.3, s32[108,128]{1,0:T(8,128)S(1)} %bitcast.8), custom_call_target="tpu_custom_call" | custom-call | tf_op jit(solution)/shard_map/start/pallas_call | solution.py:636
  19.2 0.7 dynamic_slice.3.energy_ref
  20.0 0.2 multiply_convert_fusion.tab_ref
  20.2 0.0 copy-start.2
  20.2 12.7 %scatter_zy.2.turned_ref = bf16[96,96,256]{2,1,0:T(8,128)(2,1)S(1)} custom-call(s32[4,1,128]{2,1,0:T(1,128)S(1)} %get-tuple-element.10.starts_ref, f32[4,8,14848]{2,1,0:T(8,128)S(1)} %get-tuple-element.11.data_ref.index_ref, bf16[96,96]{1,0:T(8,128)(2,1)S(1)} %multiply_convert_fusion.tab_ref), custom_call_target="tpu_custom_call" | custom-call | flops 20000000000 | bytes 8000000 | tf_op jit(solution)/shard_map/scatter_zy/pallas_call | solution.py:654
  32.9 0.0 copy-done.2
  32.9 23.7 %dense.1 = (bf16[96,96,256]{2,1,0:T(8,128)(2,1)S(1)}, bf16[4,96,48,96]{3,2,1,0:T(8,128)(2,1)S(1)}) custom-call(bf16[96,96,256]{2,1,0:T(8,128)(2,1)S(1)} %scatter_zy.2.turned_ref, f32[24,9216]{1,0:T(8,128)S(1)} %bitcast.5, bf16[96,96]{1,0:T(8,128)(2,1)S(1)} %multiply_convert_fusion.tab_ref), custom_call_target="tpu_custom_call" | custom-call | flops 20000000000 | bytes 8000000 | tf_op jit(solution)/shard_map/dense/pallas_call | solution.py:667
  56.6 0.0 copy-start
  56.6 2.1 %copy-done = bf16[96,96,256]{2,1,0:T(8,128)(2,1)} copy-done((bf16[96,96,256]{2,1,0:T(8,128)(2,1)}, bf16[96,96,256]{2,1,0:T(8,128)(2,1)S(1)}, u32[]{:S(2)}) %copy-start) | copy-done | bytes 4718616
  58.8 9.0 %gather.1.waves_ref = bf16[4,2,13824]{2,1,0:T(2,128)(2,1)S(1)} custom-call(s32[4,1,128]{2,1,0:T(1,128)S(1)} %get-tuple-element.10.starts_ref, f32[4,8,14848]{2,1,0:T(8,128)S(1)} %get-tuple-element.11.data_ref.index_ref, bf16[4,96,48,96]{3,2,1,0:T(8,128)(2,1)S(1)} %get-tuple-element.12.wave_ref), custom_call_target="tpu_custom_call" | custom-call | flops 20000000000 | bytes 8000000 | tf_op jit(solution)/shard_map/gather/pallas_call | solution.py:685
  67.7 0.0 all-gather.2.cloned.1.call-done.bands_ref
  67.8 0.0 copy-start.1
  67.8 1.5 %copy-done.1 = bf16[64,13824]{1,0:T(8,128)(2,1)S(1)} copy-done((bf16[64,13824]{1,0:T(8,128)(2,1)S(1)}, bf16[64,13824]{1,0:T(8,128)(2,1)}, u32[]{:S(2)}) %copy-start.1) | copy-done | bytes 1769496
  69.2 0.0 slice-start
  69.2 22.3 %middle.1 = (f32[4,8,14848]{2,1,0:T(8,128)S(1)}, f32[2,128]{1,0:T(2,128)S(1)}) custom-call(bf16[4,2,13824]{2,1,0:T(2,128)(2,1)S(1)} %gather.1.waves_ref, bf16[64,13824]{1,0:T(8,128)(2,1)S(1)} %copy-done.1, f32[4,8,14848]{2,1,0:T(8,128)S(1)} %get-tuple-element.11.data_ref.index_ref, f32[2]{0:T(128)S(1)} %dynamic_slice.3.energy_ref), custom_call_target="tpu_custom_call" | custom-call | tf_op jit(solution)/shard_map/middle/pallas_call | solution.py:701
  91.6 0.0 slice-start.1
  91.6 12.7 %scatter_zy.3.turned_ref = bf16[96,96,256]{2,1,0:T(8,128)(2,1)S(1)} custom-call(s32[4,1,128]{2,1,0:T(1,128)S(1)} %get-tuple-element.10.starts_ref, f32[4,8,14848]{2,1,0:T(8,128)S(1)} %get-tuple-element.13.data_ref, bf16[96,96]{1,0:T(8,128)(2,1)S(1)} %multiply_convert_fusion.tab_ref), custom_call_target="tpu_custom_call" | custom-call | flops 20000000000 | bytes 8000000 | tf_op jit(solution)/shard_map/scatter_zy/pallas_call | solution.py:654
  104.3 0.0 slice-done
  104.3 0.0 slice-done.1
  104.3 29.6 %density.1 = (f32[24,1152]{1,0:T(8,128)S(1)}, f32[8,128]{1,0:T(8,128)S(1)}) custom-call(bf16[96,96,256]{2,1,0:T(8,128)(2,1)S(1)} %scatter_zy.3.turned_ref, bf16[96,96,256]{2,1,0:T(8,128)(2,1)S(1)} %bitcast.4, f32[2,128]{1,0:T(2,128)S(1)} %get-tuple-element.15.step_ref, f32[24,9216]{1,0:T(8,128)S(1)} %bitcast.6, bf16[96,96]{1,0:T(8,128)(2,1)S(1)} %multiply_convert_fusion.tab_ref), custom_call_target="tpu_custom_call" | custom-call | tf_op jit(solution)/shard_map/density/pallas_call | solution.py:723
  133.9 0.6 copy.6
  134.5 0.6 copy.8
  (4 shorter events, 0.0 us)
Async XLA Ops:
  7.2 60.6 %all-gather.2.cloned.1.call-start = ((), (), s32[]{:S(2)}) async-start(), calls=%async_computation | async-start | bytes 1990656 | tf_op jit(solution)/shard_map/all_gather | solution.py:760
  7.9 0.9 copy-start.3
  8.9 0.8 copy-start.4
  20.2 12.7 %copy-start.2 = (f32[1,24,9216]{2,1,0:T(8,128)S(1)}, f32[1,24,9216]{2,1,0:T(8,128)}, u32[]{:S(2)}) copy-start(f32[1,24,9216]{2,1,0:T(8,128)} %param.6) | copy-start | bytes 2654212
  56.6 2.1 %copy-start = (bf16[96,96,256]{2,1,0:T(8,128)(2,1)}, bf16[96,96,256]{2,1,0:T(8,128)(2,1)S(1)}, u32[]{:S(2)}) copy-start(bf16[96,96,256]{2,1,0:T(8,128)(2,1)S(1)} %get-tuple-element.14.psi_ref) | copy-start | bytes 14155780
  67.8 1.5 %copy-start.1 = (bf16[64,13824]{1,0:T(8,128)(2,1)S(1)}, bf16[64,13824]{1,0:T(8,128)(2,1)}, u32[]{:S(2)}) copy-start(bf16[64,13824]{1,0:T(8,128)(2,1)} %all-gather.2.cloned.1.call-done.bands_ref) | copy-start | bytes 5308420
  69.2 35.1 %slice-start = ((s8[4718592]{0:T(1024)(128)(4,1)}), s8[4194304]{0:T(1024)(128)(4,1)S(1)}, s32[]{:S(2)}) async-start(s8[4718592]{0:T(1024)(128)(4,1)} %bitcast.3), calls=%async_computation.1 | async-start | bytes 8388608
  91.6 12.7 %slice-start.1 = ((s8[4718592]{0:T(1024)(128)(4,1)}), s8[524288]{0:T(1024)(128)(4,1)S(1)}, s32[]{:S(2)}) async-start(s8[4718592]{0:T(1024)(128)(4,1)} %bitcast.3), calls=%async_computation.2 | async-start | bytes 1048576
Sparse Core Ops, SparseCore 0:
  10.3 54.8 all-gather.1

commit v4 on v3

--- a/solution.py
+++ b/solution.py
@@ -12,6 +12,7 @@
 WIN = 512
 TILE = 2
 TILES = N1 // TILE
+QUARTERS = 4
 F32 = jnp.float32
 BF16 = jnp.bfloat16
 NT = (((1,), (1,)), ((), ()))
@@ -177,7 +178,9 @@
                     at = pl.multiple_of(base + i * WIN, LANES)
                     gather_window(data_ref, wave_ref, sum_ref, s, at, tile, ny)
 
-    out_ref[...] = sum_ref[:, :, : out_ref.shape[2]].astype(out_ref.dtype)
+    part = out_ref.shape[3]
+    for q in range(out_ref.shape[1]):
+        out_ref[:, q] = sum_ref[:, :, q * part : (q + 1) * part].astype(out_ref.dtype)
 
 
 SMEM = pl.BlockSpec(memory_space=pltpu.SMEM)
@@ -285,7 +288,8 @@
 
 
 def dense_kernel(
-    turned_ref, pot_ref, tab_ref, psi_ref, wave_ref, pots_ref, back_ref, send_sem, recv_sem
+    turned_ref, pot_ref, coef_ref, tab_ref, psi_ref, wave_ref, bands_ref,
+    pots_ref, back_ref, send_sem, recv_sem, coef_send, coef_recv,
 ):
     slabs = wave_ref.shape[0]
     ny = N2 // slabs
@@ -301,7 +305,10 @@
     for i in range(3):
         at = pl.ds(i * 3072, 3072)
         pots_ref[me, :, at] = pot_ref[:, at].astype(BF16)
-    greet([sibling] + [around(step, other) for step in (-1, 1) for other in (0, 1)])
+    steps = [(a, b) for a in range(2) for b in range(4) if a + b > 0]
+    others = [(lax.rem(y_hi + a, 2), lax.rem(z + b, 4)) for a, b in steps]
+    members = [device(a, y_lo, b, core) for a, b in others]
+    greet([sibling] + [around(step, other) for step in (-1, 1) for other in (0, 1)] + members)
     mine = pots_ref.at[me]
     copies = [send(mine, mine, send_sem.at[2], recv_sem.at[2], sibling)]
     for other in (0, 1):
@@ -323,6 +330,16 @@
     for other in (0, 1):
         slot = pots_ref.at[(1 - y_lo) * 2 + other]
         remote(slot, slot, send_sem.at[other], recv_sem.at[other], sibling).wait_recv()
+
+    part = bands_ref.shape[3]
+    at = pl.ds(pl.multiple_of(z * part, LANES), part)
+    bands_ref[y_hi, z] = coef_ref[:, at]
+    copies = []
+    for i, (_, b) in enumerate(others):
+        at = pl.ds(pl.multiple_of(b * part, LANES), part)
+        copies.append(
+            send(coef_ref.at[:, at], bands_ref.at[y_hi, z], coef_send.at[i], coef_recv.at[i], members[i])
+        )
 
     width = 16
     lane = iota((N1 // slabs, LANES), 1)
@@ -365,69 +382,82 @@
                 two = waves[(2 * u + 1) * N2 + s * ny : (2 * u + 1) * N2 + (s + 1) * ny]
                 wave_ref[s, group * unroll + u] = jnp.concatenate([one, two], axis=0).astype(BF16)
 
+    wait_all(copies)
+
 
 def middle_kernel(
     waves_ref, bands_ref, index_ref, energy_ref, data_ref, step_ref,
     got_ref, corr_ref, rhs_ref, back_ref, total_ref, send_sem, recv_sem,
 ):
-    slabs, two, npw = waves_ref.shape
-    chunk = 1536
-    me = lax.axis_index("slab")
-    peers = slab_peers(slabs)
-    greet([{"slab": peer} for peer in peers])
+    slabs, quarters, two, part = waves_ref.shape
+    half, zs, bands, _ = bands_ref.shape
+    chunk = 1152
+    y_hi, y_lo, z, core = place()
+    slab = lax.axis_index("slab")
+    steps = [(a, b) for a in range(quarters) for b in range(slabs) if a + b > 0]
+    others = [(lax.rem(z + a, quarters), lax.rem(slab + b, slabs)) for a, b in steps]
+    peers = [{"band": y_hi * 4 + c, "slab": t} for c, t in others]
+    greet(peers)
+    copies = []
+    for i, (c, t) in enumerate(others):
+        src, dst = waves_ref.at[t, c], got_ref.at[z, slab]
+        copies.append(send(src, dst, send_sem.at[0, i], recv_sem.at[0, i], peers[i]))
+    got_ref[z, slab] = waves_ref[slab, z]
+    data_ref[...] = index_ref[...]
+    wait_all(copies)
+
+    def waves_at(at):
+        parts = [got_ref[c, t, :, at].astype(F32) for c in range(quarters) for t in range(slabs)]
+        return jnp.concatenate(parts, axis=0)
+
+    def bands_at(at):
+        parts = [bands_ref[a, c, :, at].astype(F32) for a in range(half) for c in range(zs)]
+        return jnp.concatenate(parts, axis=0).astype(BF16)
+
+    total = jnp.zeros(total_ref.shape, F32)
+    for i in range(part // chunk):
+        at = pl.ds(i * chunk, chunk)
+        total = total + dot_nt(waves_at(at).astype(BF16), bands_at(at))
+    total_ref[...] = total
+
     copies = []
     for i, peer in enumerate(peers):
-        to = {"slab": peer}
-        copies.append(send(waves_ref.at[peer], got_ref.at[me], send_sem.at[0, i], recv_sem.at[0, i], to))
-    got_ref[me] = waves_ref[me]
-    data_ref[...] = index_ref[...]
-    wait_all(copies)
-
-    def waves_at(at):
-        return jnp.concatenate([got_ref[t, :, at].astype(F32) for t in range(slabs)], axis=0)
-
-    total = jnp.zeros(total_ref.shape, F32)
-    for i in range(npw // chunk):
-        at = pl.ds(i * chunk, chunk)
-        total = total + dot_nt(waves_at(at).astype(BF16), bands_ref[:, at])
-    total_ref[...] = total
-
-    copies = []
-    for i, peer in enumerate(peers):
-        to = {"slab": peer}
-        copies.append(send(total_ref, corr_ref.at[i], send_sem.at[1, i], recv_sem.at[1, i], to))
+        copies.append(send(total_ref, corr_ref.at[i], send_sem.at[1, i], recv_sem.at[1, i], peer))
     wait_all(copies)
     correlation = total_ref[...]
-    for i in range(slabs - 1):
+    for i in range(len(peers)):
         correlation = correlation + corr_ref[i]
     correlation = correlation.astype(BF16)
 
-    for i in range(npw // chunk):
+    for i in range(part // chunk):
         at = pl.ds(i * chunk, chunk)
-        rhs = (waves_at(at) - dot(correlation, bands_ref[:, at])).astype(BF16)
-        for t in range(slabs):
-            rhs_ref[t, :, at] = rhs[two * t : two * (t + 1)]
+        rhs = (waves_at(at) - dot(correlation, bands_at(at))).astype(BF16).astype(F32)
+        for c in range(quarters):
+            for t in range(slabs):
+                first = two * (c * slabs + t)
+                rhs_ref[c, t, :, at] = rhs[first : first + two].astype(BF16)
 
     copies = []
-    for i, peer in enumerate(peers):
-        to = {"slab": peer}
-        copies.append(send(rhs_ref.at[peer], back_ref.at[me], send_sem.at[2, i], recv_sem.at[2, i], to))
-    back_ref[me] = rhs_ref[me]
+    for i, (c, t) in enumerate(others):
+        src, dst = rhs_ref.at[c, t], back_ref.at[slab, z]
+        copies.append(send(src, dst, send_sem.at[2, i], recv_sem.at[2, i], peers[i]))
+    back_ref[slab, z] = rhs_ref[z, slab]
     wait_all(copies)
 
     numer = jnp.zeros((two, chunk), F32)
     denom = jnp.zeros((two, chunk), F32)
     energy = jnp.concatenate([jnp.full((1, chunk), energy_ref[b], F32) for b in range(two)], axis=0)
     for s in range(slabs):
-        for i in range(npw // chunk):
-            at = pl.ds(i * chunk, chunk)
-            mine = back_ref[s, :, at].astype(F32)
-            data_ref[s, 0:2, at] = mine
-            squares = mine * mine
-            numer = numer + squares
-            denom = denom + (index_ref[s, 4:5, at] - energy) * squares
+        for q in range(quarters):
+            for i in range(part // chunk):
+                at = pl.ds(q * part + i * chunk, chunk)
+                mine = back_ref[s, q, :, i * chunk : (i + 1) * chunk].astype(F32)
+                data_ref[s, 0:2, at] = mine
+                squares = mine * mine
+                numer = numer + squares
+                denom = denom + (index_ref[s, 4:5, at] - energy) * squares
     step = -jnp.sum(numer, axis=1, keepdims=True) / jnp.sum(denom, axis=1, keepdims=True)
-    scale = 4.0 * N1 * N2 * N3 / bands_ref.shape[0]
+    scale = 4.0 * N1 * N2 * N3 / (half * zs * bands)
     step_ref[...] = jnp.broadcast_to(scale * step, step_ref.shape)
 
 
@@ -663,28 +693,34 @@
     )(starts, data, tab)
 
 
-def dense_of(turned, pot, tab, slabs):
+def dense_of(turned, pot, coefs, tab, slabs):
+    bands, npw = coefs.shape
     return pl.pallas_call(
         dense_kernel,
-        out_shape=(shape((N2, N1, 2 * LANES), BF16), shape((slabs, N1, 2 * N2 // slabs, N3), BF16)),
-        in_specs=[VMEM] * 3,
-        out_specs=(VMEM, VMEM),
+        out_shape=(
+            shape((N2, N1, 2 * LANES), BF16),
+            shape((slabs, N1, 2 * N2 // slabs, N3), BF16),
+            shape((2, 4, bands, npw // QUARTERS), BF16),
+        ),
+        in_specs=[VMEM] * 4,
+        out_specs=(VMEM, VMEM, VMEM),
         scratch_shapes=[
             pltpu.VMEM((slabs,) + pot.shape, BF16),
             pltpu.VMEM((N1, N2, 2 * LANES), BF16),
         ]
-        + sems(3),
+        + sems(3)
+        + sems(7),
         compiler_params=params(4),
         cost_estimate=cost(2e10, 8e6),
         name="dense",
-    )(turned, pot, tab)
+    )(turned, pot, coefs, tab)
 
 
 def gather_of(starts, data, wave, npw):
     slabs = data.shape[0]
     return pl.pallas_call(
         gather_kernel,
-        out_shape=shape((slabs, 2, npw), BF16),
+        out_shape=shape((slabs, QUARTERS, 2, npw // QUARTERS), BF16),
         in_specs=[SMEM] + [VMEM] * 2,
         out_specs=VMEM,
         scratch_shapes=[pltpu.VMEM((slabs, 2, data.shape[2]), F32)],
@@ -695,9 +731,10 @@
 
 
 def middle_of(waves, bands, index, energies):
-    slabs, two, npw = waves.shape
+    slabs, quarters, two, part = waves.shape
     block = pltpu.VMEM(waves.shape, BF16)
-    small = (slabs * two, bands.shape[0])
+    peers = slabs * quarters - 1
+    small = (slabs * quarters * two, bands.shape[0] * bands.shape[1] * bands.shape[2])
     return pl.pallas_call(
         middle_kernel,
         out_shape=(shape(index.shape, F32), shape((two, LANES), F32)),
@@ -705,12 +742,12 @@
         out_specs=(VMEM, VMEM),
         scratch_shapes=[
             block,
-            pltpu.VMEM((slabs - 1,) + small, F32),
+            pltpu.VMEM((peers,) + small, F32),
             block,
             block,
             pltpu.VMEM(small, F32),
         ]
-        + sems(3, slabs - 1),
+        + sems(3, peers),
         compiler_params=params(2),
         name="middle",
     )(waves, bands, index, energies)
@@ -757,13 +794,12 @@
     me = lax.axis_index("slab")
     bands, npw = wave_coeffs.shape
     planes, cross = trial_potentials.shape[1:]
-    all_bands = lax.all_gather(wave_coeffs, "band", axis=0, tiled=True)
     tab = cosines(N1)
     pot = trial_potentials.reshape(planes, cross)
     energies = lax.dynamic_slice_in_dim(band_energies, me * (bands // slabs), bands // slabs, 0)
     data, starts = start_of(wave_coeffs, wave_map, slabs)
     turned = zy_of(starts, data, tab)
-    psi, wave = dense_of(turned, pot, tab, slabs)
+    psi, wave, all_bands = dense_of(turned, pot, wave_coeffs, tab, slabs)
     waves = gather_of(starts, data, wave, npw)
     data, step = middle_of(waves, all_bands, data, energies)
     turned = zy_of(starts, data, tab)

time: 142 us -> 125 us (0.88)
  between operations: 14.2 us -> 0.79 us
  local copies, waits for them, and re-layouts: 7.33 us -> 5.21 us
    pallas_call x1, Pallas kernels: 23.7 us -> 27.1 us  [dense_of(): pl.pallas_call(dense_kernel, out_shape=(shape((N2, N1, 2 * LANES), BF16),...]
    pallas_call x1, Pallas kernels: 29.6 us -> 27.3 us  [end_of(): pl.pallas_call(end_kernel, out_shape=(shape((planes, width), F32), shape(...]
    pallas_call x1, Pallas kernels: 22.3 us -> 20.2 us  [middle_of(): pl.pallas_call(middle_kernel, out_shape=(shape(index.shape, F32), shape((...]
    unnamed x16, local copies, waits for them, and re-layouts: 6.6 us -> 5.13 us
  transfers between devices with their start and end apart: 1 -> 0, of which waited for: 0 -> 0; matrix products, arithmetic and copies ran while one was open for 1% -> 0% of each run, Pallas kernels for 39% -> 0%
where the time goes in v4:
time: 125 us
  Pallas kernels  119 us (95%)
  local copies, waits for them, and re-layouts  5.21 us (4%)
    pallas_call x1, Pallas kernels, end_of(): pl.pallas_call(end_kernel, out_shape=(shape((planes, width), F32), shape(...  27.3 us
    pallas_call x1, Pallas kernels, dense_of(): pl.pallas_call(dense_kernel, out_shape=(shape((N2, N1, 2 * LANES), BF16),...  27.1 us
    pallas_call x2, Pallas kernels, zy_of(): pl.pallas_call(zy_kernel, out_shape=shape((N2, N1, 2 * LANES), BF16), in_...  25.4 us
    pallas_call x1, Pallas kernels, middle_of(): pl.pallas_call(middle_kernel, out_shape=(shape(index.shape, F32), shape((...  20.2 us
    pallas_call x1, Pallas kernels, start_of(): pl.pallas_call(start_kernel, out_shape=(shape((slabs, 8, npw + 2 * WIN),...  9.54 us
    pallas_call x1, Pallas kernels, gather_of(): pl.pallas_call(gather_kernel, out_shape=shape((slabs, QUARTERS, 2, npw //...  8.95 us
    unnamed x16, local copies, waits for them, and re-layouts  5.13 us

profile of v4, /device:TPU:1, one launch (start us, length us, event | category | flops | bytes accessed | tf_op | source)
XLA Modules:
  0.0 124.8 jit_solution(12599166898929330292)
XLA Ops:
  0.7 0.2 multiply_convert_fusion.tab_ref
  0.9 0.0 copy-start.2
  0.9 0.9 copy-done.2
  1.8 0.0 copy-start.3
  1.8 0.8 copy-done.3
  2.7 9.5 %start.1 = (f32[4,8,14848]{2,1,0:T(8,128)S(1)}, s32[4,1,128]{2,1,0:T(1,128)S(1)}) custom-call(bf16[8,13824]{1,0:T(8,128)(2,1)S(1)} %copy-done.2, s32[108,128]{1,0:T(8,128)S(1)} %bitcast.8), custom_call_target="tpu_custom_call" | custom-call | tf_op jit(solution)/shard_map/start/pallas_call | solution.py:666
  12.2 0.0 copy-start.1
  12.2 12.7 %scatter_zy.2.turned_ref = bf16[96,96,256]{2,1,0:T(8,128)(2,1)S(1)} custom-call(s32[4,1,128]{2,1,0:T(1,128)S(1)} %get-tuple-element.11.starts_ref, f32[4,8,14848]{2,1,0:T(8,128)S(1)} %get-tuple-element.12.data_ref.index_ref, bf16[96,96]{1,0:T(8,128)(2,1)S(1)} %multiply_convert_fusion.tab_ref), custom_call_target="tpu_custom_call" | custom-call | flops 20000000000 | bytes 8000000 | tf_op jit(solution)/shard_map/scatter_zy/pallas_call | solution.py:684
  24.9 0.0 copy-done.1
  24.9 27.1 %dense.1 = (bf16[96,96,256]{2,1,0:T(8,128)(2,1)S(1)}, bf16[4,96,48,96]{3,2,1,0:T(8,128)(2,1)S(1)}, bf16[2,4,8,3456]{3,2,1,0:T(8,128)(2,1)S(1)}) custom-call(bf16[96,96,256]{2,1,0:T(8,128)(2,1)S(1)} %scatter_zy.2.turned_ref, f32[24,9216]{1,0:T(8,128)S(1)} %bitcast.5, bf16[8,13824]{1,0:T(8,128)(2,1)S(1)} %copy-done.2, ...), custom_call_target="tpu_custom_call" | custom-call | flops 20000000000 | bytes 8000000 | tf_op jit(solution)/shard_map/dense/pallas_call | solution.py:698
  52.1 0.0 copy-start
  52.1 2.1 %copy-done = bf16[96,96,256]{2,1,0:T(8,128)(2,1)} copy-done((bf16[96,96,256]{2,1,0:T(8,128)(2,1)}, bf16[96,96,256]{2,1,0:T(8,128)(2,1)S(1)}, u32[]{:S(2)}) %copy-start) | copy-done | bytes 4718616
  54.2 0.0 copy-start.4
  54.2 9.0 %gather.1.waves_ref = bf16[4,4,2,3456]{3,2,1,0:T(2,128)(2,1)S(1)} custom-call(s32[4,1,128]{2,1,0:T(1,128)S(1)} %get-tuple-element.11.starts_ref, f32[4,8,14848]{2,1,0:T(8,128)S(1)} %get-tuple-element.12.data_ref.index_ref, bf16[4,96,48,96]{3,2,1,0:T(8,128)(2,1)S(1)} %get-tuple-element.13.wave_ref), custom_call_target="tpu_custom_call" | custom-call | flops 20000000000 | bytes 8000000 | tf_op jit(solution)/shard_map/gather/pallas_call | solution.py:721
  63.2 0.0 copy-done.4
  63.2 0.1 dynamic_slice.3.energy_ref
  63.3 0.0 slice-start
  63.3 20.2 %middle.1 = (f32[4,8,14848]{2,1,0:T(8,128)S(1)}, f32[2,128]{1,0:T(2,128)S(1)}) custom-call(bf16[4,4,2,3456]{3,2,1,0:T(2,128)(2,1)S(1)} %gather.1.waves_ref, bf16[2,4,8,3456]{3,2,1,0:T(8,128)(2,1)S(1)} %get-tuple-element.14.bands_ref, f32[4,8,14848]{2,1,0:T(8,128)S(1)} %get-tuple-element.12.data_ref.index_ref, f32[2]{0:T(128)S(1)} %dynamic_slice.3.energy_ref), custom_call_target="tpu_custom_call" | custom-call | tf_op jit(solution)/shard_map/middle/pallas_call | solution.py:738
  83.5 0.0 slice-start.1
  83.5 12.7 %scatter_zy.3.turned_ref = bf16[96,96,256]{2,1,0:T(8,128)(2,1)S(1)} custom-call(s32[4,1,128]{2,1,0:T(1,128)S(1)} %get-tuple-element.11.starts_ref, f32[4,8,14848]{2,1,0:T(8,128)S(1)} %get-tuple-element.15.data_ref, bf16[96,96]{1,0:T(8,128)(2,1)S(1)} %multiply_convert_fusion.tab_ref), custom_call_target="tpu_custom_call" | custom-call | flops 20000000000 | bytes 8000000 | tf_op jit(solution)/shard_map/scatter_zy/pallas_call | solution.py:684
  96.2 0.0 slice-done
  96.2 0.0 slice-done.1
  96.2 27.3 %density.1 = (f32[24,1152]{1,0:T(8,128)S(1)}, f32[8,128]{1,0:T(8,128)S(1)}) custom-call(bf16[96,96,256]{2,1,0:T(8,128)(2,1)S(1)} %scatter_zy.3.turned_ref, bf16[96,96,256]{2,1,0:T(8,128)(2,1)S(1)} %bitcast.4, f32[2,128]{1,0:T(2,128)S(1)} %get-tuple-element.17.step_ref, f32[24,9216]{1,0:T(8,128)S(1)} %bitcast.6, bf16[96,96]{1,0:T(8,128)(2,1)S(1)} %multiply_convert_fusion.tab_ref), custom_call_target="tpu_custom_call" | custom-call | tf_op jit(solution)/shard_map/density/pallas_call | solution.py:760
  123.5 0.6 copy.6
  124.1 0.6 copy.8
  (4 shorter events, 0.0 us)
Async XLA Ops:
  0.9 0.9 copy-start.2
  1.8 0.8 copy-start.3
  12.2 12.7 %copy-start.1 = (f32[1,24,9216]{2,1,0:T(8,128)S(1)}, f32[1,24,9216]{2,1,0:T(8,128)}, u32[]{:S(2)}) copy-start(f32[1,24,9216]{2,1,0:T(8,128)} %param.6) | copy-start | bytes 2654212
  52.1 2.1 %copy-start = (bf16[96,96,256]{2,1,0:T(8,128)(2,1)}, bf16[96,96,256]{2,1,0:T(8,128)(2,1)S(1)}, u32[]{:S(2)}) copy-start(bf16[96,96,256]{2,1,0:T(8,128)(2,1)S(1)} %get-tuple-element.16.psi_ref) | copy-start | bytes 14155780
  54.2 9.0 %copy-start.4 = (f32[8]{0:T(128)S(1)}, f32[8]{0:T(128)}, u32[]{:S(2)}) copy-start(f32[8]{0:T(128)} %param.5) | copy-start | bytes 100
  63.3 32.9 %slice-start = ((s8[4718592]{0:T(1024)(128)(4,1)}), s8[4194304]{0:T(1024)(128)(4,1)S(1)}, s32[]{:S(2)}) async-start(s8[4718592]{0:T(1024)(128)(4,1)} %bitcast.3), calls=%async_computation | async-start | bytes 8388608
  83.5 12.7 %slice-start.1 = ((s8[4718592]{0:T(1024)(128)(4,1)}), s8[524288]{0:T(1024)(128)(4,1)S(1)}, s32[]{:S(2)}) async-start(s8[4718592]{0:T(1024)(128)(4,1)} %bitcast.3), calls=%async_computation.1 | async-start | bytes 1048576

commit v5 on v4

--- a/solution.py
+++ b/solution.py
@@ -185,6 +185,7 @@
 
 SMEM = pl.BlockSpec(memory_space=pltpu.SMEM)
 VMEM = pl.BlockSpec(memory_space=pltpu.VMEM)
+HBM = pl.BlockSpec(memory_space=pltpu.HBM)
 LIMIT = 32 * 1024 * 1024
 
 
@@ -288,8 +289,8 @@
 
 
 def dense_kernel(
-    turned_ref, pot_ref, coef_ref, tab_ref, psi_ref, wave_ref, bands_ref,
-    pots_ref, back_ref, send_sem, recv_sem, coef_send, coef_recv,
+    turned_ref, pot_ref, coef_ref, tab_ref, psi_out, wave_ref, bands_ref,
+    psi_ref, pots_ref, back_ref, send_sem, recv_sem, coef_send, coef_recv, psi_sem,
 ):
     slabs = wave_ref.shape[0]
     ny = N2 // slabs
@@ -298,9 +299,9 @@
     y = y_hi * 2 + y_lo
     sibling = device(y_hi, y_lo, z, 1 - core)
 
-    def around(step, other):
+    def around(step):
         to = lax.rem(y + step + 4, 4)
-        return device(to // 2, lax.rem(to, 2), z, other)
+        return device(to // 2, lax.rem(to, 2), z, core)
 
     for i in range(3):
         at = pl.ds(i * 3072, 3072)
@@ -308,38 +309,41 @@
     steps = [(a, b) for a in range(2) for b in range(4) if a + b > 0]
     others = [(lax.rem(y_hi + a, 2), lax.rem(z + b, 4)) for a, b in steps]
     members = [device(a, y_lo, b, core) for a, b in others]
-    greet([sibling] + [around(step, other) for step in (-1, 1) for other in (0, 1)] + members)
+    greet([sibling, around(-1), around(1)] + members)
     mine = pots_ref.at[me]
-    copies = [send(mine, mine, send_sem.at[2], recv_sem.at[2], sibling)]
-    for other in (0, 1):
-        to = around(2 * core - 1, other)
-        copies.append(send(mine, mine, send_sem.at[other], recv_sem.at[core], to))
+    to_far = send(mine, mine, send_sem.at[0], recv_sem.at[0], around(2 * core - 1))
+    to_near = send(mine, mine, send_sem.at[1], recv_sem.at[1], sibling)
 
     inv_x = transposed(tab_ref[...])
     unroll = 8
 
-    @pl.loop(0, N2 // unroll)
-    def _(group):
-        for u in range(unroll):
-            row = group * unroll + u
-            psi_ref[row] = dot(inv_x, turned_ref[row]).astype(BF16)
-
-    copies[0].wait()
-    for copy in copies[1:]:
-        copy.wait_send()
-    for other in (0, 1):
-        slot = pots_ref.at[(1 - y_lo) * 2 + other]
-        remote(slot, slot, send_sem.at[other], recv_sem.at[other], sibling).wait_recv()
-
+    def psi_rows(first, last):
+        @pl.loop(first, last)
+        def _(group):
+            for u in range(unroll):
+                row = group * unroll + u
+                psi_ref[row] = dot(inv_x, turned_ref[row]).astype(BF16)
+
+    groups = N2 // unroll
+    psi_rows(0, groups - 3)
+    to_far.wait_send()
+    slot = pots_ref.at[(1 - y_lo) * 2 + core]
+    remote(slot, slot, send_sem.at[0], recv_sem.at[0], sibling).wait_recv()
+    passed = send(slot, slot, send_sem.at[2], recv_sem.at[2], sibling)
     part = bands_ref.shape[3]
-    at = pl.ds(pl.multiple_of(z * part, LANES), part)
-    bands_ref[y_hi, z] = coef_ref[:, at]
+    quarter = pl.ds(pl.multiple_of(lax.axis_index("pert") * part, LANES), part)
+    bands_ref[y_hi, z] = coef_ref[:, quarter]
     copies = []
-    for i, (_, b) in enumerate(others):
-        at = pl.ds(pl.multiple_of(b * part, LANES), part)
-        copies.append(
-            send(coef_ref.at[:, at], bands_ref.at[y_hi, z], coef_send.at[i], coef_recv.at[i], members[i])
-        )
+    for i, member in enumerate(members):
+        src = coef_ref.at[:, quarter]
+        copies.append(send(src, bands_ref.at[y_hi, z], coef_send.at[i], coef_recv.at[i], member))
+    psi_rows(groups - 3, groups)
+    store = pltpu.make_async_copy(psi_ref, psi_out, psi_sem)
+    store.start()
+    to_near.wait()
+    passed.wait_send()
+    slot = pots_ref.at[(1 - y_lo) * 2 + 1 - core]
+    remote(slot, slot, send_sem.at[2], recv_sem.at[2], sibling).wait_recv()
 
     width = 16
     lane = iota((N1 // slabs, LANES), 1)
@@ -382,6 +386,7 @@
                 two = waves[(2 * u + 1) * N2 + s * ny : (2 * u + 1) * N2 + (s + 1) * ny]
                 wave_ref[s, group * unroll + u] = jnp.concatenate([one, two], axis=0).astype(BF16)
 
+    store.wait()
     wait_all(copies)
 
 
@@ -392,17 +397,16 @@
     slabs, quarters, two, part = waves_ref.shape
     half, zs, bands, _ = bands_ref.shape
     chunk = 1152
-    y_hi, y_lo, z, core = place()
-    slab = lax.axis_index("slab")
+    pert, slab = lax.axis_index("pert"), lax.axis_index("slab")
     steps = [(a, b) for a in range(quarters) for b in range(slabs) if a + b > 0]
-    others = [(lax.rem(z + a, quarters), lax.rem(slab + b, slabs)) for a, b in steps]
-    peers = [{"band": y_hi * 4 + c, "slab": t} for c, t in others]
+    others = [(lax.rem(pert + a, quarters), lax.rem(slab + b, slabs)) for a, b in steps]
+    peers = [{"pert": c, "slab": t} for c, t in others]
     greet(peers)
     copies = []
     for i, (c, t) in enumerate(others):
-        src, dst = waves_ref.at[t, c], got_ref.at[z, slab]
+        src, dst = waves_ref.at[t, c], got_ref.at[pert, slab]
         copies.append(send(src, dst, send_sem.at[0, i], recv_sem.at[0, i], peers[i]))
-    got_ref[z, slab] = waves_ref[slab, z]
+    got_ref[pert, slab] = waves_ref[slab, pert]
     data_ref[...] = index_ref[...]
     wait_all(copies)
 
@@ -414,41 +418,62 @@
         parts = [bands_ref[a, c, :, at].astype(F32) for a in range(half) for c in range(zs)]
         return jnp.concatenate(parts, axis=0).astype(BF16)
 
-    total = jnp.zeros(total_ref.shape, F32)
+    rows, count = quarters * slabs * two, half * zs * bands
+    total = jnp.zeros((rows, count), F32)
     for i in range(part // chunk):
         at = pl.ds(i * chunk, chunk)
         total = total + dot_nt(waves_at(at).astype(BF16), bands_at(at))
-    total_ref[...] = total
+    total_ref[...] = jnp.concatenate([total[: rows // 2], total[rows // 2 :]], axis=1)
 
     copies = []
     for i, peer in enumerate(peers):
         copies.append(send(total_ref, corr_ref.at[i], send_sem.at[1, i], recv_sem.at[1, i], peer))
     wait_all(copies)
-    correlation = total_ref[...]
+    total = total_ref[...]
     for i in range(len(peers)):
-        correlation = correlation + corr_ref[i]
-    correlation = correlation.astype(BF16)
-
+        total = total + corr_ref[i]
+    correlation = jnp.concatenate([total[:, :count], total[:, count:]], axis=0).astype(BF16)
+
+    overlap = jnp.zeros((rows, rows), F32)
     for i in range(part // chunk):
         at = pl.ds(i * chunk, chunk)
-        rhs = (waves_at(at) - dot(correlation, bands_at(at))).astype(BF16).astype(F32)
+        waves = waves_at(at)
+        rhs = (waves - dot(correlation, bands_at(at))).astype(BF16)
+        overlap = overlap + dot_nt(rhs, waves.astype(BF16))
+        rhs = rhs.astype(F32)
         for c in range(quarters):
             for t in range(slabs):
                 first = two * (c * slabs + t)
                 rhs_ref[c, t, :, at] = rhs[first : first + two].astype(BF16)
+    own = rows // quarters
+    same = lax.rem(iota((rows, rows), 0), own) == lax.rem(iota((rows, rows), 1), own)
+    kept = jnp.where(same, overlap, 0.0)
+    lane = iota((rows, LANES), 1)
+    tail = jnp.zeros((rows, LANES), F32)
+    for p in range(quarters):
+        mine = jnp.sum(kept[:, p * own : (p + 1) * own], axis=1, keepdims=True)
+        high = mine.astype(BF16).astype(F32)
+        tail = jnp.where(lane == p, high, tail)
+        tail = jnp.where(lane == quarters + p, mine - high, tail)
+    for c in range(quarters):
+        for t in range(slabs):
+            first = two * (c * slabs + t)
+            rhs_ref[c, t, :, part:] = tail[first : first + two].astype(BF16)
 
     copies = []
     for i, (c, t) in enumerate(others):
-        src, dst = rhs_ref.at[c, t], back_ref.at[slab, z]
+        src, dst = rhs_ref.at[c, t], back_ref.at[slab, pert]
         copies.append(send(src, dst, send_sem.at[2, i], recv_sem.at[2, i], peers[i]))
-    back_ref[slab, z] = rhs_ref[z, slab]
+    back_ref[slab, pert] = rhs_ref[pert, slab]
     wait_all(copies)
 
     numer = jnp.zeros((two, chunk), F32)
     denom = jnp.zeros((two, chunk), F32)
+    tail = jnp.zeros((two, LANES), F32)
     energy = jnp.concatenate([jnp.full((1, chunk), energy_ref[b], F32) for b in range(two)], axis=0)
     for s in range(slabs):
         for q in range(quarters):
+            tail = tail + back_ref[s, q, :, part:].astype(F32)
             for i in range(part // chunk):
                 at = pl.ds(q * part + i * chunk, chunk)
                 mine = back_ref[s, q, :, i * chunk : (i + 1) * chunk].astype(F32)
@@ -457,8 +482,11 @@
                 numer = numer + squares
                 denom = denom + (index_ref[s, 4:5, at] - energy) * squares
     step = -jnp.sum(numer, axis=1, keepdims=True) / jnp.sum(denom, axis=1, keepdims=True)
-    scale = 4.0 * N1 * N2 * N3 / (half * zs * bands)
-    step_ref[...] = jnp.broadcast_to(scale * step, step_ref.shape)
+    step = step * (4.0 * N1 * N2 * N3 / count)
+    tail = step * (tail + pltpu.roll(tail, LANES - quarters, 1))
+    tail = jnp.sum(tail, axis=0, keepdims=True)
+    wide = jnp.broadcast_to(step, (two, LANES))
+    step_ref[...] = jnp.concatenate([wide, tail, jnp.zeros((8 - two - 1, LANES), F32)], axis=0)
 
 
 PART_A = 5
@@ -495,8 +523,8 @@
     lane = iota((N1, LANES), 1)
     half = 4 * PARTS
 
-    def density_half(h):
-        @pl.loop(0, 6)
+    def density_part(h, first, last):
+        @pl.loop(first, last)
         def _(group):
             for v in range(2):
                 quad = h * 12 + group * 2 + v
@@ -517,17 +545,18 @@
                         dens_ref[s, quad * 3 + j] = tile[s * planes : (s + 1) * planes].astype(BF16)
 
     halves = [1 - y_hi, y_hi]
-    core_copies = []
-    for k, h in enumerate(halves):
-        density_half(h)
+    core_copies, a_copies, b_copies = [], [], []
+
+    def to_sibling(k):
+        h = halves[k]
         for l in range(2):
             src = dens_ref.at[l * 2 + 1 - core, pl.ds(h * half, half)]
             core_copies.append(
                 send(src, from_core.at[k, l], core_send.at[k, l], core_recv.at[k, l], sibling)
             )
 
-    a_copies, b_copies = [], []
-    for k, h in enumerate(halves):
+    def to_others(k):
+        h = halves[k]
         wait_all(core_copies[2 * k : 2 * k + 2])
         for l in range(2):
             @pl.loop(0, 4)
@@ -547,18 +576,46 @@
                 send(b_ref.at[k, c], b_from_z.at[k, i], b_send.at[k, i], b_recv.at[k, i], z_peers[i])
             )
 
+    density_part(halves[0], 0, 6)
+    to_sibling(0)
+    density_part(halves[1], 0, 3)
+    to_others(0)
+    density_part(halves[1], 3, 6)
+    to_sibling(1)
+
     def total_of(pair):
         total = sum(pair(j) for j in range(PARTS))
         total = total[0:8] + total[8:16] + total[16:24]
         return jnp.sum(total, axis=0, keepdims=True)
 
-    wait_all(pot_copies)
-
     def pot(p, j):
         return pots_ref[p, :, j * LANES : (j + 1) * LANES]
 
+    wait_all(pot_copies)
     pairs = [(p, q) for p in range(perts) for q in range(p + 1)]
     sums = [total_of(lambda j: pot(p, j) * pot(q, j)) for p, q in pairs]
+    line = iota((1, LANES), 1)
+    sums += [jnp.where(line == p, step_ref[2:3], 0.0) for p in range(perts)]
+    sums += [jnp.zeros((1, LANES), F32)] * (16 - len(sums))
+    sums_ref[0] = jnp.concatenate(sums, axis=0)
+    to_others(1)
+
+    def sum_sends(level, first, group):
+        copies = []
+        for i, peer in enumerate(group):
+            k = first + i
+            copies.append(send(sums_ref.at[level], from_sums.at[k], sum_send.at[k], sum_recv.at[k], peer))
+        return copies
+
+    def sum_up(level, first, copies):
+        wait_all(copies)
+        total = sums_ref[level]
+        for i in range(len(copies)):
+            total = total + from_sums[first + i]
+        sums_ref[level + 1] = total
+
+    near = [sibling] + y_peers + y_others
+    near_copies = sum_sends(0, 0, near)
 
     wait_all(a_copies)
 
@@ -583,6 +640,8 @@
                 b_sum[k, l, j] = total.astype(BF16)
     for i, (k, l) in enumerate([(0, y_lo), (0, 1 - y_lo), (1, 1 - y_lo)]):
         copies.append(send(b_sum.at[k, l], b_from_y.at[i], b2_send.at[i], b2_recv.at[i], y_peers[i]))
+    sum_up(0, 0, near_copies)
+    far_copies = sum_sends(1, len(near), z_peers)
     wait_all(copies)
     density = []
     for j in range(PARTS):
@@ -595,22 +654,7 @@
             for i in range(3):
                 total = total + b_from_y[i, j - PART_A].astype(F32)
         density.append(total)
-    sums += [total_of(lambda j: pot(p, j) * density[j]) for p in range(perts)]
-    sums += [jnp.zeros((1, LANES), F32)] * (16 - len(sums))
-    sums_ref[0] = jnp.concatenate(sums, axis=0)
-
-    at = 0
-    for level, group in enumerate([[sibling] + y_peers + y_others, z_peers]):
-        copies = []
-        for i, peer in enumerate(group):
-            k = at + i
-            copies.append(send(sums_ref.at[level], from_sums.at[k], sum_send.at[k], sum_recv.at[k], peer))
-        wait_all(copies)
-        total = sums_ref[level]
-        for i in range(len(group)):
-            total = total + from_sums[at + i]
-        sums_ref[level + 1] = total
-        at += len(group)
+    sum_up(1, len(near), far_copies)
 
     cells = 1.0 / (N1 * N2 * N3)
     totals = jnp.broadcast_to(jnp.sum(sums_ref[2], axis=1, keepdims=True) * cells, (16, LANES))
@@ -703,13 +747,15 @@
             shape((2, 4, bands, npw // QUARTERS), BF16),
         ),
         in_specs=[VMEM] * 4,
-        out_specs=(VMEM, VMEM, VMEM),
+        out_specs=(HBM, VMEM, VMEM),
         scratch_shapes=[
+            pltpu.VMEM((N2, N1, 2 * LANES), BF16),
             pltpu.VMEM((slabs,) + pot.shape, BF16),
             pltpu.VMEM((N1, N2, 2 * LANES), BF16),
         ]
         + sems(3)
-        + sems(7),
+        + sems(7)
+        + [pltpu.SemaphoreType.DMA(())],
         compiler_params=params(4),
         cost_estimate=cost(2e10, 8e6),
         name="dense",
@@ -732,19 +778,19 @@
 
 def middle_of(waves, bands, index, energies):
     slabs, quarters, two, part = waves.shape
-    block = pltpu.VMEM(waves.shape, BF16)
     peers = slabs * quarters - 1
-    small = (slabs * quarters * two, bands.shape[0] * bands.shape[1] * bands.shape[2])
+    small = (slabs * quarters * two // 2, LANES)
+    longer = pltpu.VMEM((slabs, quarters, two, part + LANES), BF16)
     return pl.pallas_call(
         middle_kernel,
-        out_shape=(shape(index.shape, F32), shape((two, LANES), F32)),
+        out_shape=(shape(index.shape, F32), shape((8, LANES), F32)),
         in_specs=[VMEM] * 3 + [SMEM],
         out_specs=(VMEM, VMEM),
         scratch_shapes=[
-            block,
+            pltpu.VMEM(waves.shape, BF16),
             pltpu.VMEM((peers,) + small, F32),
-            block,
-            block,
+            longer,
+            longer,
             pltpu.VMEM(small, F32),
         ]
         + sems(3, peers),

time: 125 us -> 116 us (0.928)
  Pallas kernels: 119 us -> 109 us
    pallas_call x1, Pallas kernels: 27.3 us -> 19.9 us  [end_of(): pl.pallas_call(end_kernel, out_shape=(shape((planes, width), F32), shape(...]
    pallas_call x1, Pallas kernels: 27.1 us -> 24.4 us  [dense_of(): pl.pallas_call(dense_kernel, out_shape=(shape((N2, N1, 2 * LANES), BF16),...]
where the time goes in v5:
time: 116 us
  Pallas kernels  109 us (94%)
  local copies, waits for them, and re-layouts  5.21 us (4%)
    pallas_call x2, Pallas kernels, zy_of(): pl.pallas_call(zy_kernel, out_shape=shape((N2, N1, 2 * LANES), BF16), in_...  25.4 us
    pallas_call x1, Pallas kernels, dense_of(): pl.pallas_call(dense_kernel, out_shape=(shape((N2, N1, 2 * LANES), BF16),...  24.4 us
    pallas_call x1, Pallas kernels, middle_of(): pl.pallas_call(middle_kernel, out_shape=(shape(index.shape, F32), shape((...  21.2 us
    pallas_call x1, Pallas kernels, end_of(): pl.pallas_call(end_kernel, out_shape=(shape((planes, width), F32), shape(...  19.9 us
    pallas_call x1, Pallas kernels, start_of(): pl.pallas_call(start_kernel, out_shape=(shape((slabs, 8, npw + 2 * WIN),...  9.54 us
    pallas_call x1, Pallas kernels, gather_of(): pl.pallas_call(gather_kernel, out_shape=shape((slabs, QUARTERS, 2, npw //...  8.95 us
    unnamed x16, local copies, waits for them, and re-layouts  5.13 us

profile of v5, /device:TPU:1, one launch (start us, length us, event | category | flops | bytes accessed | tf_op | source)
XLA Modules:
  0.0 115.7 jit_solution(7443267093576700828)
XLA Ops:
  0.7 0.2 multiply_convert_fusion.tab_ref
  0.9 0.0 copy-start.2
  0.9 0.9 copy-done.2
  1.8 0.0 copy-start.3
  1.8 0.8 copy-done.3
  2.7 9.5 %start.1 = (f32[4,8,14848]{2,1,0:T(8,128)S(1)}, s32[4,1,128]{2,1,0:T(1,128)S(1)}) custom-call(bf16[8,13824]{1,0:T(8,128)(2,1)S(1)} %copy-done.2, s32[108,128]{1,0:T(8,128)S(1)} %bitcast.8), custom_call_target="tpu_custom_call" | custom-call | tf_op jit(solution)/shard_map/start/pallas_call | solution.py:710
  12.2 0.0 copy-start.1
  12.2 12.7 %scatter_zy.2.turned_ref = bf16[96,96,256]{2,1,0:T(8,128)(2,1)S(1)} custom-call(s32[4,1,128]{2,1,0:T(1,128)S(1)} %get-tuple-element.11.starts_ref, f32[4,8,14848]{2,1,0:T(8,128)S(1)} %get-tuple-element.12.data_ref.index_ref, bf16[96,96]{1,0:T(8,128)(2,1)S(1)} %multiply_convert_fusion.tab_ref), custom_call_target="tpu_custom_call" | custom-call | flops 20000000000 | bytes 8000000 | tf_op jit(solution)/shard_map/scatter_zy/pallas_call | solution.py:728
  24.9 0.0 copy-done.1
  24.9 24.4 %dense.1 = (bf16[96,96,256]{2,1,0:T(8,128)(2,1)S(1)}, bf16[4,96,48,96]{3,2,1,0:T(8,128)(2,1)S(1)}, bf16[2,4,8,3456]{3,2,1,0:T(8,128)(2,1)S(1)}) custom-call(bf16[96,96,256]{2,1,0:T(8,128)(2,1)S(1)} %scatter_zy.2.turned_ref, f32[24,9216]{1,0:T(8,128)S(1)} %bitcast.5, bf16[8,13824]{1,0:T(8,128)(2,1)S(1)} %copy-done.2, ...), custom_call_target="tpu_custom_call" | custom-call | flops 20000000000 | bytes 8000000 | tf_op jit(solution)/shard_map/dense/pallas_call | solution.py:742
  49.3 0.0 copy-start
  49.3 2.1 %copy-done = bf16[96,96,256]{2,1,0:T(8,128)(2,1)} copy-done((bf16[96,96,256]{2,1,0:T(8,128)(2,1)}, bf16[96,96,256]{2,1,0:T(8,128)(2,1)S(1)}, u32[]{:S(2)}) %copy-start) | copy-done | bytes 4718616
  51.5 0.0 copy-start.4
  51.5 9.0 %gather.1.waves_ref = bf16[4,4,2,3456]{3,2,1,0:T(2,128)(2,1)S(1)} custom-call(s32[4,1,128]{2,1,0:T(1,128)S(1)} %get-tuple-element.11.starts_ref, f32[4,8,14848]{2,1,0:T(8,128)S(1)} %get-tuple-element.12.data_ref.index_ref, bf16[4,96,48,96]{3,2,1,0:T(8,128)(2,1)S(1)} %get-tuple-element.13.wave_ref), custom_call_target="tpu_custom_call" | custom-call | flops 20000000000 | bytes 8000000 | tf_op jit(solution)/shard_map/gather/pallas_call | solution.py:767
  60.4 0.0 copy-done.4
  60.4 0.1 dynamic_slice.3.energy_ref
  60.5 0.0 slice-start
  60.5 21.2 %middle.1 = (f32[4,8,14848]{2,1,0:T(8,128)S(1)}, f32[8,128]{1,0:T(8,128)S(1)}) custom-call(bf16[4,4,2,3456]{3,2,1,0:T(2,128)(2,1)S(1)} %gather.1.waves_ref, bf16[2,4,8,3456]{3,2,1,0:T(8,128)(2,1)S(1)} %get-tuple-element.14.bands_ref, f32[4,8,14848]{2,1,0:T(8,128)S(1)} %get-tuple-element.12.data_ref.index_ref, f32[2]{0:T(128)S(1)} %dynamic_slice.3.energy_ref), custom_call_target="tpu_custom_call" | custom-call | tf_op jit(solution)/shard_map/middle/pallas_call | solution.py:784
  81.8 0.0 slice-start.1
  81.8 12.7 %scatter_zy.3.turned_ref = bf16[96,96,256]{2,1,0:T(8,128)(2,1)S(1)} custom-call(s32[4,1,128]{2,1,0:T(1,128)S(1)} %get-tuple-element.11.starts_ref, f32[4,8,14848]{2,1,0:T(8,128)S(1)} %get-tuple-element.15.data_ref, bf16[96,96]{1,0:T(8,128)(2,1)S(1)} %multiply_convert_fusion.tab_ref), custom_call_target="tpu_custom_call" | custom-call | flops 20000000000 | bytes 8000000 | tf_op jit(solution)/shard_map/scatter_zy/pallas_call | solution.py:728
  94.5 0.0 slice-done
  94.5 0.0 slice-done.1
  94.5 19.9 %density.1 = (f32[24,1152]{1,0:T(8,128)S(1)}, f32[8,128]{1,0:T(8,128)S(1)}) custom-call(bf16[96,96,256]{2,1,0:T(8,128)(2,1)S(1)} %scatter_zy.3.turned_ref, bf16[96,96,256]{2,1,0:T(8,128)(2,1)S(1)} %bitcast.4, f32[8,128]{1,0:T(8,128)S(1)} %get-tuple-element.17.step_ref, f32[24,9216]{1,0:T(8,128)S(1)} %bitcast.6, bf16[96,96]{1,0:T(8,128)(2,1)S(1)} %multiply_convert_fusion.tab_ref), custom_call_target="tpu_custom_call" | custom-call | tf_op jit(solution)/shard_map/density/pallas_call | solution.py:806
  114.5 0.6 copy.6
  115.1 0.6 copy.8
  (4 shorter events, 0.0 us)
Async XLA Ops:
  0.9 0.9 copy-start.2
  1.8 0.8 copy-start.3
  12.2 12.7 %copy-start.1 = (f32[1,24,9216]{2,1,0:T(8,128)S(1)}, f32[1,24,9216]{2,1,0:T(8,128)}, u32[]{:S(2)}) copy-start(f32[1,24,9216]{2,1,0:T(8,128)} %param.6) | copy-start | bytes 2654212
  49.3 2.1 %copy-start = (bf16[96,96,256]{2,1,0:T(8,128)(2,1)}, bf16[96,96,256]{2,1,0:T(8,128)(2,1)S(1)}, u32[]{:S(2)}) copy-start(bf16[96,96,256]{2,1,0:T(8,128)(2,1)S(1)} %get-tuple-element.16.psi_ref) | copy-start | bytes 14155780
  51.5 9.0 %copy-start.4 = (f32[8]{0:T(128)S(1)}, f32[8]{0:T(128)}, u32[]{:S(2)}) copy-start(f32[8]{0:T(128)} %param.5) | copy-start | bytes 100
  60.5 34.0 %slice-start = ((s8[4718592]{0:T(1024)(128)(4,1)}), s8[4194304]{0:T(1024)(128)(4,1)S(1)}, s32[]{:S(2)}) async-start(s8[4718592]{0:T(1024)(128)(4,1)} %bitcast.3), calls=%async_computation | async-start | bytes 8388608
  81.8 12.7 %slice-start.1 = ((s8[4718592]{0:T(1024)(128)(4,1)}), s8[524288]{0:T(1024)(128)(4,1)S(1)}, s32[]{:S(2)}) async-start(s8[4718592]{0:T(1024)(128)(4,1)} %bitcast.3), calls=%async_computation.1 | async-start | bytes 1048576

commit v6 on v5

--- a/solution.py
+++ b/solution.py
@@ -81,102 +81,125 @@
     return jnp.concatenate(rows, axis=0)
 
 
-def scatter_planes(starts_ref, data_ref, plane_ref):
+def tile_planes(starts_ref, data_ref, tile):
+    slabs = data_ref.shape[0]
+    ny = N2 // slabs
+    parts = [
+        scatter_window(data_ref, s, window_base(starts_ref, s, tile), tile, TILE * ny)
+        for s in range(slabs)
+    ]
+    return [plane_of(parts, t, ny) for t in range(TILE)]
+
+
+def more_planes(starts_ref, data_ref, tile):
     slabs = data_ref.shape[0]
     ny = N2 // slabs
     cells = TILE * ny
-    unroll = 4
-
-    @pl.loop(0, TILES // unroll)
+    parts = []
+    for s in range(slabs):
+        base = window_base(starts_ref, s, tile)
+
+        def more(i, acc):
+            at = pl.multiple_of(base + i * WIN, LANES)
+            return acc + scatter_window(data_ref, s, at, tile, cells)
+
+        windows = (starts_ref[s, 0, tile + 1] - base + WIN - 1) // WIN
+        parts.append(lax.fori_loop(1, windows, more, jnp.zeros((2 * cells, N3), F32)))
+    return [plane_of(parts, t, ny) for t in range(TILE)]
+
+
+def zy_kernel(starts_ref, data_ref, tab_ref, turned_ref, plane_ref):
+    inv_y = transposed(tab_ref[...])
+    inv_z = dot(tab_ref[...], ones_at(N3, LANES)).astype(BF16)
+    width = 32
+    over = overflow(starts_ref, data_ref.shape[0])
+
+    def transform(planes, first):
+        done = []
+        for plane in planes:
+            z_done = dot(plane, inv_z).astype(BF16)
+            done.append(dot(inv_y, jnp.concatenate([z_done[:N2], z_done[N2:]], axis=1)).astype(BF16))
+        turned_ref[:, pl.ds(first, width), :] = jnp.swapaxes(jnp.stack(done, axis=0), 0, 1)
+
+    @pl.when(jnp.logical_not(over))
+    def _():
+        @pl.loop(0, N1 // width)
+        def _(group):
+            first = pl.multiple_of(group * width, width)
+            planes = []
+            for u in range(width // TILE):
+                tile = group * (width // TILE) + u
+                planes += [plane.astype(BF16) for plane in tile_planes(starts_ref, data_ref, tile)]
+            transform(planes, first)
+
+    @pl.when(over)
+    def _():
+        @pl.loop(0, TILES)
+        def _(tile):
+            planes = tile_planes(starts_ref, data_ref, tile)
+            added = more_planes(starts_ref, data_ref, tile)
+            for t in range(TILE):
+                plane_ref[tile * TILE + t] = (planes[t] + added[t]).astype(BF16)
+
+        @pl.loop(0, N1 // width)
+        def _(group):
+            first = pl.multiple_of(group * width, width)
+            transform([plane_ref[first + u] for u in range(width)], first)
+
+
+def gather_window(data_ref, planes, s, base, tile):
+    ny = N2 // data_ref.shape[0]
+    cells = TILE * ny
+    rows = data_ref[s, :, pl.ds(base, WIN)]
+    hot = hot_rows(rows, tile, cells)
+    mine = [plane[b * N2 + s * ny : b * N2 + (s + 1) * ny] for b in range(2) for plane in planes]
+    picked = dot(jnp.concatenate(mine, axis=0).astype(BF16), hot_z(rows))
+    found = [
+        jnp.sum(jnp.where(hot, picked[b * cells : (b + 1) * cells], 0.0), axis=0, keepdims=True)
+        for b in range(2)
+    ]
+    return jnp.concatenate(found, axis=0)
+
+
+def gather_kernel(starts_ref, data_ref, back_ref, tab_ref, out_ref, sum_ref):
+    slabs = data_ref.shape[0]
+    sum_ref[...] = jnp.zeros_like(sum_ref)
+    fwd_z = dot_nt(ones_at(LANES, N3), tab_ref[...]).astype(BF16)
+    several = 16
+
+    def wave_planes(tile, count):
+        done = []
+        for t in range(count):
+            y_done = dot(tab_ref[...], back_ref[tile * TILE + t]).astype(BF16)
+            done += [y_done[:, :LANES], y_done[:, LANES:]]
+        waves = dot(jnp.concatenate(done, axis=0), fwd_z)
+        return [waves[2 * N2 * t : 2 * N2 * (t + 1)] for t in range(count)]
+
+    @pl.loop(0, TILES // several)
     def _(group):
-        for u in range(unroll):
-            tile = group * unroll + u
-            parts = [
-                scatter_window(data_ref, s, window_base(starts_ref, s, tile), tile, cells)
-                for s in range(slabs)
-            ]
-            for t in range(TILE):
-                plane_ref[tile * TILE + t] = plane_of(parts, t, ny).astype(BF16)
+        all_planes = wave_planes(group * several, several * TILE)
+        found = []
+        for u in range(several):
+            tile = group * several + u
+            planes = all_planes[TILE * u : TILE * (u + 1)]
+            for s in range(slabs):
+                base = window_base(starts_ref, s, tile)
+                found.append((s, base, gather_window(data_ref, planes, s, base, tile)))
+        for s, base, value in found:
+            sum_ref[s, :, pl.ds(base, WIN)] += value
 
     @pl.when(overflow(starts_ref, slabs))
     def _():
         @pl.loop(0, TILES)
         def _(tile):
-            parts = []
-            for s in range(slabs):
-                base = window_base(starts_ref, s, tile)
-
-                def more(i, acc):
-                    at = pl.multiple_of(base + i * WIN, LANES)
-                    return acc + scatter_window(data_ref, s, at, tile, cells)
-
-                windows = (starts_ref[s, 0, tile + 1] - base + WIN - 1) // WIN
-                zero = jnp.zeros((2 * cells, N3), F32)
-                parts.append(lax.fori_loop(1, windows, more, zero))
-            for t in range(TILE):
-                old = plane_ref[tile * TILE + t].astype(F32)
-                plane_ref[tile * TILE + t] = (old + plane_of(parts, t, ny)).astype(BF16)
-
-
-def zy_kernel(starts_ref, data_ref, tab_ref, turned_ref, plane_ref):
-    scatter_planes(starts_ref, data_ref, plane_ref)
-    inv_y = transposed(tab_ref[...])
-    inv_z = dot(tab_ref[...], ones_at(N3, LANES)).astype(BF16)
-    width = 16
-
-    @pl.loop(0, N1 // width)
-    def _(group):
-        first = pl.multiple_of(group * width, width)
-        flat = plane_ref[pl.ds(first, width)].reshape(width * 2 * N2, N3)
-        z_done = dot(flat, inv_z).astype(BF16)
-        done = []
-        for u in range(width):
-            one = z_done[2 * N2 * u : 2 * N2 * u + N2]
-            two = z_done[2 * N2 * u + N2 : 2 * N2 * (u + 1)]
-            done.append(dot(inv_y, jnp.concatenate([one, two], axis=1)).astype(BF16))
-        turned_ref[:, pl.ds(first, width), :] = jnp.swapaxes(jnp.stack(done, axis=0), 0, 1)
-
-
-def gather_window(data_ref, wave_ref, sum_ref, s, base, tile, ny):
-    cells = TILE * ny
-    at = pl.ds(base, WIN)
-    rows = data_ref[s, :, at]
-    hot = hot_rows(rows, tile, cells)
-    mine = wave_ref[s, pl.ds(tile * TILE, TILE)].reshape(TILE * 2 * ny, N3)
-    picked = dot(mine, hot_z(rows))
-    found = []
-    for b in range(2):
-        part = jnp.concatenate(
-            [picked[(2 * t + b) * ny : (2 * t + b + 1) * ny] for t in range(TILE)], axis=0
-        )
-        found.append(jnp.sum(jnp.where(hot, part, 0.0), axis=0, keepdims=True))
-    sum_ref[s, :, at] += jnp.concatenate(found, axis=0)
-
-
-def gather_kernel(starts_ref, data_ref, wave_ref, out_ref, sum_ref):
-    slabs = data_ref.shape[0]
-    ny = N2 // slabs
-    sum_ref[...] = jnp.zeros_like(sum_ref)
-    several = 4
-
-    @pl.loop(0, TILES // several)
-    def _(group):
-        for u in range(several):
-            tile = group * several + u
-            for s in range(slabs):
-                gather_window(data_ref, wave_ref, sum_ref, s, window_base(starts_ref, s, tile), tile, ny)
-
-    @pl.when(overflow(starts_ref, slabs))
-    def _():
-        @pl.loop(0, TILES)
-        def _(tile):
+            planes = wave_planes(tile, TILE)
             for s in range(slabs):
                 base = window_base(starts_ref, s, tile)
 
                 @pl.loop(1, (starts_ref[s, 0, tile + 1] - base + WIN - 1) // WIN)
                 def _(i):
                     at = pl.multiple_of(base + i * WIN, LANES)
-                    gather_window(data_ref, wave_ref, sum_ref, s, at, tile, ny)
+                    sum_ref[s, :, pl.ds(at, WIN)] += gather_window(data_ref, planes, s, at, tile)
 
     part = out_ref.shape[3]
     for q in range(out_ref.shape[1]):
@@ -289,11 +312,10 @@
 
 
 def dense_kernel(
-    turned_ref, pot_ref, coef_ref, tab_ref, psi_out, wave_ref, bands_ref,
-    psi_ref, pots_ref, back_ref, send_sem, recv_sem, coef_send, coef_recv, psi_sem,
+    turned_ref, pot_ref, coef_ref, tab_ref, psi_out, back_ref, bands_ref,
+    psi_ref, pots_ref, send_sem, recv_sem, coef_send, coef_recv, psi_sem,
 ):
-    slabs = wave_ref.shape[0]
-    ny = N2 // slabs
+    slabs = pots_ref.shape[0]
     y_hi, y_lo, z, core = place()
     me = lax.axis_index("slab")
     y = y_hi * 2 + y_lo
@@ -320,9 +342,10 @@
     def psi_rows(first, last):
         @pl.loop(first, last)
         def _(group):
-            for u in range(unroll):
-                row = group * unroll + u
-                psi_ref[row] = dot(inv_x, turned_ref[row]).astype(BF16)
+            rows = [group * unroll + u for u in range(unroll)]
+            done = [dot(inv_x, turned_ref[row]).astype(BF16) for row in rows]
+            for row, value in zip(rows, done):
+                psi_ref[row] = value
 
     groups = N2 // unroll
     psi_rows(0, groups - 3)
@@ -370,21 +393,6 @@
                 product = jnp.concatenate([pot * psi[:, :LANES], pot * psi[:, LANES:]], axis=1)
                 done.append(dot(tab_ref[...], product.astype(BF16)).astype(BF16))
         back_ref[:, pl.ds(first, width), :] = jnp.swapaxes(jnp.stack(done, axis=0), 0, 1)
-
-    fwd_z = dot_nt(ones_at(LANES, N3), tab_ref[...]).astype(BF16)
-
-    @pl.loop(0, N1 // unroll)
-    def _(group):
-        done = []
-        for u in range(unroll):
-            y_done = dot(tab_ref[...], back_ref[group * unroll + u]).astype(BF16)
-            done += [y_done[:, :LANES], y_done[:, LANES:]]
-        waves = dot(jnp.concatenate(done, axis=0), fwd_z)
-        for u in range(unroll):
-            for s in range(slabs):
-                one = waves[2 * u * N2 + s * ny : 2 * u * N2 + (s + 1) * ny]
-                two = waves[(2 * u + 1) * N2 + s * ny : (2 * u + 1) * N2 + (s + 1) * ny]
-                wave_ref[s, group * unroll + u] = jnp.concatenate([one, two], axis=0).astype(BF16)
 
     store.wait()
     wait_all(copies)
@@ -526,6 +534,7 @@
     def density_part(h, first, last):
         @pl.loop(first, last)
         def _(group):
+            done = []
             for v in range(2):
                 quad = h * 12 + group * 2 + v
                 parts = []
@@ -540,9 +549,10 @@
                     jnp.where(lane < 64, one, two),
                     jnp.where(lane < 32, two, three),
                 ]
-                for j, tile in enumerate(tiles):
-                    for s in range(slabs):
-                        dens_ref[s, quad * 3 + j] = tile[s * planes : (s + 1) * planes].astype(BF16)
+                done += [(quad * 3 + j, tile) for j, tile in enumerate(tiles)]
+            for at, tile in done:
+                for s in range(slabs):
+                    dens_ref[s, at] = tile[s * planes : (s + 1) * planes].astype(BF16)
 
     halves = [1 - y_hi, y_hi]
     core_copies, a_copies, b_copies = [], [], []
@@ -561,13 +571,16 @@
         for l in range(2):
             @pl.loop(0, 4)
             def _(c):
+                done = []
                 for j in range(PARTS):
                     at = c * PARTS + j
                     total = dens_ref[l * 2 + core, h * half + at].astype(F32) + from_core[k, l, at].astype(F32)
+                    done.append(total.astype(BF16))
+                for j in range(PARTS):
                     if j < PART_A:
-                        a_ref[k, l, c, j] = total.astype(BF16)
+                        a_ref[k, l, c, j] = done[j]
                     else:
-                        b_ref[k, c, l, j - PART_A] = total.astype(BF16)
+                        b_ref[k, c, l, j - PART_A] = done[j]
         targets = [(0, y_lo), (1, 1 - y_lo)] if k == 0 else [(2, 1 - y_lo)]
         for i, l in targets:
             a_copies.append(send(a_ref.at[k, l], a_from_y.at[i], a_send.at[i], a_recv.at[i], y_peers[i]))
@@ -621,23 +634,28 @@
 
     @pl.loop(0, 4)
     def _(c):
+        done = []
         for j in range(PART_A):
             total = a_ref[1, y_lo, c, j].astype(F32)
             for i in range(3):
                 total = total + a_from_y[i, c, j].astype(F32)
-            a_sum[c, j] = total.astype(BF16)
+            done.append(total.astype(BF16))
+        for j in range(PART_A):
+            a_sum[c, j] = done[j]
 
     copies = []
     for i, c in enumerate(z_coords):
         copies.append(send(a_sum.at[c], a_from_z.at[i], a2_send.at[i], a2_recv.at[i], z_peers[i]))
     wait_all(b_copies)
-    for k in range(2):
-        for l in range(2):
-            for j in range(PART_B):
-                total = b_ref[k, z, l, j].astype(F32)
-                for i in range(3):
-                    total = total + b_from_z[k, i, l, j].astype(F32)
-                b_sum[k, l, j] = total.astype(BF16)
+    spots = [(k, l, j) for k in range(2) for l in range(2) for j in range(PART_B)]
+    done = []
+    for k, l, j in spots:
+        total = b_ref[k, z, l, j].astype(F32)
+        for i in range(3):
+            total = total + b_from_z[k, i, l, j].astype(F32)
+        done.append(total.astype(BF16))
+    for (k, l, j), value in zip(spots, done):
+        b_sum[k, l, j] = value
     for i, (k, l) in enumerate([(0, y_lo), (0, 1 - y_lo), (1, 1 - y_lo)]):
         copies.append(send(b_sum.at[k, l], b_from_y.at[i], b2_send.at[i], b2_recv.at[i], y_peers[i]))
     sum_up(0, 0, near_copies)
@@ -743,7 +761,7 @@
         dense_kernel,
         out_shape=(
             shape((N2, N1, 2 * LANES), BF16),
-            shape((slabs, N1, 2 * N2 // slabs, N3), BF16),
+            shape((N1, N2, 2 * LANES), BF16),
             shape((2, 4, bands, npw // QUARTERS), BF16),
         ),
         in_specs=[VMEM] * 4,
@@ -751,7 +769,6 @@
         scratch_shapes=[
             pltpu.VMEM((N2, N1, 2 * LANES), BF16),
             pltpu.VMEM((slabs,) + pot.shape, BF16),
-            pltpu.VMEM((N1, N2, 2 * LANES), BF16),
         ]
         + sems(3)
         + sems(7)
@@ -762,18 +779,18 @@
     )(turned, pot, coefs, tab)
 
 
-def gather_of(starts, data, wave, npw):
+def gather_of(starts, data, back, tab, npw):
     slabs = data.shape[0]
     return pl.pallas_call(
         gather_kernel,
         out_shape=shape((slabs, QUARTERS, 2, npw // QUARTERS), BF16),
-        in_specs=[SMEM] + [VMEM] * 2,
+        in_specs=[SMEM] + [VMEM] * 3,
         out_specs=VMEM,
         scratch_shapes=[pltpu.VMEM((slabs, 2, data.shape[2]), F32)],
         compiler_params=params(),
         cost_estimate=cost(2e10, 8e6),
         name="gather",
-    )(starts, data, wave)
+    )(starts, data, back, tab)
 
 
 def middle_of(waves, bands, index, energies):
@@ -845,8 +862,8 @@
     energies = lax.dynamic_slice_in_dim(band_energies, me * (bands // slabs), bands // slabs, 0)
     data, starts = start_of(wave_coeffs, wave_map, slabs)
     turned = zy_of(starts, data, tab)
-    psi, wave, all_bands = dense_of(turned, pot, wave_coeffs, tab, slabs)
-    waves = gather_of(starts, data, wave, npw)
+    psi, back, all_bands = dense_of(turned, pot, wave_coeffs, tab, slabs)
+    waves = gather_of(starts, data, back, tab, npw)
     data, step = middle_of(waves, all_bands, data, energies)
     turned = zy_of(starts, data, tab)
     residual, projected = end_of(turned, psi, step, pot, tab, slabs, lax.axis_size("pert"))

time: 116 us -> 110 us (0.948)
  Pallas kernels: 109 us -> 103 us
    pallas_call x2, Pallas kernels: 25.4 us -> 20.1 us  [zy_of(): pl.pallas_call(zy_kernel, out_shape=shape((N2, N1, 2 * LANES), BF16), in_...]
    pallas_call x1, Pallas kernels: 24.4 us -> 20.6 us  [dense_of(): pl.pallas_call(dense_kernel, out_shape=(shape((N2, N1, 2 * LANES), BF16),...]
    pallas_call x1, Pallas kernels: 8.95 us -> 10.7 us  [gather_of(): pl.pallas_call(gather_kernel, out_shape=shape((slabs, QUARTERS, 2, npw //...]
where the time goes in v6:
time: 110 us
  Pallas kernels  103 us (94%)
  local copies, waits for them, and re-layouts  5.21 us (5%)
    pallas_call x1, Pallas kernels, middle_of(): pl.pallas_call(middle_kernel, out_shape=(shape(index.shape, F32), shape((...  22.3 us
    pallas_call x1, Pallas kernels, dense_of(): pl.pallas_call(dense_kernel, out_shape=(shape((N2, N1, 2 * LANES), BF16),...  20.6 us
    pallas_call x1, Pallas kernels, end_of(): pl.pallas_call(end_kernel, out_shape=(shape((planes, width), F32), shape(...  20.3 us
    pallas_call x2, Pallas kernels, zy_of(): pl.pallas_call(zy_kernel, out_shape=shape((N2, N1, 2 * LANES), BF16), in_...  20.1 us
    pallas_call x1, Pallas kernels, gather_of(): pl.pallas_call(gather_kernel, out_shape=shape((slabs, QUARTERS, 2, npw //...  10.7 us
    pallas_call x1, Pallas kernels, start_of(): pl.pallas_call(start_kernel, out_shape=(shape((slabs, 8, npw + 2 * WIN),...  9.54 us
    unnamed x16, local copies, waits for them, and re-layouts  5.13 us

profile of v6, /device:TPU:1, one launch (start us, length us, event | category | flops | bytes accessed | tf_op | source)
XLA Modules:
  0.0 109.7 jit_solution(16805662817847841825)
XLA Ops:
  0.7 0.2 multiply_convert_fusion.tab_ref
  0.9 0.0 copy-start.2
  0.9 0.9 copy-done.2
  1.8 0.0 copy-start.3
  1.8 0.8 copy-done.3
  2.7 9.5 %start.1 = (f32[4,8,14848]{2,1,0:T(8,128)S(1)}, s32[4,1,128]{2,1,0:T(1,128)S(1)}) custom-call(bf16[8,13824]{1,0:T(8,128)(2,1)S(1)} %copy-done.2, s32[108,128]{1,0:T(8,128)S(1)} %bitcast.8), custom_call_target="tpu_custom_call" | custom-call | tf_op jit(solution)/shard_map/start/pallas_call | solution.py:728
  12.2 0.0 copy-start.1
  12.2 10.1 %scatter_zy.2.turned_ref = bf16[96,96,256]{2,1,0:T(8,128)(2,1)S(1)} custom-call(s32[4,1,128]{2,1,0:T(1,128)S(1)} %get-tuple-element.11.starts_ref, f32[4,8,14848]{2,1,0:T(8,128)S(1)} %get-tuple-element.12.data_ref.index_ref, bf16[96,96]{1,0:T(8,128)(2,1)S(1)} %multiply_convert_fusion.tab_ref), custom_call_target="tpu_custom_call" | custom-call | flops 20000000000 | bytes 8000000 | tf_op jit(solution)/shard_map/scatter_zy/pallas_call | solution.py:746
  22.3 0.0 copy-done.1
  22.3 20.6 %dense.1 = (bf16[96,96,256]{2,1,0:T(8,128)(2,1)S(1)}, bf16[96,96,256]{2,1,0:T(8,128)(2,1)S(1)}, bf16[2,4,8,3456]{3,2,1,0:T(8,128)(2,1)S(1)}) custom-call(bf16[96,96,256]{2,1,0:T(8,128)(2,1)S(1)} %scatter_zy.2.turned_ref, f32[24,9216]{1,0:T(8,128)S(1)} %bitcast.5, bf16[8,13824]{1,0:T(8,128)(2,1)S(1)} %copy-done.2, bf16[96,96]{1,0:T(8,128)(2,1)S(1)} %multiply_convert_fusion.tab_ref), custom_call_target="tpu_custom_call" | custom-call | flops 20000000000 | bytes 8000000 | tf_op jit(solution)/shard_map/dense/pallas_call | solution.py:760
  42.9 0.0 copy-start
  42.9 2.1 %copy-done = bf16[96,96,256]{2,1,0:T(8,128)(2,1)} copy-done((bf16[96,96,256]{2,1,0:T(8,128)(2,1)}, bf16[96,96,256]{2,1,0:T(8,128)(2,1)S(1)}, u32[]{:S(2)}) %copy-start) | copy-done | bytes 4718616
  45.0 0.0 copy-start.4
  45.0 10.7 %gather.1.waves_ref = bf16[4,4,2,3456]{3,2,1,0:T(2,128)(2,1)S(1)} custom-call(s32[4,1,128]{2,1,0:T(1,128)S(1)} %get-tuple-element.11.starts_ref, f32[4,8,14848]{2,1,0:T(8,128)S(1)} %get-tuple-element.12.data_ref.index_ref, bf16[96,96,256]{2,1,0:T(8,128)(2,1)S(1)} %get-tuple-element.13.back_ref, bf16[96,96]{1,0:T(8,128)(2,1)S(1)} %multiply_convert_fusion.tab_ref), custom_call_target="tpu_custom_call" | custom-call | flops 20000000000 | bytes 8000000 | tf_op jit(solution)/shard_map/gather/pallas_call | solution.py:784
  55.7 0.0 copy-done.4
  55.7 0.1 dynamic_slice.3.energy_ref
  55.8 0.0 slice-start
  55.8 22.3 %middle.1 = (f32[4,8,14848]{2,1,0:T(8,128)S(1)}, f32[8,128]{1,0:T(8,128)S(1)}) custom-call(bf16[4,4,2,3456]{3,2,1,0:T(2,128)(2,1)S(1)} %gather.1.waves_ref, bf16[2,4,8,3456]{3,2,1,0:T(8,128)(2,1)S(1)} %get-tuple-element.14.bands_ref, f32[4,8,14848]{2,1,0:T(8,128)S(1)} %get-tuple-element.12.data_ref.index_ref, f32[2]{0:T(128)S(1)} %dynamic_slice.3.energy_ref), custom_call_target="tpu_custom_call" | custom-call | tf_op jit(solution)/shard_map/middle/pallas_call | solution.py:801
  78.1 0.0 slice-start.1
  78.1 10.1 %scatter_zy.3.turned_ref = bf16[96,96,256]{2,1,0:T(8,128)(2,1)S(1)} custom-call(s32[4,1,128]{2,1,0:T(1,128)S(1)} %get-tuple-element.11.starts_ref, f32[4,8,14848]{2,1,0:T(8,128)S(1)} %get-tuple-element.15.data_ref, bf16[96,96]{1,0:T(8,128)(2,1)S(1)} %multiply_convert_fusion.tab_ref), custom_call_target="tpu_custom_call" | custom-call | flops 20000000000 | bytes 8000000 | tf_op jit(solution)/shard_map/scatter_zy/pallas_call | solution.py:746
  88.1 0.0 slice-done
  88.1 0.0 slice-done.1
  88.2 20.3 %density.1 = (f32[24,1152]{1,0:T(8,128)S(1)}, f32[8,128]{1,0:T(8,128)S(1)}) custom-call(bf16[96,96,256]{2,1,0:T(8,128)(2,1)S(1)} %scatter_zy.3.turned_ref, bf16[96,96,256]{2,1,0:T(8,128)(2,1)S(1)} %bitcast.4, f32[8,128]{1,0:T(8,128)S(1)} %get-tuple-element.17.step_ref, f32[24,9216]{1,0:T(8,128)S(1)} %bitcast.6, bf16[96,96]{1,0:T(8,128)(2,1)S(1)} %multiply_convert_fusion.tab_ref), custom_call_target="tpu_custom_call" | custom-call | tf_op jit(solution)/shard_map/density/pallas_call | solution.py:823
  108.4 0.6 copy.6
  109.0 0.6 copy.8
  (4 shorter events, 0.0 us)
Async XLA Ops:
  0.9 0.9 copy-start.2
  1.8 0.8 copy-start.3
  12.2 10.1 %copy-start.1 = (f32[1,24,9216]{2,1,0:T(8,128)S(1)}, f32[1,24,9216]{2,1,0:T(8,128)}, u32[]{:S(2)}) copy-start(f32[1,24,9216]{2,1,0:T(8,128)} %param.6) | copy-start | bytes 2654212
  42.9 2.1 %copy-start = (bf16[96,96,256]{2,1,0:T(8,128)(2,1)}, bf16[96,96,256]{2,1,0:T(8,128)(2,1)S(1)}, u32[]{:S(2)}) copy-start(bf16[96,96,256]{2,1,0:T(8,128)(2,1)S(1)} %get-tuple-element.16.psi_ref) | copy-start | bytes 14155780
  45.0 10.7 %copy-start.4 = (f32[8]{0:T(128)S(1)}, f32[8]{0:T(128)}, u32[]{:S(2)}) copy-start(f32[8]{0:T(128)} %param.5) | copy-start | bytes 100
  55.8 32.3 %slice-start = ((s8[4718592]{0:T(1024)(128)(4,1)}), s8[4194304]{0:T(1024)(128)(4,1)S(1)}, s32[]{:S(2)}) async-start(s8[4718592]{0:T(1024)(128)(4,1)} %bitcast.3), calls=%async_computation | async-start | bytes 8388608
  78.1 10.1 %slice-start.1 = ((s8[4718592]{0:T(1024)(128)(4,1)}), s8[524288]{0:T(1024)(128)(4,1)S(1)}, s32[]{:S(2)}) async-start(s8[4718592]{0:T(1024)(128)(4,1)} %bitcast.3), calls=%async_computation.1 | async-start | bytes 1048576

commit v7 on v6

--- a/solution.py
+++ b/solution.py
@@ -208,15 +208,16 @@
 
 SMEM = pl.BlockSpec(memory_space=pltpu.SMEM)
 VMEM = pl.BlockSpec(memory_space=pltpu.VMEM)
-HBM = pl.BlockSpec(memory_space=pltpu.HBM)
 LIMIT = 32 * 1024 * 1024
 
 
 def greet(peers):
-    barrier = pltpu.get_barrier_semaphore()
     for peer in peers:
-        pl.semaphore_signal(barrier, inc=1, device_id=peer, device_id_type=MESH)
-    pl.semaphore_wait(barrier, len(peers))
+        pl.semaphore_signal(pltpu.get_barrier_semaphore(), inc=1, device_id=peer, device_id_type=MESH)
+
+
+def greeted(peers):
+    pl.semaphore_wait(pltpu.get_barrier_semaphore(), len(peers))
 
 
 def remote(src, dst, send_sem, recv_sem, peer):
@@ -251,13 +252,15 @@
 
 
 def start_kernel(
-    coef_ref, map_ref, data_ref, starts_ref, own_coef, own_map, coefs_ref, maps_ref, send_sem, recv_sem
+    coef_ref, map_ref, pot_ref, data_ref, starts_ref, narrow_ref,
+    own_coef, own_map, coefs_ref, maps_ref, send_sem, recv_sem,
 ):
     slabs, two, npw = coefs_ref.shape
     ny = N2 // slabs
     me = lax.axis_index("slab")
     peers = slab_peers(slabs)
     chunk = 1536
+    greet([{"slab": peer} for peer in peers])
     for r in range(npw // LANES):
         own_map[0:1, r * LANES : (r + 1) * LANES] = map_ref[r : r + 1, :]
     for i in range(npw // chunk):
@@ -265,7 +268,7 @@
         block = coef_ref[:, at].astype(F32)
         for t in range(slabs):
             own_coef[t, :, at] = block[two * t : two * (t + 1)].astype(BF16)
-    greet([{"slab": peer} for peer in peers])
+    greeted(peers)
     coef_copies = []
     for i, peer in enumerate(peers):
         to = {"slab": peer}
@@ -289,6 +292,7 @@
         copies.append(send(own_map, maps_ref.at[me], send_sem.at[1, i], recv_sem.at[1, i], to))
     maps_ref[me] = own_map[...]
     data_ref[...] = jnp.full(data_ref.shape, -1.0, F32)
+    narrow_ref[...] = pot_ref[...].astype(BF16)
     wait_all(copies)
     for s in range(slabs):
         starts_ref[s] = maps_ref[s, :, npw : npw + LANES]
@@ -312,61 +316,44 @@
 
 
 def dense_kernel(
-    turned_ref, pot_ref, coef_ref, tab_ref, psi_out, back_ref, bands_ref,
-    psi_ref, pots_ref, send_sem, recv_sem, coef_send, coef_recv, psi_sem,
+    turned_ref, pot_ref, far_ref, coef_ref, tab_ref, psi_ref, back_ref, bands_ref,
+    pots_ref, send_sem, recv_sem, coef_send, coef_recv,
 ):
     slabs = pots_ref.shape[0]
     y_hi, y_lo, z, core = place()
     me = lax.axis_index("slab")
-    y = y_hi * 2 + y_lo
+    distant = (1 - y_lo) * 2 + core
     sibling = device(y_hi, y_lo, z, 1 - core)
-
-    def around(step):
-        to = lax.rem(y + step + 4, 4)
-        return device(to // 2, lax.rem(to, 2), z, core)
-
-    for i in range(3):
-        at = pl.ds(i * 3072, 3072)
-        pots_ref[me, :, at] = pot_ref[:, at].astype(BF16)
     steps = [(a, b) for a in range(2) for b in range(4) if a + b > 0]
     others = [(lax.rem(y_hi + a, 2), lax.rem(z + b, 4)) for a, b in steps]
     members = [device(a, y_lo, b, core) for a, b in others]
-    greet([sibling, around(-1), around(1)] + members)
-    mine = pots_ref.at[me]
-    to_far = send(mine, mine, send_sem.at[0], recv_sem.at[0], around(2 * core - 1))
-    to_near = send(mine, mine, send_sem.at[1], recv_sem.at[1], sibling)
-
-    inv_x = transposed(tab_ref[...])
-    unroll = 8
-
-    def psi_rows(first, last):
-        @pl.loop(first, last)
-        def _(group):
-            rows = [group * unroll + u for u in range(unroll)]
-            done = [dot(inv_x, turned_ref[row]).astype(BF16) for row in rows]
-            for row, value in zip(rows, done):
-                psi_ref[row] = value
-
-    groups = N2 // unroll
-    psi_rows(0, groups - 3)
-    to_far.wait_send()
-    slot = pots_ref.at[(1 - y_lo) * 2 + core]
-    remote(slot, slot, send_sem.at[0], recv_sem.at[0], sibling).wait_recv()
-    passed = send(slot, slot, send_sem.at[2], recv_sem.at[2], sibling)
+    greet([sibling] + members)
     part = bands_ref.shape[3]
     quarter = pl.ds(pl.multiple_of(lax.axis_index("pert") * part, LANES), part)
     bands_ref[y_hi, z] = coef_ref[:, quarter]
+    pots_ref[me] = pot_ref[...]
+    pots_ref[distant] = far_ref[...]
+    greeted([sibling] + members)
     copies = []
     for i, member in enumerate(members):
         src = coef_ref.at[:, quarter]
         copies.append(send(src, bands_ref.at[y_hi, z], coef_send.at[i], coef_recv.at[i], member))
-    psi_rows(groups - 3, groups)
-    store = pltpu.make_async_copy(psi_ref, psi_out, psi_sem)
-    store.start()
-    to_near.wait()
-    passed.wait_send()
-    slot = pots_ref.at[(1 - y_lo) * 2 + 1 - core]
-    remote(slot, slot, send_sem.at[2], recv_sem.at[2], sibling).wait_recv()
+    near = [
+        send(pot_ref, pots_ref.at[me], send_sem.at[0], recv_sem.at[0], sibling),
+        send(far_ref, pots_ref.at[distant], send_sem.at[1], recv_sem.at[1], sibling),
+    ]
+
+    inv_x = transposed(tab_ref[...])
+    unroll = 16
+
+    @pl.loop(0, N2 // unroll)
+    def _(group):
+        rows = [group * unroll + u for u in range(unroll)]
+        done = [dot(inv_x, turned_ref[row]).astype(BF16) for row in rows]
+        for row, value in zip(rows, done):
+            psi_ref[row] = value
+
+    wait_all(near)
 
     width = 16
     lane = iota((N1 // slabs, LANES), 1)
@@ -394,7 +381,6 @@
                 done.append(dot(tab_ref[...], product.astype(BF16)).astype(BF16))
         back_ref[:, pl.ds(first, width), :] = jnp.swapaxes(jnp.stack(done, axis=0), 0, 1)
 
-    store.wait()
     wait_all(copies)
 
 
@@ -410,6 +396,7 @@
     others = [(lax.rem(pert + a, quarters), lax.rem(slab + b, slabs)) for a, b in steps]
     peers = [{"pert": c, "slab": t} for c, t in others]
     greet(peers)
+    greeted(peers)
     copies = []
     for i, (c, t) in enumerate(others):
         src, dst = waves_ref.at[t, c], got_ref.at[pert, slab]
@@ -478,7 +465,8 @@
     numer = jnp.zeros((two, chunk), F32)
     denom = jnp.zeros((two, chunk), F32)
     tail = jnp.zeros((two, LANES), F32)
-    energy = jnp.concatenate([jnp.full((1, chunk), energy_ref[b], F32) for b in range(two)], axis=0)
+    energy = [jnp.full((1, chunk), energy_ref[slab * two + b], F32) for b in range(two)]
+    energy = jnp.concatenate(energy, axis=0)
     for s in range(slabs):
         for q in range(quarters):
             tail = tail + back_ref[s, q, :, part:].astype(F32)
@@ -519,13 +507,9 @@
     z_coords = [lax.rem(z + d, 4) for d in range(1, 4)]
     z_peers = [device(y_hi, y_lo, c, core) for c in z_coords]
     p_peers = [{"pert": lax.rem(pert + d, perts)} for d in range(1, perts)]
-    greet([sibling] + y_peers + y_others + z_peers + p_peers)
-
+    everyone = [sibling] + y_peers + y_others + z_peers + p_peers
+    greet(everyone)
     pots_ref[pert] = pot_ref[:, pl.ds(pl.multiple_of(band * width, LANES), width)]
-    pot_copies = []
-    for i, peer in enumerate(p_peers):
-        mine = pots_ref.at[pert]
-        pot_copies.append(send(mine, mine, pot_send.at[i], pot_recv.at[i], peer))
 
     inv_x = transposed(tab_ref[...])
     lane = iota((N1, LANES), 1)
@@ -535,8 +519,8 @@
         @pl.loop(first, last)
         def _(group):
             done = []
-            for v in range(2):
-                quad = h * 12 + group * 2 + v
+            for v in range(4):
+                quad = h * 12 + group * 4 + v
                 parts = []
                 for u in range(4):
                     row = quad * 4 + u
@@ -589,11 +573,16 @@
                 send(b_ref.at[k, c], b_from_z.at[k, i], b_send.at[k, i], b_recv.at[k, i], z_peers[i])
             )
 
-    density_part(halves[0], 0, 6)
+    density_part(halves[0], 0, 3)
+    greeted(everyone)
     to_sibling(0)
-    density_part(halves[1], 0, 3)
+    pot_copies = []
+    for i, peer in enumerate(p_peers):
+        mine = pots_ref.at[pert]
+        pot_copies.append(send(mine, mine, pot_send.at[i], pot_recv.at[i], peer))
+    density_part(halves[1], 0, 1)
     to_others(0)
-    density_part(halves[1], 3, 6)
+    density_part(halves[1], 1, 3)
     to_sibling(1)
 
     def total_of(pair):
@@ -722,14 +711,18 @@
     return [pltpu.SemaphoreType.DMA(dims)] * 2
 
 
-def start_of(coefs, wave_map, slabs):
+def start_of(coefs, wave_map, pot, slabs):
     bands, npw = coefs.shape
     block = (slabs, bands // slabs, npw)
     return pl.pallas_call(
         start_kernel,
-        out_shape=(shape((slabs, 8, npw + 2 * WIN), F32), shape((slabs, 1, LANES), jnp.int32)),
-        in_specs=[VMEM] * 2,
-        out_specs=(VMEM, VMEM),
+        out_shape=(
+            shape((slabs, 8, npw + 2 * WIN), F32),
+            shape((slabs, 1, LANES), jnp.int32),
+            shape(pot.shape, BF16),
+        ),
+        in_specs=[VMEM] * 3,
+        out_specs=(VMEM, VMEM, VMEM),
         scratch_shapes=[
             pltpu.VMEM(block, BF16),
             pltpu.VMEM((1, npw + LANES), jnp.int32),
@@ -739,7 +732,7 @@
         + sems(2, slabs - 1),
         compiler_params=params(1),
         name="start",
-    )(coefs, wave_map.reshape(npw // LANES, LANES))
+    )(coefs, wave_map.reshape(npw // LANES, LANES), pot)
 
 
 def zy_of(starts, data, tab):
@@ -755,7 +748,7 @@
     )(starts, data, tab)
 
 
-def dense_of(turned, pot, coefs, tab, slabs):
+def dense_of(turned, pot, far, coefs, tab, slabs):
     bands, npw = coefs.shape
     return pl.pallas_call(
         dense_kernel,
@@ -764,19 +757,17 @@
             shape((N1, N2, 2 * LANES), BF16),
             shape((2, 4, bands, npw // QUARTERS), BF16),
         ),
-        in_specs=[VMEM] * 4,
-        out_specs=(HBM, VMEM, VMEM),
+        in_specs=[VMEM] * 5,
+        out_specs=(VMEM, VMEM, VMEM),
         scratch_shapes=[
-            pltpu.VMEM((N2, N1, 2 * LANES), BF16),
             pltpu.VMEM((slabs,) + pot.shape, BF16),
         ]
-        + sems(3)
-        + sems(7)
-        + [pltpu.SemaphoreType.DMA(())],
+        + sems(2)
+        + sems(7),
         compiler_params=params(4),
         cost_estimate=cost(2e10, 8e6),
         name="dense",
-    )(turned, pot, coefs, tab)
+    )(turned, pot, far, coefs, tab)
 
 
 def gather_of(starts, data, back, tab, npw):
@@ -852,19 +843,28 @@
     )(turned, psi, step, pot, tab)
 
 
+def next_chip():
+    pairs = []
+    for band in range(8):
+        for slab in range(4):
+            core = slab % 2
+            to = (band // 4 * 2 + slab // 2 + 2 * core - 1) % 4
+            pairs.append((band * 4 + slab, (to // 2 * 4 + band % 4) * 4 + to % 2 * 2 + core))
+    return pairs
+
+
 def per_device(wave_coeffs, band_energies, trial_potentials, wave_map):
     slabs = lax.axis_size("slab")
-    me = lax.axis_index("slab")
-    bands, npw = wave_coeffs.shape
+    npw = wave_coeffs.shape[1]
     planes, cross = trial_potentials.shape[1:]
     tab = cosines(N1)
     pot = trial_potentials.reshape(planes, cross)
-    energies = lax.dynamic_slice_in_dim(band_energies, me * (bands // slabs), bands // slabs, 0)
-    data, starts = start_of(wave_coeffs, wave_map, slabs)
+    data, starts, narrow = start_of(wave_coeffs, wave_map, pot, slabs)
+    far = lax.ppermute(narrow, ("band", "slab"), next_chip())
     turned = zy_of(starts, data, tab)
-    psi, back, all_bands = dense_of(turned, pot, wave_coeffs, tab, slabs)
+    psi, back, all_bands = dense_of(turned, narrow, far, wave_coeffs, tab, slabs)
     waves = gather_of(starts, data, back, tab, npw)
-    data, step = middle_of(waves, all_bands, data, energies)
+    data, step = middle_of(waves, all_bands, data, band_energies)
     turned = zy_of(starts, data, tab)
     residual, projected = end_of(turned, psi, step, pot, tab, slabs, lax.axis_size("pert"))
     return (residual.reshape(1, planes, -1), projected[: lax.axis_size("pert"), :1])

time: 110 us -> 102 us (0.927)
  Pallas kernels: 103 us -> 95.5 us
  starting transfers between devices: 0 us -> 1.45 us
    pallas_call x1, Pallas kernels: 20.6 us -> 13.4 us  [dense_of(): pl.pallas_call(dense_kernel, out_shape=(shape((N2, N1, 2 * LANES), BF16),...]
    ppermute x0 -> x1, starting transfers between devices: none -> 1.45 us  [per_device(): far = lax.ppermute(narrow, ('band', 'slab'), next_chip())]
    unnamed x16 -> x12, local copies, waits for them, and re-layouts: 5.13 us -> 4.17 us
  transfers between devices with their start and end apart: 0 -> 1, of which waited for: 0 -> 0; matrix products, arithmetic and copies ran while one was open for 0% -> 0% of each run, Pallas kernels for 0% -> 10%
where the time goes in v7:
time: 102 us
  Pallas kernels  95.5 us (94%)
  local copies, waits for them, and re-layouts  4.17 us (4%)
  starting transfers between devices  1.45 us (1%)
    pallas_call x1, Pallas kernels, middle_of(): pl.pallas_call(middle_kernel, out_shape=(shape(index.shape, F32), shape((...  21.5 us
    pallas_call x1, Pallas kernels, end_of(): pl.pallas_call(end_kernel, out_shape=(shape((planes, width), F32), shape(...  20.4 us
    pallas_call x2, Pallas kernels, zy_of(): pl.pallas_call(zy_kernel, out_shape=shape((N2, N1, 2 * LANES), BF16), in_...  20.1 us
    pallas_call x1, Pallas kernels, dense_of(): pl.pallas_call(dense_kernel, out_shape=(shape((N2, N1, 2 * LANES), BF16),...  13.4 us
    pallas_call x1, Pallas kernels, gather_of(): pl.pallas_call(gather_kernel, out_shape=shape((slabs, QUARTERS, 2, npw //...  10.7 us
    pallas_call x1, Pallas kernels, start_of(): pl.pallas_call(start_kernel, out_shape=(shape((slabs, 8, npw + 2 * WIN),...  9.43 us
    unnamed x12, local copies, waits for them, and re-layouts  4.17 us
  transfers between devices with their start and end apart: 1, of which 0 were waited for; matrix products, arithmetic and copies ran while one was open for 0% of the time, Pallas kernels for 10%

profile of v7, /device:TPU:1, one launch (start us, length us, event | category | flops | bytes accessed | tf_op | source)
XLA Modules:
  0.0 102.2 jit_solution(13725992658617021662)
XLA Ops:
  0.6 0.0 copy-start
  0.6 1.2 %copy-done = f32[1,24,9216]{2,1,0:T(8,128)S(1)} copy-done((f32[1,24,9216]{2,1,0:T(8,128)S(1)}, f32[1,24,9216]{2,1,0:T(8,128)}, u32[]{:S(2)}) %copy-start) | copy-done | bytes 884760
  1.8 0.0 copy-start.2
  1.8 0.9 copy-done.2
  2.7 0.0 copy-start.3
  2.7 0.8 copy-done.3
  3.6 9.4 %start.1 = (f32[4,8,14848]{2,1,0:T(8,128)S(1)}, s32[4,1,128]{2,1,0:T(1,128)S(1)}, bf16[24,9216]{1,0:T(8,128)(2,1)S(1)}) custom-call(bf16[8,13824]{1,0:T(8,128)(2,1)S(1)} %copy-done.2, s32[108,128]{1,0:T(8,128)S(1)} %bitcast.6, f32[24,9216]{1,0:T(8,128)S(1)} %bitcast.3), custom_call_target="tpu_custom_call" | custom-call | tf_op jit(solution)/shard_map/start/pallas_call | solution.py:717
  13.0 1.4 %collective-permute-start = (bf16[24,9216]{1,0:T(8,128)(2,1)S(1)}, bf16[24,9216]{1,0:T(8,128)(2,1)S(1)}, u32[]{:S(2)}, u32[]{:S(2)}) collective-permute-start(bf16[24,9216]{1,0:T(8,128)(2,1)S(1)} %get-tuple-element.14.pot_ref), channel_id=1, source_target_pairs={{0,18},{1,3},{2,0},{3,17},{4,22},{5,7},{6,4},{7,21},{8,26},{9,11},... | collective-permute-start | bytes 1327112 | tf_op jit(solution)/shard_map/ppermute | solution.py:863
  14.5 0.3 multiply_convert_fusion.tab_ref
  14.7 10.1 %scatter_zy.2.turned_ref = bf16[96,96,256]{2,1,0:T(8,128)(2,1)S(1)} custom-call(s32[4,1,128]{2,1,0:T(1,128)S(1)} %get-tuple-element.12.starts_ref, f32[4,8,14848]{2,1,0:T(8,128)S(1)} %get-tuple-element.13.data_ref.index_ref, bf16[96,96]{1,0:T(8,128)(2,1)S(1)} %multiply_convert_fusion.tab_ref), custom_call_target="tpu_custom_call" | custom-call | flops 20000000000 | bytes 8000000 | tf_op jit(solution)/shard_map/scatter_zy/pallas_call | solution.py:739
  24.8 0.0 collective-permute-done.far_ref
  24.8 13.4 %dense.1 = (bf16[96,96,256]{2,1,0:T(8,128)(2,1)S(1)}, bf16[96,96,256]{2,1,0:T(8,128)(2,1)S(1)}, bf16[2,4,8,3456]{3,2,1,0:T(8,128)(2,1)S(1)}) custom-call(bf16[96,96,256]{2,1,0:T(8,128)(2,1)S(1)} %scatter_zy.2.turned_ref, bf16[24,9216]{1,0:T(8,128)(2,1)S(1)} %get-tuple-element.14.pot_ref, bf16[24,9216]{1,0:T(8,128)(2,1)S(1)} %collective-permute-done.far_ref, ...), custom_call_target="tpu_custom_call" | custom-call | flops 20000000000 | bytes 8000000 | tf_op jit(solution)/shard_map/dense/pallas_call | solution.py:753
  38.2 0.0 copy-start.4
  38.2 10.7 %gather.1.waves_ref = bf16[4,4,2,3456]{3,2,1,0:T(2,128)(2,1)S(1)} custom-call(s32[4,1,128]{2,1,0:T(1,128)S(1)} %get-tuple-element.12.starts_ref, f32[4,8,14848]{2,1,0:T(8,128)S(1)} %get-tuple-element.13.data_ref.index_ref, bf16[96,96,256]{2,1,0:T(8,128)(2,1)S(1)} %get-tuple-element.15.back_ref, bf16[96,96]{1,0:T(8,128)(2,1)S(1)} %multiply_convert_fusion.tab_ref), custom_call_target="tpu_custom_call" | custom-call | flops 20000000000 | bytes 8000000 | tf_op jit(solution)/shard_map/gather/pallas_call | solution.py:775
  48.8 0.0 copy-done.4
  48.9 21.5 %middle.1 = (f32[4,8,14848]{2,1,0:T(8,128)S(1)}, f32[8,128]{1,0:T(8,128)S(1)}) custom-call(bf16[4,4,2,3456]{3,2,1,0:T(2,128)(2,1)S(1)} %gather.1.waves_ref, bf16[2,4,8,3456]{3,2,1,0:T(8,128)(2,1)S(1)} %get-tuple-element.16.bands_ref, f32[4,8,14848]{2,1,0:T(8,128)S(1)} %get-tuple-element.13.data_ref.index_ref, f32[8]{0:T(128)S(1)} %copy-done.4), custom_call_target="tpu_custom_call" | custom-call | tf_op jit(solution)/shard_map/middle/pallas_call | solution.py:792
  70.4 0.0 copy-start.1
  70.4 10.1 %scatter_zy.3.turned_ref = bf16[96,96,256]{2,1,0:T(8,128)(2,1)S(1)} custom-call(s32[4,1,128]{2,1,0:T(1,128)S(1)} %get-tuple-element.12.starts_ref, f32[4,8,14848]{2,1,0:T(8,128)S(1)} %get-tuple-element.17.data_ref, bf16[96,96]{1,0:T(8,128)(2,1)S(1)} %multiply_convert_fusion.tab_ref), custom_call_target="tpu_custom_call" | custom-call | flops 20000000000 | bytes 8000000 | tf_op jit(solution)/shard_map/scatter_zy/pallas_call | solution.py:739
  80.5 0.0 copy-done.1
  80.5 20.4 %density.1 = (f32[24,1152]{1,0:T(8,128)S(1)}, f32[8,128]{1,0:T(8,128)S(1)}) custom-call(bf16[96,96,256]{2,1,0:T(8,128)(2,1)S(1)} %scatter_zy.3.turned_ref, bf16[96,96,256]{2,1,0:T(8,128)(2,1)S(1)} %get-tuple-element.18.psi_ref, f32[8,128]{1,0:T(8,128)S(1)} %get-tuple-element.19.step_ref, f32[24,9216]{1,0:T(8,128)S(1)} %bitcast.4, ...), custom_call_target="tpu_custom_call" | custom-call | tf_op jit(solution)/shard_map/density/pallas_call | solution.py:814
  100.9 0.6 copy.6
  101.5 0.6 copy.8
  (3 shorter events, 0.0 us)
Async XLA Ops:
  0.6 1.2 %copy-start = (f32[1,24,9216]{2,1,0:T(8,128)S(1)}, f32[1,24,9216]{2,1,0:T(8,128)}, u32[]{:S(2)}) copy-start(f32[1,24,9216]{2,1,0:T(8,128)} %param.6) | copy-start | bytes 2654212
  1.8 0.9 copy-start.2
  2.7 0.8 copy-start.3
  13.0 11.8 %collective-permute-start = (bf16[24,9216]{1,0:T(8,128)(2,1)S(1)}, bf16[24,9216]{1,0:T(8,128)(2,1)S(1)}, u32[]{:S(2)}, u32[]{:S(2)}) collective-permute-start(bf16[24,9216]{1,0:T(8,128)(2,1)S(1)} %get-tuple-element.14.pot_ref), channel_id=1, source_target_pairs={{0,18},{1,3},{2,0},{3,17},{4,22},{5,7},{6,4},{7,21},{8,26},{9,11},... | collective-permute-start | bytes 1327112 | tf_op jit(solution)/shard_map/ppermute | solution.py:863
  38.2 10.7 %copy-start.4 = (f32[8]{0:T(128)S(1)}, f32[8]{0:T(128)}, u32[]{:S(2)}) copy-start(f32[8]{0:T(128)} %energy_ref.1) | copy-start | bytes 100
  70.4 10.1 %copy-start.1 = (f32[1,24,9216]{2,1,0:T(8,128)S(1)}, f32[1,24,9216]{2,1,0:T(8,128)}, u32[]{:S(2)}) copy-start(f32[1,24,9216]{2,1,0:T(8,128)} %param.6) | copy-start | bytes 2654212

commit v8 on v7

--- a/solution.py
+++ b/solution.py
@@ -10,9 +10,13 @@
 N3 = 96
 LANES = 128
 WIN = 512
+NEAR = WIN - LANES
 TILE = 2
 TILES = N1 // TILE
 QUARTERS = 4
+PART_A = 5
+PART_B = 4
+PARTS = PART_A + PART_B
 F32 = jnp.float32
 BF16 = jnp.bfloat16
 NT = (((1,), (1,)), ((), ()))
@@ -58,13 +62,19 @@
     return total > 0
 
 
+def near_at(starts_ref, s, tile, i=0):
+    first = starts_ref[s, 0, tile]
+    base = (first // LANES) * LANES
+    return pl.multiple_of(base + i * NEAR, LANES), first - base
+
+
 def hot_rows(rows, tile, cells):
     at = rows[2:3] - (tile * cells).astype(F32)
-    return iota((cells, WIN), 0).astype(F32) == at
+    return iota((cells, rows.shape[1]), 0).astype(F32) == at
 
 
 def hot_z(rows):
-    here = iota((N3, WIN), 0).astype(F32) == rows[3:4]
+    here = iota((N3, rows.shape[1]), 0).astype(F32) == rows[3:4]
     return here.astype(F32).astype(BF16)
 
 
@@ -147,10 +157,11 @@
             transform([plane_ref[first + u] for u in range(width)], first)
 
 
-def gather_window(data_ref, planes, s, base, tile):
+def gather_window(data_ref, planes, s, at, tile):
     ny = N2 // data_ref.shape[0]
     cells = TILE * ny
-    rows = data_ref[s, :, pl.ds(base, WIN)]
+    base, off = at
+    rows = pltpu.roll(data_ref[s, :, pl.ds(base, WIN)], WIN - off, 1)[:, :NEAR]
     hot = hot_rows(rows, tile, cells)
     mine = [plane[b * N2 + s * ny : b * N2 + (s + 1) * ny] for b in range(2) for plane in planes]
     picked = dot(jnp.concatenate(mine, axis=0).astype(BF16), hot_z(rows))
@@ -158,7 +169,9 @@
         jnp.sum(jnp.where(hot, picked[b * cells : (b + 1) * cells], 0.0), axis=0, keepdims=True)
         for b in range(2)
     ]
-    return jnp.concatenate(found, axis=0)
+    found = jnp.concatenate(found + [jnp.zeros((6, NEAR), F32)], axis=0)
+    found = jnp.concatenate([found, jnp.zeros((8, WIN - NEAR), F32)], axis=1)
+    return pltpu.roll(found, off, 1)[:2]
 
 
 def gather_kernel(starts_ref, data_ref, back_ref, tab_ref, out_ref, sum_ref):
@@ -183,8 +196,8 @@
             tile = group * several + u
             planes = all_planes[TILE * u : TILE * (u + 1)]
             for s in range(slabs):
-                base = window_base(starts_ref, s, tile)
-                found.append((s, base, gather_window(data_ref, planes, s, base, tile)))
+                at = near_at(starts_ref, s, tile)
+                found.append((s, at[0], gather_window(data_ref, planes, s, at, tile)))
         for s, base, value in found:
             sum_ref[s, :, pl.ds(base, WIN)] += value
 
@@ -194,12 +207,12 @@
         def _(tile):
             planes = wave_planes(tile, TILE)
             for s in range(slabs):
-                base = window_base(starts_ref, s, tile)
-
-                @pl.loop(1, (starts_ref[s, 0, tile + 1] - base + WIN - 1) // WIN)
+                count = starts_ref[s, 0, tile + 1] - starts_ref[s, 0, tile]
+
+                @pl.loop(1, (count + NEAR - 1) // NEAR)
                 def _(i):
-                    at = pl.multiple_of(base + i * WIN, LANES)
-                    sum_ref[s, :, pl.ds(at, WIN)] += gather_window(data_ref, planes, s, at, tile)
+                    at = near_at(starts_ref, s, tile, i)
+                    sum_ref[s, :, pl.ds(at[0], WIN)] += gather_window(data_ref, planes, s, at, tile)
 
     part = out_ref.shape[3]
     for q in range(out_ref.shape[1]):
@@ -251,8 +264,18 @@
     return {"band": y_hi * 4 + z, "slab": y_lo * 2 + core}
 
 
+def pairs_of(perts):
+    return [(p, q) for p in range(perts) for q in range(p + 1)]
+
+
+def total_of(one, two):
+    total = sum(a * b for a, b in zip(one, two))
+    total = total[0:8] + total[8:16] + total[16:24]
+    return jnp.sum(total, axis=0, keepdims=True)
+
+
 def start_kernel(
-    coef_ref, map_ref, pot_ref, data_ref, starts_ref, narrow_ref,
+    coef_ref, map_ref, pot_ref, data_ref, starts_ref, narrow_ref, share_ref,
     own_coef, own_map, coefs_ref, maps_ref, send_sem, recv_sem,
 ):
     slabs, two, npw = coefs_ref.shape
@@ -283,7 +306,7 @@
     starts = jnp.sum(spread, axis=0, keepdims=True).astype(jnp.int32)
     after = pltpu.roll(starts, LANES - 1, 1)
     lane = iota((1, LANES), 1)
-    over = (after > jnp.bitwise_and(starts, -LANES) + WIN) & (lane < TILES)
+    over = (after > starts + NEAR) & (lane < TILES)
     flag = jnp.max(over.astype(F32), axis=1, keepdims=True).astype(jnp.int32)
     own_map[0:1, npw : npw + LANES] = jnp.where(lane == TILES + 1, flag, starts)
     copies = []
@@ -293,6 +316,8 @@
     maps_ref[me] = own_map[...]
     data_ref[...] = jnp.full(data_ref.shape, -1.0, F32)
     narrow_ref[...] = pot_ref[...].astype(BF16)
+    width = share_ref.shape[1]
+    share_ref[...] = pot_ref[:, pl.ds(pl.multiple_of(lax.axis_index("band") * width, LANES), width)]
     wait_all(copies)
     for s in range(slabs):
         starts_ref[s] = maps_ref[s, :, npw : npw + LANES]
@@ -316,8 +341,9 @@
 
 
 def dense_kernel(
-    turned_ref, pot_ref, far_ref, coef_ref, tab_ref, psi_ref, back_ref, bands_ref,
-    pots_ref, send_sem, recv_sem, coef_send, coef_recv,
+    turned_ref, pot_ref, far_ref, share_ref, coef_ref, tab_ref,
+    psi_ref, back_ref, bands_ref, shares_ref, gram_ref,
+    pots_ref, send_sem, recv_sem, coef_send, coef_recv, share_send, share_recv,
 ):
     slabs = pots_ref.shape[0]
     y_hi, y_lo, z, core = place()
@@ -327,13 +353,18 @@
     steps = [(a, b) for a in range(2) for b in range(4) if a + b > 0]
     others = [(lax.rem(y_hi + a, 2), lax.rem(z + b, 4)) for a, b in steps]
     members = [device(a, y_lo, b, core) for a, b in others]
-    greet([sibling] + members)
+    perts = shares_ref.shape[0]
+    pert = lax.axis_index("pert")
+    p_peers = [{"pert": lax.rem(pert + d, perts)} for d in range(1, perts)]
+    everyone = [sibling] + members + p_peers
+    greet(everyone)
     part = bands_ref.shape[3]
     quarter = pl.ds(pl.multiple_of(lax.axis_index("pert") * part, LANES), part)
     bands_ref[y_hi, z] = coef_ref[:, quarter]
     pots_ref[me] = pot_ref[...]
     pots_ref[distant] = far_ref[...]
-    greeted([sibling] + members)
+    shares_ref[pert] = share_ref[...]
+    greeted(everyone)
     copies = []
     for i, member in enumerate(members):
         src = coef_ref.at[:, quarter]
@@ -342,6 +373,8 @@
         send(pot_ref, pots_ref.at[me], send_sem.at[0], recv_sem.at[0], sibling),
         send(far_ref, pots_ref.at[distant], send_sem.at[1], recv_sem.at[1], sibling),
     ]
+    for i, peer in enumerate(p_peers):
+        copies.append(send(share_ref, shares_ref.at[pert], share_send.at[i], share_recv.at[i], peer))
 
     inv_x = transposed(tab_ref[...])
     unroll = 16
@@ -382,6 +415,10 @@
         back_ref[:, pl.ds(first, width), :] = jnp.swapaxes(jnp.stack(done, axis=0), 0, 1)
 
     wait_all(copies)
+    parts = [[shares_ref[p, :, j * LANES : (j + 1) * LANES] for j in range(PARTS)] for p in range(perts)]
+    sums = [total_of(parts[p], parts[q]) for p, q in pairs_of(perts)]
+    sums.append(jnp.zeros((16 - len(sums), LANES), F32))
+    gram_ref[...] = jnp.concatenate(sums, axis=0)
 
 
 def middle_kernel(
@@ -485,31 +522,29 @@
     step_ref[...] = jnp.concatenate([wide, tail, jnp.zeros((8 - two - 1, LANES), F32)], axis=0)
 
 
-PART_A = 5
-PART_B = 4
-PARTS = PART_A + PART_B
-
-
 def end_kernel(
-    turned_ref, psi_ref, step_ref, pot_ref, tab_ref, out_ref, projected_ref,
+    turned_ref, psi_ref, step_ref, pots_ref, gram_ref, tab_ref, out_ref, projected_ref,
     dens_ref, from_core, a_ref, b_ref, a_from_y, b_from_z, a_sum, b_sum, a_from_z, b_from_y,
-    pots_ref, sums_ref, from_sums, core_send, core_recv, pot_send, pot_recv, a_send, a_recv, b_send, b_recv,
+    sums_ref, from_sums, core_send, core_recv, a_send, a_recv, b_send, b_recv,
     a2_send, a2_recv, b2_send, b2_recv, sum_send, sum_recv,
 ):
-    perts, planes, width = pots_ref.shape
+    perts, planes, _ = pots_ref.shape
     slabs = dens_ref.shape[0]
     y_hi, y_lo, z, core = place()
-    pert, band = lax.axis_index("pert"), lax.axis_index("band")
     sibling = device(y_hi, y_lo, z, 1 - core)
     y_coords = [(1 - y_hi, y_lo), (1 - y_hi, 1 - y_lo), (y_hi, 1 - y_lo)]
     y_peers = [device(a, b, z, core) for a, b in y_coords]
     y_others = [device(a, b, z, 1 - core) for a, b in y_coords]
     z_coords = [lax.rem(z + d, 4) for d in range(1, 4)]
     z_peers = [device(y_hi, y_lo, c, core) for c in z_coords]
-    p_peers = [{"pert": lax.rem(pert + d, perts)} for d in range(1, perts)]
-    everyone = [sibling] + y_peers + y_others + z_peers + p_peers
+    everyone = [sibling] + y_peers + y_others + z_peers
     greet(everyone)
-    pots_ref[pert] = pot_ref[:, pl.ds(pl.multiple_of(band * width, LANES), width)]
+    pairs = pairs_of(perts)
+    line = iota((1, LANES), 1)
+    sums = [gram_ref[0 : len(pairs)]]
+    sums += [jnp.where(line == p, step_ref[2:3], 0.0) for p in range(perts)]
+    sums.append(jnp.zeros((16 - len(pairs) - perts, LANES), F32))
+    sums_ref[0] = jnp.concatenate(sums, axis=0)
 
     inv_x = transposed(tab_ref[...])
     lane = iota((N1, LANES), 1)
@@ -573,35 +608,6 @@
                 send(b_ref.at[k, c], b_from_z.at[k, i], b_send.at[k, i], b_recv.at[k, i], z_peers[i])
             )
 
-    density_part(halves[0], 0, 3)
-    greeted(everyone)
-    to_sibling(0)
-    pot_copies = []
-    for i, peer in enumerate(p_peers):
-        mine = pots_ref.at[pert]
-        pot_copies.append(send(mine, mine, pot_send.at[i], pot_recv.at[i], peer))
-    density_part(halves[1], 0, 1)
-    to_others(0)
-    density_part(halves[1], 1, 3)
-    to_sibling(1)
-
-    def total_of(pair):
-        total = sum(pair(j) for j in range(PARTS))
-        total = total[0:8] + total[8:16] + total[16:24]
-        return jnp.sum(total, axis=0, keepdims=True)
-
-    def pot(p, j):
-        return pots_ref[p, :, j * LANES : (j + 1) * LANES]
-
-    wait_all(pot_copies)
-    pairs = [(p, q) for p in range(perts) for q in range(p + 1)]
-    sums = [total_of(lambda j: pot(p, j) * pot(q, j)) for p, q in pairs]
-    line = iota((1, LANES), 1)
-    sums += [jnp.where(line == p, step_ref[2:3], 0.0) for p in range(perts)]
-    sums += [jnp.zeros((1, LANES), F32)] * (16 - len(sums))
-    sums_ref[0] = jnp.concatenate(sums, axis=0)
-    to_others(1)
-
     def sum_sends(level, first, group):
         copies = []
         for i, peer in enumerate(group):
@@ -616,9 +622,23 @@
             total = total + from_sums[first + i]
         sums_ref[level + 1] = total
 
+    density_part(halves[0], 0, 3)
+    greeted(everyone)
+    to_sibling(0)
     near = [sibling] + y_peers + y_others
     near_copies = sum_sends(0, 0, near)
-
+    density_part(halves[1], 0, 1)
+    to_others(0)
+    density_part(halves[1], 1, 3)
+    to_sibling(1)
+
+    def pot(p, j):
+        return pots_ref[p, :, j * LANES : (j + 1) * LANES]
+
+    to_others(1)
+
+    sum_up(0, 0, near_copies)
+    far_copies = sum_sends(1, len(near), z_peers)
     wait_all(a_copies)
 
     @pl.loop(0, 4)
@@ -647,8 +667,6 @@
         b_sum[k, l, j] = value
     for i, (k, l) in enumerate([(0, y_lo), (0, 1 - y_lo), (1, 1 - y_lo)]):
         copies.append(send(b_sum.at[k, l], b_from_y.at[i], b2_send.at[i], b2_recv.at[i], y_peers[i]))
-    sum_up(0, 0, near_copies)
-    far_copies = sum_sends(1, len(near), z_peers)
     wait_all(copies)
     density = []
     for j in range(PARTS):
@@ -720,9 +738,10 @@
             shape((slabs, 8, npw + 2 * WIN), F32),
             shape((slabs, 1, LANES), jnp.int32),
             shape(pot.shape, BF16),
+            shape((pot.shape[0], pot.shape[1] // 8), F32),
         ),
         in_specs=[VMEM] * 3,
-        out_specs=(VMEM, VMEM, VMEM),
+        out_specs=(VMEM,) * 4,
         scratch_shapes=[
             pltpu.VMEM(block, BF16),
             pltpu.VMEM((1, npw + LANES), jnp.int32),
@@ -748,7 +767,7 @@
     )(starts, data, tab)
 
 
-def dense_of(turned, pot, far, coefs, tab, slabs):
+def dense_of(turned, pot, far, share, coefs, tab, slabs, perts):
     bands, npw = coefs.shape
     return pl.pallas_call(
         dense_kernel,
@@ -756,18 +775,21 @@
             shape((N2, N1, 2 * LANES), BF16),
             shape((N1, N2, 2 * LANES), BF16),
             shape((2, 4, bands, npw // QUARTERS), BF16),
+            shape((perts,) + share.shape, F32),
+            shape((16, LANES), F32),
         ),
-        in_specs=[VMEM] * 5,
-        out_specs=(VMEM, VMEM, VMEM),
+        in_specs=[VMEM] * 6,
+        out_specs=(VMEM,) * 5,
         scratch_shapes=[
             pltpu.VMEM((slabs,) + pot.shape, BF16),
         ]
         + sems(2)
-        + sems(7),
+        + sems(7)
+        + sems(perts - 1),
         compiler_params=params(4),
         cost_estimate=cost(2e10, 8e6),
         name="dense",
-    )(turned, pot, far, coefs, tab)
+    )(turned, pot, far, share, coefs, tab)
 
 
 def gather_of(starts, data, back, tab, npw):
@@ -807,14 +829,13 @@
     )(waves, bands, index, energies)
 
 
-def end_of(turned, psi, step, pot, tab, slabs, perts):
-    planes, cross = pot.shape
-    width = cross // 8
+def end_of(turned, psi, step, pots, gram, tab, slabs):
+    _, planes, width = pots.shape
     tile = (planes, LANES)
     return pl.pallas_call(
         end_kernel,
         out_shape=(shape((planes, width), F32), shape((8, LANES), F32)),
-        in_specs=[VMEM] * 5,
+        in_specs=[VMEM] * 6,
         out_specs=(VMEM, VMEM),
         scratch_shapes=[
             pltpu.VMEM((slabs, 8 * PARTS) + tile, BF16),
@@ -827,12 +848,10 @@
             pltpu.VMEM((2, 2, PART_B) + tile, BF16),
             pltpu.VMEM((3, PART_A) + tile, BF16),
             pltpu.VMEM((3, PART_B) + tile, BF16),
-            pltpu.VMEM((perts, planes, width), F32),
             pltpu.VMEM((3, 16, LANES), F32),
             pltpu.VMEM((10, 16, LANES), F32),
         ]
         + sems(2, 2)
-        + sems(3)
         + sems(3)
         + sems(2, 3)
         + sems(3)
@@ -840,7 +859,7 @@
         + sems(10),
         compiler_params=params(3),
         name="density",
-    )(turned, psi, step, pot, tab)
+    )(turned, psi, step, pots, gram, tab)
 
 
 def next_chip():
@@ -859,15 +878,16 @@
     planes, cross = trial_potentials.shape[1:]
     tab = cosines(N1)
     pot = trial_potentials.reshape(planes, cross)
-    data, starts, narrow = start_of(wave_coeffs, wave_map, pot, slabs)
+    data, starts, narrow, share = start_of(wave_coeffs, wave_map, pot, slabs)
     far = lax.ppermute(narrow, ("band", "slab"), next_chip())
     turned = zy_of(starts, data, tab)
-    psi, back, all_bands = dense_of(turned, narrow, far, wave_coeffs, tab, slabs)
+    perts = lax.axis_size("pert")
+    psi, back, all_bands, pots, gram = dense_of(turned, narrow, far, share, wave_coeffs, tab, slabs, perts)
     waves = gather_of(starts, data, back, tab, npw)
     data, step = middle_of(waves, all_bands, data, band_energies)
     turned = zy_of(starts, data, tab)
-    residual, projected = end_of(turned, psi, step, pot, tab, slabs, lax.axis_size("pert"))
-    return (residual.reshape(1, planes, -1), projected[: lax.axis_size("pert"), :1])
+    residual, projected = end_of(turned, psi, step, pots, gram, tab, slabs)
+    return (residual.reshape(1, planes, -1), projected[:perts, :1])
 
 
 def solution(mesh):

time: 102 us -> 97.9 us (0.960)
  Pallas kernels: 95.5 us -> 90.6 us
    pallas_call x1, Pallas kernels: 20.4 us -> 15.2 us  [end_of(): pl.pallas_call(end_kernel, out_shape=(shape((planes, width), F32), shape(...]
    pallas_call x1, Pallas kernels: 13.4 us -> 15.1 us  [dense_of(): pl.pallas_call(dense_kernel, out_shape=(shape((N2, N1, 2 * LANES), BF16),...]
    unnamed x12 -> x10, local copies, waits for them, and re-layouts: 4.17 us -> 4.16 us
where the time goes in v8:
time: 97.9 us; the launch traced here: 97.2 us
  Pallas kernels  90.6 us (93%)
  local copies, waits for them, and re-layouts  4.16 us (4%)
  starting transfers between devices  1.45 us (1%)
    pallas_call x1, Pallas kernels, middle_of(): pl.pallas_call(middle_kernel, out_shape=(shape(index.shape, F32), shape((...  20.8 us
    pallas_call x2, Pallas kernels, zy_of(): pl.pallas_call(zy_kernel, out_shape=shape((N2, N1, 2 * LANES), BF16), in_...  20.1 us
    pallas_call x1, Pallas kernels, end_of(): pl.pallas_call(end_kernel, out_shape=(shape((planes, width), F32), shape(...  15.2 us
    pallas_call x1, Pallas kernels, dense_of(): pl.pallas_call(dense_kernel, out_shape=(shape((N2, N1, 2 * LANES), BF16),...  15.1 us
    pallas_call x1, Pallas kernels, gather_of(): pl.pallas_call(gather_kernel, out_shape=shape((slabs, QUARTERS, 2, npw //...  9.97 us
    pallas_call x1, Pallas kernels, start_of(): pl.pallas_call(start_kernel, out_shape=(shape((slabs, 8, npw + 2 * WIN),...  9.43 us
    unnamed x10, local copies, waits for them, and re-layouts  4.16 us
  transfers between devices with their start and end apart: 1, of which 0 were waited for; matrix products, arithmetic and copies ran while one was open for 0% of the time, Pallas kernels for 10%

profile of v8, /device:TPU:1, one launch (start us, length us, event | category | flops | bytes accessed | tf_op | source)
XLA Modules:
  0.0 97.2 jit_solution(7899817459010327514)
XLA Ops:
  0.6 0.0 copy-start
  0.6 1.2 %copy-done = f32[1,24,9216]{2,1,0:T(8,128)S(1)} copy-done((f32[1,24,9216]{2,1,0:T(8,128)S(1)}, f32[1,24,9216]{2,1,0:T(8,128)}, u32[]{:S(2)}) %copy-start) | copy-done | bytes 884760
  1.8 0.0 copy-start.1
  1.8 0.9 copy-done.1
  2.7 0.0 copy-start.2
  2.7 0.8 copy-done.2
  3.6 9.4 %start.1 = (f32[4,8,14848]{2,1,0:T(8,128)S(1)}, s32[4,1,128]{2,1,0:T(1,128)S(1)}, bf16[24,9216]{1,0:T(8,128)(2,1)S(1)}, f32[24,1152]{1,0:T(8,128)S(1)}) custom-call(bf16[8,13824]{1,0:T(8,128)(2,1)S(1)} %copy-done.1, s32[108,128]{1,0:T(8,128)S(1)} %bitcast.5, f32[24,9216]{1,0:T(8,128)S(1)} %bitcast.3), custom_call_target="tpu_custom_call" | custom-call | tf_op jit(solution)/shard_map/start/pallas_call | solution.py:735
  13.0 1.4 %collective-permute-start = (bf16[24,9216]{1,0:T(8,128)(2,1)S(1)}, bf16[24,9216]{1,0:T(8,128)(2,1)S(1)}, u32[]{:S(2)}, u32[]{:S(2)}) collective-permute-start(bf16[24,9216]{1,0:T(8,128)(2,1)S(1)} %get-tuple-element.17.pot_ref), channel_id=1, source_target_pairs={{0,18},{1,3},{2,0},{3,17},{4,22},{5,7},{6,4},{7,21},{8,26},{9,11},... | collective-permute-start | bytes 1327112 | tf_op jit(solution)/shard_map/ppermute | solution.py:882
  14.5 0.3 multiply_convert_fusion.tab_ref
  14.7 10.1 %scatter_zy.2.turned_ref = bf16[96,96,256]{2,1,0:T(8,128)(2,1)S(1)} custom-call(s32[4,1,128]{2,1,0:T(1,128)S(1)} %get-tuple-element.15.starts_ref, f32[4,8,14848]{2,1,0:T(8,128)S(1)} %get-tuple-element.16.data_ref.index_ref, bf16[96,96]{1,0:T(8,128)(2,1)S(1)} %multiply_convert_fusion.tab_ref), custom_call_target="tpu_custom_call" | custom-call | flops 20000000000 | bytes 8000000 | tf_op jit(solution)/shard_map/scatter_zy/pallas_call | solution.py:758
  24.8 0.0 collective-permute-done.far_ref
  24.8 15.1 %dense.1 = (bf16[96,96,256]{2,1,0:T(8,128)(2,1)S(1)}, bf16[96,96,256]{2,1,0:T(8,128)(2,1)S(1)}, bf16[2,4,8,3456]{3,2,1,0:T(8,128)(2,1)S(1)}, f32[4,24,1152]{2,1,0:T(8,128)S(1)}, f32[16,128]{1,0:T(8,128)S(1)}) custom-call(bf16[96,96,256]{2,1,0:T(8,128)(2,1)S(1)} %scatter_zy.2.turned_ref, bf16[24,9216]{1,0:T(8,128)(2,1)S(1)} %get-tuple-element.17.pot_ref, ...), custom_call_target="tpu_custom_call" | custom-call | flops 20000000000 | bytes 8000000 | tf_op jit(solution)/shard_map/dense/pallas_call | solution.py:772
  39.9 0.0 copy-start.3
  39.9 10.0 %gather.1.waves_ref = bf16[4,4,2,3456]{3,2,1,0:T(2,128)(2,1)S(1)} custom-call(s32[4,1,128]{2,1,0:T(1,128)S(1)} %get-tuple-element.15.starts_ref, f32[4,8,14848]{2,1,0:T(8,128)S(1)} %get-tuple-element.16.data_ref.index_ref, bf16[96,96,256]{2,1,0:T(8,128)(2,1)S(1)} %get-tuple-element.19.back_ref, bf16[96,96]{1,0:T(8,128)(2,1)S(1)} %multiply_convert_fusion.tab_ref), custom_call_target="tpu_custom_call" | custom-call | flops 20000000000 | bytes 8000000 | tf_op jit(solution)/shard_map/gather/pallas_call | solution.py:797
  49.9 0.0 copy-done.3
  49.9 20.8 %middle.1 = (f32[4,8,14848]{2,1,0:T(8,128)S(1)}, f32[8,128]{1,0:T(8,128)S(1)}) custom-call(bf16[4,4,2,3456]{3,2,1,0:T(2,128)(2,1)S(1)} %gather.1.waves_ref, bf16[2,4,8,3456]{3,2,1,0:T(8,128)(2,1)S(1)} %get-tuple-element.20.bands_ref, f32[4,8,14848]{2,1,0:T(8,128)S(1)} %get-tuple-element.16.data_ref.index_ref, f32[8]{0:T(128)S(1)} %copy-done.3), custom_call_target="tpu_custom_call" | custom-call | tf_op jit(solution)/shard_map/middle/pallas_call | solution.py:814
  70.7 10.1 %scatter_zy.3.turned_ref = bf16[96,96,256]{2,1,0:T(8,128)(2,1)S(1)} custom-call(s32[4,1,128]{2,1,0:T(1,128)S(1)} %get-tuple-element.15.starts_ref, f32[4,8,14848]{2,1,0:T(8,128)S(1)} %get-tuple-element.21.data_ref, bf16[96,96]{1,0:T(8,128)(2,1)S(1)} %multiply_convert_fusion.tab_ref), custom_call_target="tpu_custom_call" | custom-call | flops 20000000000 | bytes 8000000 | tf_op jit(solution)/shard_map/scatter_zy/pallas_call | solution.py:758
  80.8 15.2 %density.1 = (f32[24,1152]{1,0:T(8,128)S(1)}, f32[8,128]{1,0:T(8,128)S(1)}) custom-call(bf16[96,96,256]{2,1,0:T(8,128)(2,1)S(1)} %scatter_zy.3.turned_ref, bf16[96,96,256]{2,1,0:T(8,128)(2,1)S(1)} %get-tuple-element.22.psi_ref, f32[8,128]{1,0:T(8,128)S(1)} %get-tuple-element.23.step_ref, f32[4,24,1152]{2,1,0:T(8,128)S(1)} %get-tuple-element.24.pots_ref, ...), custom_call_target="tpu_custom_call" | custom-call | tf_op jit(solution)/shard_map/density/pallas_call | solution.py:835
  96.0 0.6 copy.6
  96.6 0.6 copy.8
  (3 shorter events, 0.0 us)
Async XLA Ops:
  0.6 1.2 %copy-start = (f32[1,24,9216]{2,1,0:T(8,128)S(1)}, f32[1,24,9216]{2,1,0:T(8,128)}, u32[]{:S(2)}) copy-start(f32[1,24,9216]{2,1,0:T(8,128)} %param.6) | copy-start | bytes 2654212
  1.8 0.9 copy-start.1
  2.7 0.8 copy-start.2
  13.0 11.8 %collective-permute-start = (bf16[24,9216]{1,0:T(8,128)(2,1)S(1)}, bf16[24,9216]{1,0:T(8,128)(2,1)S(1)}, u32[]{:S(2)}, u32[]{:S(2)}) collective-permute-start(bf16[24,9216]{1,0:T(8,128)(2,1)S(1)} %get-tuple-element.17.pot_ref), channel_id=1, source_target_pairs={{0,18},{1,3},{2,0},{3,17},{4,22},{5,7},{6,4},{7,21},{8,26},{9,11},... | collective-permute-start | bytes 1327112 | tf_op jit(solution)/shard_map/ppermute | solution.py:882
  39.9 10.0 %copy-start.3 = (f32[8]{0:T(128)S(1)}, f32[8]{0:T(128)}, u32[]{:S(2)}) copy-start(f32[8]{0:T(128)} %energy_ref.1) | copy-start | bytes 100

commit v9 on v8

--- a/solution.py
+++ b/solution.py
@@ -283,7 +283,15 @@
     me = lax.axis_index("slab")
     peers = slab_peers(slabs)
     chunk = 1536
-    greet([{"slab": peer} for peer in peers])
+    y_hi, y_lo, z, core = place()
+
+    def around(step, other):
+        to = lax.rem(y_hi * 2 + y_lo + step + 4, 4)
+        return device(to // 2, lax.rem(to, 2), z, other)
+
+    chips = [around(step, other) for step in (-1, 1) for other in (0, 1)]
+    everyone = [device(y_hi, y_lo, z, 1 - core)] + chips
+    greet(everyone)
     for r in range(npw // LANES):
         own_map[0:1, r * LANES : (r + 1) * LANES] = map_ref[r : r + 1, :]
     for i in range(npw // chunk):
@@ -291,7 +299,7 @@
         block = coef_ref[:, at].astype(F32)
         for t in range(slabs):
             own_coef[t, :, at] = block[two * t : two * (t + 1)].astype(BF16)
-    greeted(peers)
+    greeted(everyone)
     coef_copies = []
     for i, peer in enumerate(peers):
         to = {"slab": peer}
@@ -309,16 +317,21 @@
     over = (after > starts + NEAR) & (lane < TILES)
     flag = jnp.max(over.astype(F32), axis=1, keepdims=True).astype(jnp.int32)
     own_map[0:1, npw : npw + LANES] = jnp.where(lane == TILES + 1, flag, starts)
+    near = send(own_map, maps_ref.at[me], send_sem.at[1, 2], recv_sem.at[1, 2], everyone[0])
     copies = []
-    for i, peer in enumerate(peers):
-        to = {"slab": peer}
-        copies.append(send(own_map, maps_ref.at[me], send_sem.at[1, i], recv_sem.at[1, i], to))
+    for other in (0, 1):
+        to = around(2 * core - 1, other)
+        copies.append(send(own_map, maps_ref.at[me], send_sem.at[1, other], recv_sem.at[1, core], to))
     maps_ref[me] = own_map[...]
     data_ref[...] = jnp.full(data_ref.shape, -1.0, F32)
     narrow_ref[...] = pot_ref[...].astype(BF16)
     width = share_ref.shape[1]
     share_ref[...] = pot_ref[:, pl.ds(pl.multiple_of(lax.axis_index("band") * width, LANES), width)]
-    wait_all(copies)
+    near.wait()
+    for other in (0, 1):
+        copies[other].wait_send()
+        slot = maps_ref.at[(1 - y_lo) * 2 + other]
+        remote(own_map, slot, send_sem.at[1, other], recv_sem.at[1, other], everyone[0]).wait_recv()
     for s in range(slabs):
         starts_ref[s] = maps_ref[s, :, npw : npw + LANES]
     y_first = (iota((slabs, 1), 0) * ny).astype(F32)
@@ -455,15 +468,15 @@
     for i in range(part // chunk):
         at = pl.ds(i * chunk, chunk)
         total = total + dot_nt(waves_at(at).astype(BF16), bands_at(at))
-    total_ref[...] = jnp.concatenate([total[: rows // 2], total[rows // 2 :]], axis=1)
+    total_ref[...] = jnp.concatenate([total[: rows // 2], total[rows // 2 :]], axis=1).astype(BF16)
 
     copies = []
     for i, peer in enumerate(peers):
         copies.append(send(total_ref, corr_ref.at[i], send_sem.at[1, i], recv_sem.at[1, i], peer))
     wait_all(copies)
-    total = total_ref[...]
+    total = total_ref[...].astype(F32)
     for i in range(len(peers)):
-        total = total + corr_ref[i]
+        total = total + corr_ref[i].astype(F32)
     correlation = jnp.concatenate([total[:, :count], total[:, count:]], axis=0).astype(BF16)
 
     overlap = jnp.zeros((rows, rows), F32)
@@ -818,10 +831,10 @@
         out_specs=(VMEM, VMEM),
         scratch_shapes=[
             pltpu.VMEM(waves.shape, BF16),
-            pltpu.VMEM((peers,) + small, F32),
+            pltpu.VMEM((peers,) + small, BF16),
             longer,
             longer,
-            pltpu.VMEM(small, F32),
+            pltpu.VMEM(small, BF16),
         ]
         + sems(3, peers),
         compiler_params=params(2),

time: 97.9 us -> 97 us (level)
    pallas_call x1, Pallas kernels: 15.1 us -> 12.4 us  [dense_of(): pl.pallas_call(dense_kernel, out_shape=(shape((N2, N1, 2 * LANES), BF16),...]
    pallas_call x1, Pallas kernels: 20.8 us -> 21.9 us  [middle_of(): pl.pallas_call(middle_kernel, out_shape=(shape(index.shape, F32), shape((...]
where the time goes in v9:
time: 97 us; the launch traced here: 96.6 us
  Pallas kernels  89.8 us (93%)
  local copies, waits for them, and re-layouts  4.16 us (4%)
  starting transfers between devices  1.67 us (2%)
    pallas_call x1, Pallas kernels, middle_of(): pl.pallas_call(middle_kernel, out_shape=(shape(index.shape, F32), shape((...  21.9 us
    pallas_call x2, Pallas kernels, zy_of(): pl.pallas_call(zy_kernel, out_shape=shape((N2, N1, 2 * LANES), BF16), in_...  20.1 us
    pallas_call x1, Pallas kernels, end_of(): pl.pallas_call(end_kernel, out_shape=(shape((planes, width), F32), shape(...  15.9 us
    pallas_call x1, Pallas kernels, dense_of(): pl.pallas_call(dense_kernel, out_shape=(shape((N2, N1, 2 * LANES), BF16),...  12.4 us
    pallas_call x1, Pallas kernels, gather_of(): pl.pallas_call(gather_kernel, out_shape=shape((slabs, QUARTERS, 2, npw //...  9.98 us
    pallas_call x1, Pallas kernels, start_of(): pl.pallas_call(start_kernel, out_shape=(shape((slabs, 8, npw + 2 * WIN),...  9.45 us
    unnamed x10, local copies, waits for them, and re-layouts  4.16 us
  transfers between devices with their start and end apart: 1, of which 0 were waited for; matrix products, arithmetic and copies ran while one was open for 0% of the time, Pallas kernels for 10%

profile of v9, /device:TPU:1, one launch (start us, length us, event | category | flops | bytes accessed | tf_op | source)
XLA Modules:
  0.0 96.6 jit_solution(14402360912807744405)
XLA Ops:
  0.6 0.0 copy-start
  0.6 1.2 %copy-done = f32[1,24,9216]{2,1,0:T(8,128)S(1)} copy-done((f32[1,24,9216]{2,1,0:T(8,128)S(1)}, f32[1,24,9216]{2,1,0:T(8,128)}, u32[]{:S(2)}) %copy-start) | copy-done | bytes 884760
  1.8 0.0 copy-start.1
  1.8 0.9 copy-done.1
  2.7 0.0 copy-start.2
  2.7 0.8 copy-done.2
  3.6 9.4 %start.1 = (f32[4,8,14848]{2,1,0:T(8,128)S(1)}, s32[4,1,128]{2,1,0:T(1,128)S(1)}, bf16[24,9216]{1,0:T(8,128)(2,1)S(1)}, f32[24,1152]{1,0:T(8,128)S(1)}) custom-call(bf16[8,13824]{1,0:T(8,128)(2,1)S(1)} %copy-done.1, s32[108,128]{1,0:T(8,128)S(1)} %bitcast.5, f32[24,9216]{1,0:T(8,128)S(1)} %bitcast.3), custom_call_target="tpu_custom_call" | custom-call | tf_op jit(solution)/shard_map/start/pallas_call | solution.py:748
  13.0 1.7 %collective-permute-start = (bf16[24,9216]{1,0:T(8,128)(2,1)S(1)}, bf16[24,9216]{1,0:T(8,128)(2,1)S(1)}, u32[]{:S(2)}, u32[]{:S(2)}) collective-permute-start(bf16[24,9216]{1,0:T(8,128)(2,1)S(1)} %get-tuple-element.17.pot_ref), channel_id=1, source_target_pairs={{0,18},{1,3},{2,0},{3,17},{4,22},{5,7},{6,4},{7,21},{8,26},{9,11},... | collective-permute-start | bytes 1327112 | tf_op jit(solution)/shard_map/ppermute | solution.py:895
  14.7 0.3 multiply_convert_fusion.tab_ref
  15.0 10.1 %scatter_zy.2.turned_ref = bf16[96,96,256]{2,1,0:T(8,128)(2,1)S(1)} custom-call(s32[4,1,128]{2,1,0:T(1,128)S(1)} %get-tuple-element.15.starts_ref, f32[4,8,14848]{2,1,0:T(8,128)S(1)} %get-tuple-element.16.data_ref.index_ref, bf16[96,96]{1,0:T(8,128)(2,1)S(1)} %multiply_convert_fusion.tab_ref), custom_call_target="tpu_custom_call" | custom-call | flops 20000000000 | bytes 8000000 | tf_op jit(solution)/shard_map/scatter_zy/pallas_call | solution.py:771
  25.0 0.0 collective-permute-done.far_ref
  25.0 12.4 %dense.1 = (bf16[96,96,256]{2,1,0:T(8,128)(2,1)S(1)}, bf16[96,96,256]{2,1,0:T(8,128)(2,1)S(1)}, bf16[2,4,8,3456]{3,2,1,0:T(8,128)(2,1)S(1)}, f32[4,24,1152]{2,1,0:T(8,128)S(1)}, f32[16,128]{1,0:T(8,128)S(1)}) custom-call(bf16[96,96,256]{2,1,0:T(8,128)(2,1)S(1)} %scatter_zy.2.turned_ref, bf16[24,9216]{1,0:T(8,128)(2,1)S(1)} %get-tuple-element.17.pot_ref, ...), custom_call_target="tpu_custom_call" | custom-call | flops 20000000000 | bytes 8000000 | tf_op jit(solution)/shard_map/dense/pallas_call | solution.py:785
  37.4 0.0 copy-start.3
  37.5 10.0 %gather.1.waves_ref = bf16[4,4,2,3456]{3,2,1,0:T(2,128)(2,1)S(1)} custom-call(s32[4,1,128]{2,1,0:T(1,128)S(1)} %get-tuple-element.15.starts_ref, f32[4,8,14848]{2,1,0:T(8,128)S(1)} %get-tuple-element.16.data_ref.index_ref, bf16[96,96,256]{2,1,0:T(8,128)(2,1)S(1)} %get-tuple-element.19.back_ref, bf16[96,96]{1,0:T(8,128)(2,1)S(1)} %multiply_convert_fusion.tab_ref), custom_call_target="tpu_custom_call" | custom-call | flops 20000000000 | bytes 8000000 | tf_op jit(solution)/shard_map/gather/pallas_call | solution.py:810
  47.4 0.0 copy-done.3
  47.5 21.9 %middle.1 = (f32[4,8,14848]{2,1,0:T(8,128)S(1)}, f32[8,128]{1,0:T(8,128)S(1)}) custom-call(bf16[4,4,2,3456]{3,2,1,0:T(2,128)(2,1)S(1)} %gather.1.waves_ref, bf16[2,4,8,3456]{3,2,1,0:T(8,128)(2,1)S(1)} %get-tuple-element.20.bands_ref, f32[4,8,14848]{2,1,0:T(8,128)S(1)} %get-tuple-element.16.data_ref.index_ref, f32[8]{0:T(128)S(1)} %copy-done.3), custom_call_target="tpu_custom_call" | custom-call | tf_op jit(solution)/shard_map/middle/pallas_call | solution.py:827
  69.4 10.1 %scatter_zy.3.turned_ref = bf16[96,96,256]{2,1,0:T(8,128)(2,1)S(1)} custom-call(s32[4,1,128]{2,1,0:T(1,128)S(1)} %get-tuple-element.15.starts_ref, f32[4,8,14848]{2,1,0:T(8,128)S(1)} %get-tuple-element.21.data_ref, bf16[96,96]{1,0:T(8,128)(2,1)S(1)} %multiply_convert_fusion.tab_ref), custom_call_target="tpu_custom_call" | custom-call | flops 20000000000 | bytes 8000000 | tf_op jit(solution)/shard_map/scatter_zy/pallas_call | solution.py:771
  79.5 15.9 %density.1 = (f32[24,1152]{1,0:T(8,128)S(1)}, f32[8,128]{1,0:T(8,128)S(1)}) custom-call(bf16[96,96,256]{2,1,0:T(8,128)(2,1)S(1)} %scatter_zy.3.turned_ref, bf16[96,96,256]{2,1,0:T(8,128)(2,1)S(1)} %get-tuple-element.22.psi_ref, f32[8,128]{1,0:T(8,128)S(1)} %get-tuple-element.23.step_ref, f32[4,24,1152]{2,1,0:T(8,128)S(1)} %get-tuple-element.24.pots_ref, ...), custom_call_target="tpu_custom_call" | custom-call | tf_op jit(solution)/shard_map/density/pallas_call | solution.py:848
  95.4 0.6 copy.6
  96.0 0.6 copy.8
  (3 shorter events, 0.0 us)
Async XLA Ops:
  0.6 1.2 %copy-start = (f32[1,24,9216]{2,1,0:T(8,128)S(1)}, f32[1,24,9216]{2,1,0:T(8,128)}, u32[]{:S(2)}) copy-start(f32[1,24,9216]{2,1,0:T(8,128)} %param.6) | copy-start | bytes 2654212
  1.8 0.9 copy-start.1
  2.7 0.8 copy-start.2
  13.0 12.0 %collective-permute-start = (bf16[24,9216]{1,0:T(8,128)(2,1)S(1)}, bf16[24,9216]{1,0:T(8,128)(2,1)S(1)}, u32[]{:S(2)}, u32[]{:S(2)}) collective-permute-start(bf16[24,9216]{1,0:T(8,128)(2,1)S(1)} %get-tuple-element.17.pot_ref), channel_id=1, source_target_pairs={{0,18},{1,3},{2,0},{3,17},{4,22},{5,7},{6,4},{7,21},{8,26},{9,11},... | collective-permute-start | bytes 1327112 | tf_op jit(solution)/shard_map/ppermute | solution.py:895
  37.4 10.0 %copy-start.3 = (f32[8]{0:T(128)S(1)}, f32[8]{0:T(128)}, u32[]{:S(2)}) copy-start(f32[8]{0:T(128)} %energy_ref.1) | copy-start | bytes 100

commit v10 on v9

--- a/solution.py
+++ b/solution.py
@@ -121,7 +121,7 @@
 def zy_kernel(starts_ref, data_ref, tab_ref, turned_ref, plane_ref):
     inv_y = transposed(tab_ref[...])
     inv_z = dot(tab_ref[...], ones_at(N3, LANES)).astype(BF16)
-    width = 32
+    width = 48
     over = overflow(starts_ref, data_ref.shape[0])
 
     def transform(planes, first):
@@ -442,7 +442,7 @@
     half, zs, bands, _ = bands_ref.shape
     chunk = 1152
     pert, slab = lax.axis_index("pert"), lax.axis_index("slab")
-    steps = [(a, b) for a in range(quarters) for b in range(slabs) if a + b > 0]
+    steps = [(a, b) for a in (2, 1, 3, 0) for b in (2, 3, 1, 0) if a + b > 0]
     others = [(lax.rem(pert + a, quarters), lax.rem(slab + b, slabs)) for a, b in steps]
     peers = [{"pert": c, "slab": t} for c, t in others]
     greet(peers)

time: 97 us -> 96.3 us (level)
    pallas_call x1, Pallas kernels: 21.9 us -> 20.9 us  [middle_of(): pl.pallas_call(middle_kernel, out_shape=(shape(index.shape, F32), shape((...]
where the time goes in v10:
time: 96.3 us; the launch traced here: 96 us
  Pallas kernels  89.2 us (93%)
  local copies, waits for them, and re-layouts  4.16 us (4%)
  starting transfers between devices  1.67 us (2%)
    pallas_call x1, Pallas kernels, middle_of(): pl.pallas_call(middle_kernel, out_shape=(shape(index.shape, F32), shape((...  20.9 us
    pallas_call x2, Pallas kernels, zy_of(): pl.pallas_call(zy_kernel, out_shape=shape((N2, N1, 2 * LANES), BF16), in_...  19.9 us
    pallas_call x1, Pallas kernels, end_of(): pl.pallas_call(end_kernel, out_shape=(shape((planes, width), F32), shape(...  16.7 us
    pallas_call x1, Pallas kernels, dense_of(): pl.pallas_call(dense_kernel, out_shape=(shape((N2, N1, 2 * LANES), BF16),...  12.4 us
    pallas_call x1, Pallas kernels, gather_of(): pl.pallas_call(gather_kernel, out_shape=shape((slabs, QUARTERS, 2, npw //...  9.83 us
    pallas_call x1, Pallas kernels, start_of(): pl.pallas_call(start_kernel, out_shape=(shape((slabs, 8, npw + 2 * WIN),...  9.45 us
    unnamed x10, local copies, waits for them, and re-layouts  4.16 us
  transfers between devices with their start and end apart: 1, of which 0 were waited for; matrix products, arithmetic and copies ran while one was open for 0% of the time, Pallas kernels for 10%

profile of v10, /device:TPU:1, one launch (start us, length us, event | category | flops | bytes accessed | tf_op | source)
XLA Modules:
  0.0 96.0 jit_solution(12529041881824762609)
XLA Ops:
  0.6 0.0 copy-start
  0.6 1.2 %copy-done = f32[1,24,9216]{2,1,0:T(8,128)S(1)} copy-done((f32[1,24,9216]{2,1,0:T(8,128)S(1)}, f32[1,24,9216]{2,1,0:T(8,128)}, u32[]{:S(2)}) %copy-start) | copy-done | bytes 884760
  1.8 0.0 copy-start.1
  1.8 0.9 copy-done.1
  2.7 0.0 copy-start.2
  2.7 0.8 copy-done.2
  3.6 9.4 %start.1 = (f32[4,8,14848]{2,1,0:T(8,128)S(1)}, s32[4,1,128]{2,1,0:T(1,128)S(1)}, bf16[24,9216]{1,0:T(8,128)(2,1)S(1)}, f32[24,1152]{1,0:T(8,128)S(1)}) custom-call(bf16[8,13824]{1,0:T(8,128)(2,1)S(1)} %copy-done.1, s32[108,128]{1,0:T(8,128)S(1)} %bitcast.5, f32[24,9216]{1,0:T(8,128)S(1)} %bitcast.3), custom_call_target="tpu_custom_call" | custom-call | tf_op jit(solution)/shard_map/start/pallas_call | solution.py:748
  13.0 1.7 %collective-permute-start = (bf16[24,9216]{1,0:T(8,128)(2,1)S(1)}, bf16[24,9216]{1,0:T(8,128)(2,1)S(1)}, u32[]{:S(2)}, u32[]{:S(2)}) collective-permute-start(bf16[24,9216]{1,0:T(8,128)(2,1)S(1)} %get-tuple-element.17.pot_ref), channel_id=1, source_target_pairs={{0,18},{1,3},{2,0},{3,17},{4,22},{5,7},{6,4},{7,21},{8,26},{9,11},... | collective-permute-start | bytes 1327112 | tf_op jit(solution)/shard_map/ppermute | solution.py:895
  14.7 0.3 multiply_convert_fusion.tab_ref
  15.0 9.9 %scatter_zy.2.turned_ref = bf16[96,96,256]{2,1,0:T(8,128)(2,1)S(1)} custom-call(s32[4,1,128]{2,1,0:T(1,128)S(1)} %get-tuple-element.15.starts_ref, f32[4,8,14848]{2,1,0:T(8,128)S(1)} %get-tuple-element.16.data_ref.index_ref, bf16[96,96]{1,0:T(8,128)(2,1)S(1)} %multiply_convert_fusion.tab_ref), custom_call_target="tpu_custom_call" | custom-call | flops 20000000000 | bytes 8000000 | tf_op jit(solution)/shard_map/scatter_zy/pallas_call | solution.py:771
  24.9 0.0 collective-permute-done.far_ref
  24.9 12.4 %dense.1 = (bf16[96,96,256]{2,1,0:T(8,128)(2,1)S(1)}, bf16[96,96,256]{2,1,0:T(8,128)(2,1)S(1)}, bf16[2,4,8,3456]{3,2,1,0:T(8,128)(2,1)S(1)}, f32[4,24,1152]{2,1,0:T(8,128)S(1)}, f32[16,128]{1,0:T(8,128)S(1)}) custom-call(bf16[96,96,256]{2,1,0:T(8,128)(2,1)S(1)} %scatter_zy.2.turned_ref, bf16[24,9216]{1,0:T(8,128)(2,1)S(1)} %get-tuple-element.17.pot_ref, ...), custom_call_target="tpu_custom_call" | custom-call | flops 20000000000 | bytes 8000000 | tf_op jit(solution)/shard_map/dense/pallas_call | solution.py:785
  37.3 0.0 copy-start.3
  37.3 9.8 %gather.1.waves_ref = bf16[4,4,2,3456]{3,2,1,0:T(2,128)(2,1)S(1)} custom-call(s32[4,1,128]{2,1,0:T(1,128)S(1)} %get-tuple-element.15.starts_ref, f32[4,8,14848]{2,1,0:T(8,128)S(1)} %get-tuple-element.16.data_ref.index_ref, bf16[96,96,256]{2,1,0:T(8,128)(2,1)S(1)} %get-tuple-element.19.back_ref, bf16[96,96]{1,0:T(8,128)(2,1)S(1)} %multiply_convert_fusion.tab_ref), custom_call_target="tpu_custom_call" | custom-call | flops 20000000000 | bytes 8000000 | tf_op jit(solution)/shard_map/gather/pallas_call | solution.py:810
  47.2 0.0 copy-done.3
  47.2 20.9 %middle.1 = (f32[4,8,14848]{2,1,0:T(8,128)S(1)}, f32[8,128]{1,0:T(8,128)S(1)}) custom-call(bf16[4,4,2,3456]{3,2,1,0:T(2,128)(2,1)S(1)} %gather.1.waves_ref, bf16[2,4,8,3456]{3,2,1,0:T(8,128)(2,1)S(1)} %get-tuple-element.20.bands_ref, f32[4,8,14848]{2,1,0:T(8,128)S(1)} %get-tuple-element.16.data_ref.index_ref, f32[8]{0:T(128)S(1)} %copy-done.3), custom_call_target="tpu_custom_call" | custom-call | tf_op jit(solution)/shard_map/middle/pallas_call | solution.py:827
  68.1 10.0 %scatter_zy.3.turned_ref = bf16[96,96,256]{2,1,0:T(8,128)(2,1)S(1)} custom-call(s32[4,1,128]{2,1,0:T(1,128)S(1)} %get-tuple-element.15.starts_ref, f32[4,8,14848]{2,1,0:T(8,128)S(1)} %get-tuple-element.21.data_ref, bf16[96,96]{1,0:T(8,128)(2,1)S(1)} %multiply_convert_fusion.tab_ref), custom_call_target="tpu_custom_call" | custom-call | flops 20000000000 | bytes 8000000 | tf_op jit(solution)/shard_map/scatter_zy/pallas_call | solution.py:771
  78.1 16.7 %density.1 = (f32[24,1152]{1,0:T(8,128)S(1)}, f32[8,128]{1,0:T(8,128)S(1)}) custom-call(bf16[96,96,256]{2,1,0:T(8,128)(2,1)S(1)} %scatter_zy.3.turned_ref, bf16[96,96,256]{2,1,0:T(8,128)(2,1)S(1)} %get-tuple-element.22.psi_ref, f32[8,128]{1,0:T(8,128)S(1)} %get-tuple-element.23.step_ref, f32[4,24,1152]{2,1,0:T(8,128)S(1)} %get-tuple-element.24.pots_ref, ...), custom_call_target="tpu_custom_call" | custom-call | tf_op jit(solution)/shard_map/density/pallas_call | solution.py:848
  94.8 0.6 copy.6
  95.4 0.6 copy.8
  (3 shorter events, 0.0 us)
Async XLA Ops:
  0.6 1.2 %copy-start = (f32[1,24,9216]{2,1,0:T(8,128)S(1)}, f32[1,24,9216]{2,1,0:T(8,128)}, u32[]{:S(2)}) copy-start(f32[1,24,9216]{2,1,0:T(8,128)} %param.6) | copy-start | bytes 2654212
  1.8 0.9 copy-start.1
  2.7 0.8 copy-start.2
  13.0 11.9 %collective-permute-start = (bf16[24,9216]{1,0:T(8,128)(2,1)S(1)}, bf16[24,9216]{1,0:T(8,128)(2,1)S(1)}, u32[]{:S(2)}, u32[]{:S(2)}) collective-permute-start(bf16[24,9216]{1,0:T(8,128)(2,1)S(1)} %get-tuple-element.17.pot_ref), channel_id=1, source_target_pairs={{0,18},{1,3},{2,0},{3,17},{4,22},{5,7},{6,4},{7,21},{8,26},{9,11},... | collective-permute-start | bytes 1327112 | tf_op jit(solution)/shard_map/ppermute | solution.py:895
  37.3 9.8 %copy-start.3 = (f32[8]{0:T(128)S(1)}, f32[8]{0:T(128)}, u32[]{:S(2)}) copy-start(f32[8]{0:T(128)} %energy_ref.1) | copy-start | bytes 100
